TPU v7x, 128 devices: a whole 4x4x4 slice. The times are simulated.
128 devices in a mesh: ctx: 16 (over z, x), tp: 8 (over y, core).
Axes of the slice: x: 4, y: 4, z: 4, core: 2. Of those that a mesh axis runs over, the one named last changes fastest.
Arguments:
- inputs: bfloat16 [8192, 16384], P('ctx', 'tp'), may hold values from -6 to 6
- gate_input: bfloat16 [8192, 16384], P('ctx', 'tp'), may hold values from -120 to 120
- step_size: float32 [256, 8192], P('tp', 'ctx'), may hold values from 0 to 1, as said below
- input_map: bfloat16 [8192, 2048], P('ctx', 'tp'), may hold values from -6 to 6
- output_map: bfloat16 [8192, 2048], P('ctx', 'tp'), may hold values from -6 to 6
- decay_rate: float32 [256], P('tp'), may hold values from 1 to 4
- skip_weight: float32 [256], P('tp'), may hold values from 0.5 to 1.5
- norm_gain: float32 [16384], P('tp'), may hold values from 0.1 to 1.9
- out_grad: bfloat16 [8192, 16384], P('ctx', 'tp'), may hold values from -6 to 6
Outputs:
- normed: bfloat16 [8192, 16384], P('ctx', 'tp')
- grad_inputs: bfloat16 [8192, 16384], P('ctx', 'tp')
- grad_gate: bfloat16 [8192, 16384], P('ctx', 'tp')
- grad_input_map: bfloat16 [8192, 2048], P('ctx', 'tp')
- grad_output_map: bfloat16 [8192, 2048], P('ctx', 'tp')
Inputs may be any that keep to these rules, and one draw needn't show every extreme that they name: `step_size`: positive.
All inputs are finite; a program needn't handle non-finite values.
Results may differ from a plain program's by a relative error of at most 0.015.
Values may be sent and summed in bfloat16 or wider, within the bound.
No kernel may reach another device: no remote copies, remote signals or barrier semaphores. Data moves between devices by JAX's collectives and lax.ppermute only.
A program may use at most 192 MiB of HBM per device.

v0:
```python
import jax
import jax.numpy as jnp
from jax import lax
from jax.sharding import PartitionSpec as P

H = 256
P_SIZE = 64
N = 256
BLOCK = 256


EPS = 1e-05


def decay_logs(step_size, decay_rate):
    return -decay_rate[:, None] * step_size


def segment_parts(inputs, step_size, input_map, output_map, decay_rate, skip_weight):
    length = inputs.shape[0]
    head_count = step_size.shape[0]
    groups = input_map.shape[1] // N
    per_group = head_count // groups
    blocks = length // BLOCK
    log_decay = decay_logs(step_size, decay_rate).reshape(head_count, blocks, BLOCK)
    inner_cum = jnp.cumsum(log_decay, axis=2)
    cum_heads = inner_cum.reshape(groups, per_group, blocks, BLOCK)
    total_heads = inner_cum[:, :, -1].reshape(groups, per_group, blocks)
    values = inputs.reshape(blocks, BLOCK, groups, per_group, P_SIZE)
    keys_in = input_map.reshape(blocks, BLOCK, groups, N)
    queries = output_map.reshape(blocks, BLOCK, groups, N)
    steps_blk = step_size.reshape(groups, per_group, blocks, BLOCK)
    scores = jnp.einsum("bqgn,bsgn->bgqs", queries, keys_in, preferred_element_type=jnp.float32)
    lower_mask = jnp.arange(BLOCK)[:, None] >= jnp.arange(BLOCK)[None, :]
    cum_order = cum_heads.transpose(2, 0, 1, 3)
    decay_gap = jnp.where(lower_mask, cum_order[..., :, None] - cum_order[..., None, :], 0.0)
    step_order = steps_blk.transpose(2, 0, 1, 3)
    weights = (
        jnp.where(lower_mask, jnp.exp(decay_gap), 0.0)
        * scores[:, :, None]
        * step_order[..., None, :]
    )
    weights = weights.astype(jnp.bfloat16)
    within = jnp.einsum("bghqs,bsghp->bqghp", weights, values, preferred_element_type=jnp.float32)
    end_weight = (jnp.exp(cum_heads[..., -1:] - cum_heads) * steps_blk).transpose(2, 3, 0, 1)
    scaled_keys = (keys_in[:, :, :, None, :] * end_weight[..., None]).astype(jnp.bfloat16)
    block_states = jnp.einsum(
        "bsghp,bsghn->bghpn", values, scaled_keys, preferred_element_type=jnp.float32
    )
    running = jnp.zeros((groups, per_group, P_SIZE, N), jnp.float32)
    inter_list = []
    for block_id in range(blocks):
        inter_list.append(
            jnp.einsum(
                "qgn,ghpn->qghp",
                queries[block_id].astype(jnp.float32),
                running,
                precision=lax.Precision.HIGHEST,
            )
        )
        running = (
            jnp.exp(total_heads[:, :, block_id])[:, :, None, None] * running
            + block_states[block_id]
        )
    carried = jnp.stack(inter_list) * jnp.exp(cum_heads).transpose(2, 3, 0, 1)[..., None]
    skip_heads = skip_weight.reshape(groups, per_group)[:, :, None]
    mixed_out = within + carried + skip_heads * values.astype(jnp.float32)
    return (
        mixed_out.reshape(length, groups, per_group, P_SIZE),
        running.reshape(head_count, P_SIZE, N),
    )


def body(
    inputs,
    gate_input,
    step_size,
    input_map,
    output_map,
    decay_rate,
    skip_weight,
    norm_gain,
    out_grad,
):
    length = inputs.shape[0]
    head_count = step_size.shape[0]
    groups = input_map.shape[1] // N
    per_group = head_count // groups
    zero_state = jnp.zeros((head_count, P_SIZE, N), jnp.float32)

    def parts_fn(values_in, keys_map, query_map):
        return segment_parts(values_in, step_size, keys_map, query_map, decay_rate, skip_weight)

    (mixed_zero, end_zero), pull_parts = jax.vjp(parts_fn, inputs, input_map, output_map)
    local_end = end_zero.astype(jnp.bfloat16)
    seg_decay = jnp.exp(jnp.sum(decay_logs(step_size, decay_rate), axis=1)).astype(jnp.bfloat16)
    local_end, seg_decay = lax.optimization_barrier((local_end, seg_decay))
    all_ends, all_decays = (
        lax.all_gather(local_end[None], "ctx", axis=0, tiled=True),
        lax.all_gather(seg_decay[None], "ctx", axis=0, tiled=True),
    )
    position = lax.axis_index("ctx")
    seg_count = all_ends.shape[0]

    def forward_turn(segment, running):
        updated = all_decays[segment].astype(jnp.float32)[:, None, None] * running + all_ends[
            segment
        ].astype(jnp.float32)
        return jnp.where(segment < position, updated, running)

    state_in = lax.fori_loop(0, seg_count, forward_turn, zero_state)
    seg_cum = jnp.exp(jnp.cumsum(decay_logs(step_size, decay_rate), axis=1)).T.reshape(
        length, groups, per_group
    )
    queries_wide = output_map.reshape(length, groups, N).astype(jnp.float32)
    state_view = state_in.reshape(groups, per_group, P_SIZE, N)
    carried_in = (
        jnp.einsum("tgn,ghpn->tghp", queries_wide, state_view, precision=lax.Precision.HIGHEST)
        * seg_cum[..., None]
    )
    mixed = mixed_zero + carried_in
    gate_wide = gate_input.astype(jnp.float32).reshape(length, groups, per_group, P_SIZE)
    gate_sig = jax.nn.sigmoid(gate_wide)
    silu_gate = gate_wide * gate_sig
    gated_out = (mixed * silu_gate).reshape(length, head_count * P_SIZE)
    full_width = H * P_SIZE
    squares = lax.psum(jnp.sum(gated_out * gated_out, axis=1), "tp")
    inv_rms = lax.rsqrt(squares / full_width + EPS)
    normed = (gated_out * inv_rms[:, None] * norm_gain).astype(jnp.bfloat16)
    scaled_grad = norm_gain * out_grad.astype(jnp.float32)
    product = lax.psum(jnp.sum(gated_out * scaled_grad, axis=1), "tp")
    grad_gated = (
        inv_rms[:, None] * scaled_grad - gated_out * (inv_rms**3 * product / full_width)[:, None]
    )
    grad_view = grad_gated.reshape(length, groups, per_group, P_SIZE)
    grad_mixed = grad_view * silu_gate
    weighted = grad_mixed * seg_cum[..., None]
    local_grad = (
        jnp.einsum("tghp,tgn->ghpn", weighted, queries_wide, precision=lax.Precision.HIGHEST)
        .reshape(head_count, P_SIZE, N)
        .astype(jnp.bfloat16)
    )
    local_grad = lax.optimization_barrier(local_grad)
    all_grads = lax.all_gather(local_grad[None], "ctx", axis=0, tiled=True)

    def backward_turn(reverse_turn, running):
        segment = seg_count - 1 - reverse_turn
        updated = all_decays[segment].astype(jnp.float32)[:, None, None] * running + all_grads[
            segment
        ].astype(jnp.float32)
        return jnp.where(segment > position, updated, running)

    state_grad = lax.fori_loop(0, seg_count, backward_turn, zero_state)
    grad_gate = grad_view * mixed * gate_sig * (1.0 + gate_wide * (1.0 - gate_sig))
    grad_values, grad_keys, grad_queries = pull_parts((grad_mixed, state_grad))
    extra_queries = jnp.einsum(
        "tghp,ghpn->tgn", weighted, state_view, precision=lax.Precision.HIGHEST
    ).reshape(length, groups * N)
    return (
        normed,
        grad_values,
        grad_gate.reshape(length, head_count * P_SIZE).astype(jnp.bfloat16),
        grad_keys,
        (grad_queries + extra_queries).astype(jnp.bfloat16),
    )


def solution(mesh):
    return jax.shard_map(
        body,
        mesh=mesh,
        in_specs=(
            P("ctx", "tp"),
            P("ctx", "tp"),
            P("tp", "ctx"),
            P("ctx", "tp"),
            P("ctx", "tp"),
            P("tp"),
            P("tp"),
            P("tp"),
            P("ctx", "tp"),
        ),
        out_specs=(P("ctx", "tp"), P("ctx", "tp"), P("ctx", "tp"), P("ctx", "tp"), P("ctx", "tp")),
        check_vma=False,
    )
```

profile of v0, /device:TPU:0, one launch (start us, length us, event | category | flops | bytes accessed | tf_op | source)
XLA Modules:
  0.0 404.7 jit_solution(6735440339834430310)
XLA Ops:
  11.7 7.1 %reshape.658 = bf16[2,256,32,64]{3,2,1,0:T(8,128)(2,1)} reshape(bf16[512,2048]{1,0:T(8,128)(2,1)} %param.13) | data formatting | bytes 4194304 | tf_op jit(solution)/shard_map/reshape.16
  18.8 4.9 %copy.103 = bf16[2,256,32,64]{1,3,2,0:T(8,128)(2,1)S(1)} copy(bf16[2,256,32,64]{3,2,1,0:T(8,128)(2,1)} %reshape.658) | data formatting | bytes 4194304 | tf_op jit(solution)/shard_map/reshape.16
  24.1 2.8 fusion.24
  30.3 7.4 %reshape.656 = f32[2,256,1,32,64]{4,3,1,0,2:T(8,128)} reshape(bf16[512,2048]{1,0:T(8,128)(2,1)} %param.13) | data formatting | bytes 6291456 | tf_op jit(solution)/shard_map/jvp()/convert_element_type | solution.py:67
  39.2 42.7 %all-reduce.4 = bf16[512]{0:T(512)(128)(2,1)S(1)} all-reduce(bf16[512]{0:T(512)(128)(2,1)S(1)} %dynamic-update-slice), channel_id=2, replica_groups=mesh['ctx'=16,'tp'=8] {'ctx'}, use_global_device_ids=true, to_apply=%add.4 | all-reduce | flops 512 | bytes 2048
  82.0 7.9 %copy.108 = f32[2,256,1,32,64]{1,4,3,0,2:T(8,128)} copy(f32[2,256,1,32,64]{4,3,1,0,2:T(8,128)} %reshape.656) | data formatting | bytes 8388608 | tf_op jit(solution)/shard_map/jvp()/convert_element_type | solution.py:67
  91.0 3.5 fusion.36
  94.8 5.4 %fusion.14 = f32[1,2,32,8,8,256]{5,4,3,2,1,0:T(8,128)S(1)} fusion(f32[1,256,1,32,64]{1,4,3,0,2:T(8,128)S(1)} %fusion.36, f32[1,256,1,32,64]{1,4,3,0,2:T(8,128)S(1)} %convolution_bitcast_fusion, f32[2,256,1,32,64]{1,4,3,0,2:T(8,128)S(1)} %copy-done.9, bf16[2,256,32,64]{1,3,2,0:T(8,128)(2,1)S(1)} %copy-done.12, f32[2,32,256]{2,1,0:T(8,128)S(1)} %copy.101, ...), kind=kOutput, calls=%fused_computation.24 | convolution fusion | flops 567279616 | bytes 15466624 | tf_op jit(solution)/shard_map/jvp(bghqs,bsghp->bqghp)/dot_general | solution.py:44
  100.2 2.5 copy.136
  104.1 3.9 copy.112
  108.0 4.1 %convert_element_type.212 = f32[512,2048]{0,1:T(8,128)} convert(bf16[512,2048]{0,1:T(8,128)(2,1)} %copy.112) | non-fusion elementwise | flops 1048576 | bytes 6291456 | tf_op jit(solution)/shard_map/convert_element_type | solution.py:122
  112.1 4.0 copy.113
  116.2 28.3 %all-gather.6.cloned.1.call-done = bf16[512,64,256]{2,1,0:T(8,128)(2,1)} async-done(((bf16[32,64,256]{2,1,0:T(8,128)(2,1)}), bf16[512,64,256]{2,1,0:T(8,128)(2,1)}) %all-gather.6.cloned.1.call-update) | async-done | bytes 16777232 | tf_op jit(solution)/shard_map/all_gather | solution.py:99
  144.6 36.3 %while.30 = (s32[]{:T(128)}, f32[32,64,256]{2,1,0:T(8,128)S(1)}, s32[]{:T(128)}, bf16[16,32]{1,0:T(8,128)(2,1)S(1)}, bf16[16,32,64,256]{3,2,1,0:T(8,128)(2,1)}, /*index=5*/s32[]{:T(128)}, s32[]{:T(128)}) while((s32[]{:T(128)}, f32[32,64,256]{2,1,0:T(8,128)S(1)}, s32[]{:T(128)}, bf16[16,32]{1,0:T(8,128)(2,1)S(1)}, ...), condition=%wide.region_4.5_spmd.clone, body=%wide.region_3.4_spmd.clone.sunk | while | flops 2621476 | bytes 5243305 | solution.py:111
  180.9 7.8 %multiply_reduce_fusion.1 = (f32[512]{0:T(512)S(1)}, f32[512,1,32,64]{0,3,2,1:T(8,128)S(1)}, f32[512,1,32,64]{0,3,2,1:T(8,128)}) fusion(f32[512,1,32,64]{0,3,2,1:T(8,128)} %bitcast.280, f32[512,1,32,64]{0,3,2,1:T(8,128)} %bitcast.281, f32[512,32]{0,1:T(8,128)S(1)} %bitcast_bitcast_fusion, f32[32,64,256]{2,1,0:T(8,128)S(1)} %get-tuple-element.235, ...), kind=kOutput, calls=%fused_computation.44 | convolution fusion | flops 3230662144 | bytes 19204096 | tf_op jit(solution)/shard_map/tgn,ghpn->tghp/dot_general | solution.py:118
  190.9 14.7 %all-reduce.5 = (f32[512]{0:T(512)S(1)}, f32[512]{0:T(512)S(1)}) all-reduce(f32[512]{0:T(512)S(1)} %get-tuple-element.319, f32[512]{0:T(512)S(1)} %fusion.22), channel_id=1, replica_groups=mesh['ctx'=16,'tp'=8] {'tp'}, use_global_device_ids=true, to_apply=%region_8.9 | all-reduce | flops 1024 | bytes 8192 | tf_op jit(solution)/shard_map/psum | solution.py:127
  205.5 5.8 %bitcast_multiply_fusion.1 = (f32[512,2048]{0,1:T(8,128)S(1)}, f32[512,2048]{0,1:T(8,128)}, bf16[512,2048]{0,1:T(8,128)(2,1)}) fusion(f32[512,32]{0,1:T(8,128)S(1)} %bitcast_bitcast_fusion, bf16[512,2048]{0,1:T(8,128)(2,1)S(1)} %copy-done.1, f32[512]{0:T(512)S(1)} %get-tuple-element.326, f32[512,1,32,64]{0,3,2,1:T(8,128)} %copy-done.4, ...), kind=kLoop, calls=%fused_computation.31 | loop fusion | flops 15728640 | bytes 18952192 | tf_op jit(solution)/shard_map/mul | solution.py:137
  213.2 3.1 convolution_convert_fusion
  216.3 4.0 reshape.621
  220.3 6.3 %reshape.620 = f32[2,256,1,32,64]{1,0,4,3,2:T(2,128)} reshape(f32[512,2048]{0,1:T(8,128)} %get-tuple-element.318) | data formatting | bytes 8388608 | tf_op jit(solution)/shard_map/reshape | solution.py:135
  226.6 5.0 %broadcast_multiply_fusion = (f32[2,256,1,32,64]{1,4,3,0,2:T(8,128)S(1)}, f32[2,256,1,32,64]{1,4,3,0,2:T(8,128)S(1)}) fusion(f32[2,256,32]{1,2,0:T(8,128)S(1)} %get-tuple-element.324, f32[2,256,1,32,64]{1,0,4,3,2:T(2,128)} %reshape.621, f32[2,256,1,32,64]{1,0,4,3,2:T(2,128)} %reshape.620), kind=kLoop, calls=%fused_computation.61 | loop fusion | flops 6291456 | bytes 16842752 | tf_op jit(solution)/shard_map/transpose(jvp())/mul | solution.py:65
  231.7 3.4 fusion.55
  235.2 3.7 fusion.52
  238.9 7.4 %multiply_reduce_fusion = bf16[2,256,256]{2,1,0:T(8,128)(2,1)S(1)} fusion(f32[2,32,256]{2,1,0:T(8,128)S(1)} %copy.101, f32[2,32,256]{2,1,0:T(8,128)S(1)} %bitcast.289, pred[256,256]{1,0:T(8,128)(4,1)S(1)} %copy-done.20, bf16[2,256,32,64]{1,3,2,0:T(8,128)(2,1)S(1)} %copy-done.13, f32[2,256,1,32,64]{1,4,3,0,2:T(8,128)S(1)} %get-tuple-element.316), kind=kOutput, calls=%fused_computation.9 | convolution fusion | flops 566099968 | bytes 6750208 | tf_op jit(solution)/shard_map/transpose(jvp(bghqs,bsghp->bqghp))/dot_general | solution.py:44
  248.3 6.5 %fusion.40 = bf16[512,256]{0,1:T(8,128)(2,1)S(1)} fusion(f32[512,256]{0,1:T(8,128)} %copy.122, f32[32,64,256]{2,1,0:T(8,128)} %copy-done, f32[512,32,64]{0,2,1:T(8,128)} %bitcast.276), kind=kOutput, calls=%fused_computation.68 | convolution fusion | flops 3221487616 | bytes 7077888 | tf_op jit(solution)/shard_map/tghp,ghpn->tgn/dot_general | solution.py:156
  255.7 7.5 %multiply_convert_fusion.6 = bf16[512,1,32,64]{0,3,2,1:T(8,128)(2,1)} fusion(f32[512,1,32,64]{0,3,2,1:T(8,128)} %bitcast.274, f32[512,1,32,64]{0,3,2,1:T(8,128)} %get-tuple-element.330, bf16[512,2048]{0,1:T(8,128)(2,1)} %copy.112), kind=kLoop, calls=%fused_computation.40 | loop fusion | flops 11534336 | bytes 12582912 | tf_op jit(solution)/shard_map/convert_element_type | solution.py:162
  263.2 3.9 copy.125
  267.1 3.9 copy.123
  271.0 54.1 %all-gather.8.cloned.1.call-done = bf16[512,64,256]{2,1,0:T(8,128)(2,1)} async-done(((bf16[32,64,256]{2,1,0:T(8,128)(2,1)}), bf16[512,64,256]{2,1,0:T(8,128)(2,1)}) %all-gather.8.cloned.1.call-update) | async-done | bytes 16777232 | tf_op jit(solution)/shard_map/all_gather | solution.py:144
  325.1 36.5 %while.31 = (s32[]{:T(128)}, f32[32,64,256]{2,1,0:T(8,128)S(1)}, s32[]{:T(128)}, bf16[16,32]{1,0:T(8,128)(2,1)S(1)}, bf16[16,32,64,256]{3,2,1,0:T(8,128)(2,1)}, ...) while((s32[]{:T(128)}, f32[32,64,256]{2,1,0:T(8,128)S(1)}, s32[]{:T(128)}, ...), condition=%wide.region_12.13_spmd.clone, body=%wide.region_11.12_spmd.clone.sunk | while | flops 2621480 | bytes 5243367 | solution.py:153
  327.4 2.2 fusion.106
  331.9 2.2 fusion.106
  334.2 2.2 fusion.106
  336.5 2.2 fusion.106
  338.8 2.2 fusion.106
  343.4 2.2 fusion.106
  345.6 2.2 fusion.106
  347.9 2.2 fusion.106
  350.2 2.2 fusion.106
  354.8 2.2 fusion.106
  357.1 2.2 fusion.106
  359.3 2.2 fusion.106
  361.6 2.8 add_bitcast_fusion
  364.4 3.1 fusion.3
  367.6 4.4 %fusion.4 = bf16[2,32,64,256]{3,2,1,0:T(8,128)(2,1)} fusion(f32[2,256,32]{1,2,0:T(8,128)S(1)} %copy-done.22, f32[2,256,256]{2,1,0:T(8,128)S(1)} %convert_element_type.205, f32[1,1,32,64,256]{4,3,2,1,0:T(8,128)S(1)} %add_bitcast_fusion, f32[1,1,32,64,256]{4,3,2,1,0:T(8,128)S(1)} %bitcast.273), kind=kOutput, calls=%fused_computation.13 | convolution fusion | flops 546308096 | bytes 6881280 | tf_op jit(solution)/shard_map/transpose(jvp(bsghp,bsghn->bghpn))/dot_general | solution.py:47
  375.0 8.9 %fusion.26 = bf16[2,256,1,32,64]{1,4,3,0,2:T(8,128)(2,1)S(1)} fusion(f32[2,256,1,32,64]{1,4,3,0,2:T(8,128)} %copy-done.10, bf16[2,32,64,256]{3,2,1,0:T(8,128)(2,1)} %fusion.4, f32[32]{0:T(128)S(1)} %copy-done.24, f32[2,32,256]{2,1,0:T(8,128)S(1)} %copy.101, f32[2,256,256]{2,1,0:T(8,128)S(1)} %copy-done.17, f32[2,32,256]{2,1,0:T(8,128)S(1)} %bitcast.290, ...), kind=kOutput, calls=%fused_computation.49 | convolution fusion | flops 567279616 | bytes 9109632 | tf_op jit(solution)/shard_map/transpose(jvp(bghqs,bsghp->bqghp))/dot_general | solution.py:44
  383.9 6.6 %copy.130 = bf16[2,256,1,32,64]{4,3,1,0,2:T(8,128)(2,1)} copy(bf16[2,256,1,32,64]{1,4,3,0,2:T(8,128)(2,1)S(1)} %fusion.26) | data formatting | bytes 4194304
  390.6 6.7 %reshape.657 = bf16[512,2048]{1,0:T(8,128)(2,1)} reshape(bf16[2,256,1,32,64]{4,3,1,0,2:T(8,128)(2,1)} %copy.130) | data formatting | bytes 4194304
  (154 shorter events, 66.8 us)
Async XLA Ops:
  7.2 137.4 %all-gather.6.cloned.1.call-start = ((), (), s32[]{:S(2)}) async-start(), calls=%async_computation | async-start | bytes 17825792 | tf_op jit(solution)/shard_map/all_gather | solution.py:99
  18.8 4.9 %copy-start.15 = (bf16[512,256]{1,0:T(8,128)(2,1)S(1)}, bf16[512,256]{1,0:T(8,128)(2,1)}, u32[]{:S(2)}) copy-start(bf16[512,256]{1,0:T(8,128)(2,1)} %param.16) | copy-start | bytes 786436
  23.7 3.1 copy-start.11
  24.1 2.8 copy-start.21
  26.9 2.0 copy-start.5
  30.2 294.9 %all-gather.8.cloned.1.call-start = ((), (), s32[]{:S(2)}) async-start(), calls=%async_computation.1 | async-start | bytes 17825792 | tf_op jit(solution)/shard_map/all_gather | solution.py:144
  30.3 7.4 %copy-start.25 = (u32[128]{0:T(128)S(1)}, u32[128]{0:T(128)}, u32[]{:S(2)}) copy-start(u32[128]{0:T(128)} %constant.102) | copy-start | bytes 1540
  82.0 7.9 %copy-start.8 = (bf16[512,256]{1,0:T(8,128)(2,1)S(1)}, bf16[512,256]{1,0:T(8,128)(2,1)}, u32[]{:S(2)}) copy-start(bf16[512,256]{1,0:T(8,128)(2,1)} %param.17) | copy-start | bytes 786436
  89.9 4.8 %copy-start.9 = (f32[2,256,1,32,64]{1,4,3,0,2:T(8,128)S(1)}, f32[2,256,1,32,64]{1,4,3,0,2:T(8,128)}, u32[]{:S(2)}) copy-start(f32[2,256,1,32,64]{1,4,3,0,2:T(8,128)} %copy.108) | copy-start | bytes 12582916
  89.9 4.8 %copy-start.12 = (bf16[2,256,32,64]{1,3,2,0:T(8,128)(2,1)S(1)}, bf16[2,256,32,64]{1,3,2,0:T(8,128)(2,1)}, u32[]{:S(2)}) copy-start(bf16[2,256,32,64]{1,3,2,0:T(8,128)(2,1)} %copy-done.11) | copy-start | bytes 6291460
  89.9 4.9 %copy-start.24 = (f32[32]{0:T(128)S(1)}, f32[32]{0:T(128)}, u32[]{:S(2)}) copy-start(f32[32]{0:T(128)} %param.19) | copy-start | bytes 388
  90.0 10.2 %copy-start.19 = (pred[256,256]{1,0:T(8,128)(4,1)}, pred[256,256]{1,0:T(8,128)(4,1)S(1)}, u32[]{:S(2)}) copy-start(pred[256,256]{1,0:T(8,128)(4,1)S(1)} %iota_compare_fusion) | copy-start | bytes 196612
  94.7 5.4 %copy-start.16 = (f32[2,256,256]{2,1,0:T(8,128)}, f32[2,256,256]{2,1,0:T(8,128)S(1)}, u32[]{:S(2)}) copy-start(f32[2,256,256]{2,1,0:T(8,128)S(1)} %fusion.83) | copy-start | bytes 1572868
  180.9 7.9 %copy-start = (f32[32,64,256]{2,1,0:T(8,128)}, f32[32,64,256]{2,1,0:T(8,128)S(1)}, u32[]{:S(2)}) copy-start(f32[32,64,256]{2,1,0:T(8,128)S(1)} %get-tuple-element.235) | copy-start | bytes 6291460
  180.9 7.9 %copy-start.2 = (bf16[512,2048]{0,1:T(8,128)(2,1)S(1)}, bf16[512,2048]{0,1:T(8,128)(2,1)}, u32[]{:S(2)}) copy-start(bf16[512,2048]{0,1:T(8,128)(2,1)} %copy.113) | copy-start | bytes 6291460
  180.9 7.9 %copy-start.23 = (f32[2048]{0:T(1024)S(1)}, f32[2048]{0:T(1024)}, u32[]{:S(2)}) copy-start(f32[2048]{0:T(1024)} %param.20) | copy-start | bytes 24580
  188.7 2.1 copy-start.4
  188.7 16.8 %copy-start.1 = (bf16[512,2048]{0,1:T(8,128)(2,1)S(1)}, bf16[512,2048]{0,1:T(8,128)(2,1)}, u32[]{:S(2)}) copy-start(bf16[512,2048]{0,1:T(8,128)(2,1)} %copy.112) | copy-start | bytes 6291460
  211.3 2.0 copy-start.3
  226.6 8.5 %copy-start.6 = (f32[2,32,64,256]{3,2,1,0:T(8,128)S(1)}, f32[2,32,64,256]{3,2,1,0:T(8,128)}, u32[]{:S(2)}) copy-start(f32[2,32,64,256]{3,2,1,0:T(8,128)} %copy-done.5) | copy-start | bytes 12582916
  231.7 7.1 %copy-start.7 = (f32[2,256,1,32,64]{1,4,3,0,2:T(8,128)}, f32[2,256,1,32,64]{1,4,3,0,2:T(8,128)S(1)}, u32[]{:S(2)}) copy-start(f32[2,256,1,32,64]{1,4,3,0,2:T(8,128)S(1)} %get-tuple-element.315) | copy-start | bytes 12582916
  231.7 7.1 %copy-start.10 = (f32[2,256,1,32,64]{1,4,3,0,2:T(8,128)}, f32[2,256,1,32,64]{1,4,3,0,2:T(8,128)S(1)}, u32[]{:S(2)}) copy-start(f32[2,256,1,32,64]{1,4,3,0,2:T(8,128)S(1)} %get-tuple-element.316) | copy-start | bytes 12582916
  231.7 7.1 %copy-start.13 = (bf16[2,256,32,64]{1,3,2,0:T(8,128)(2,1)S(1)}, bf16[2,256,32,64]{1,3,2,0:T(8,128)(2,1)}, u32[]{:S(2)}) copy-start(bf16[2,256,32,64]{1,3,2,0:T(8,128)(2,1)} %copy-done.11) | copy-start | bytes 6291460
  231.7 7.1 %copy-start.20 = (pred[256,256]{1,0:T(8,128)(4,1)S(1)}, pred[256,256]{1,0:T(8,128)(4,1)}, u32[]{:S(2)}) copy-start(pred[256,256]{1,0:T(8,128)(4,1)} %copy-done.19) | copy-start | bytes 196612
  246.3 0.7 copy-start.18
  361.6 2.8 copy-start.14
  361.6 2.8 copy-start.22
  367.6 7.5 %copy-start.17 = (f32[2,256,256]{2,1,0:T(8,128)S(1)}, f32[2,256,256]{2,1,0:T(8,128)}, u32[]{:S(2)}) copy-start(f32[2,256,256]{2,1,0:T(8,128)} %copy-done.16) | copy-start | bytes 1572868
Sparse Core Ops, SparseCore 0:
  30.3 114.1 all-gather.5
  216.4 108.5 all-gather.7
where the time goes:
time: 413 us; the launch traced here: 405 us
  other arithmetic  101 us (24%)
  waiting for transfers between devices  82.4 us (20%)
  local copies, waits for them, and re-layouts  81 us (20%)
  matrix products  66.2 us (16%)
  blocking collectives  57.4 us (14%)
  between operations  15.8 us (4%)
    all_gather x1, waiting for transfers between devices, body(): all_grads = lax.all_gather(local_grad[None], 'ctx', axis=0, tiled=True)  54.1 us
    unnamed x1, blocking collectives  42.7 us
    unnamed x62, local copies, waits for them, and re-layouts  37.1 us
    select_n x16, other arithmetic, backward_turn(): return jnp.where(segment > position, updated, running)  35.6 us
    select_n x16, other arithmetic, forward_turn(): return jnp.where(segment < position, updated, running)  35.6 us
    all_gather x1, waiting for transfers between devices, body(): lax.all_gather(local_end[None], 'ctx', axis=0, tiled=True)  28.3 us
    dot_general x3, matrix products, segment_parts(): jnp.einsum('bghqs,bsghp->bqghp', weights, values, preferred_element_type=...  21.7 us
    convert_element_type x2, local copies, waits for them, and re-layouts, segment_parts(): mixed_out = within + carried + skip_heads * values.astype(jnp.float32)  15.3 us
  transfers between devices with their start and end apart: 2, of which 2 were waited for; matrix products, arithmetic and copies ran while one was open for 24% of the time, Pallas kernels for 0%

commit v1 on v0

v1 whole, which is shorter than its diff:
```python
import jax
import jax.numpy as jnp
from jax import lax
from jax.experimental import pallas as pl
from jax.experimental.pallas import tpu as pltpu
from jax.sharding import PartitionSpec as P

H = 256
P_SIZE = 64
N = 256
EPS = 1e-05
LOG2E = 1.4426950408889634

SEGS = 16
PARTS = 8
TOK = 512
HEADS = 32
COLS = HEADS * P_SIZE
SLICE = 128
TAIL = 16
WIDE = 256
STEPS = COLS // WIDE
HPS = WIDE // P_SIZE
SUB = 128
BLKS = TOK // SUB
HALF = TOK // 2

F32 = jnp.float32
BF16 = jnp.bfloat16
END, START, MIDDLE, QUARTER = range(4)


def nn(a, b):
    return jnp.dot(a, b, preferred_element_type=F32)


def nt(a, b):
    return lax.dot_general(a, b, (((1,), (1,)), ((), ())), preferred_element_type=F32)


def transposed(a):
    return a.astype(F32).T.astype(a.dtype)


def split(a):
    high = a.astype(BF16)
    return high, (a - high.astype(F32)).astype(BF16)


def expand(factors, which, step):
    row = lax.broadcasted_iota(jnp.int32, (2 * SLICE, WIDE), 0)
    head = (lax.broadcasted_iota(jnp.int32, (2 * SLICE, WIDE), 1) >> 6) + HPS * step
    pick = jnp.where((row & 127) == head + HEADS * which, 1.0, 0.0).astype(BF16)
    return nn(factors, pick)


def two_heads(a):
    lane = lax.broadcasted_iota(jnp.int32, a.shape, 1)
    zero = jnp.zeros_like(a)
    return jnp.concatenate([jnp.where(lane < P_SIZE, a, zero), jnp.where(lane < P_SIZE, zero, a)], 0)


def blk(i):
    return slice(i * SUB, (i + 1) * SUB)


def ends_kernel(step_ref, rate_ref, x_ref, keys_ref, out_ref, fac_ref, col_ref, row_ref, keys_t):
    step = pl.program_id(0)

    @pl.when(step == 0)
    def _():
        steps = step_ref[...]
        logs = steps * (rate_ref[...] * -LOG2E)
        high, rest = split(logs)
        rest = logs - high.astype(F32)
        mid, low = split(rest)
        source = lax.broadcasted_iota(jnp.int32, (TOK, TOK), 0)
        target = lax.broadcasted_iota(jnp.int32, (TOK, TOK), 1)
        upper = jnp.where(source <= target, 1.0, 0.0).astype(BF16)
        sums = nn(jnp.concatenate([high.astype(F32), mid.astype(F32), low.astype(F32)], 0).astype(BF16), upper)
        cum = sums[:HEADS] + sums[HEADS : 2 * HEADS] + sums[2 * HEADS :]
        shifted = cum - jnp.log(steps) * LOG2E
        token = lax.broadcasted_iota(jnp.int32, (HEADS, TOK), 1)
        one = jnp.ones_like(steps)
        end = jnp.exp2(cum[:, TOK - 1 :] - cum) * steps
        start = jnp.exp2(cum)
        middle = jnp.exp2(-jnp.abs(cum - cum[:, HALF - 1 : HALF])) * jnp.where(token < HALF, steps, one)
        near = jnp.where(token < HALF, cum[:, SUB - 1 : SUB], cum[:, 3 * SUB - 1 : 3 * SUB])
        quarter = jnp.exp2(-jnp.abs(cum - near)) * jnp.where((token & SUB) == 0, steps, one)
        high, low = split(jnp.concatenate([end, start, middle, quarter], 0).T)
        fac_ref[:, :128] = high
        fac_ref[:, 128:] = low
        col_ref[...] = jnp.concatenate([cum, shifted, cum, shifted], 0).T
        for part in range(STEPS):
            heads = slice(part * HPS, (part + 1) * HPS)
            row_ref[part] = jnp.concatenate([cum[heads], shifted[heads]], 0)
        keys_t[...] = transposed(keys_ref[...])

    factors = fac_ref[...]
    scaled = (x_ref[...].astype(F32) * expand(factors, END, step)).astype(BF16)
    ends = nn(keys_t[...], scaled).astype(BF16)
    decay = expand(factors[TOK - 16 :], START, step)
    decay = jnp.broadcast_to(decay[15:16], (TAIL, WIDE)).astype(BF16)
    for part in range(WIDE // SLICE):
        lanes = slice(part * SLICE, (part + 1) * SLICE)
        out_ref[part, :N] = ends[:, lanes]
        out_ref[part, N:] = decay[:, lanes]


def weights(col, row, scores):
    return (jnp.exp2(jnp.minimum(col - row, 0.0)) * scores).astype(BF16)


def local_kernel(x_ref, keys_ref, queries_ref, fac_ref, col_ref, row_ref, skip_ref, out_ref, near, off1, off2):
    step = pl.program_id(0)

    @pl.when(step == 0)
    def _():
        target = lax.broadcasted_iota(jnp.int32, (SUB, SUB), 0)
        source = lax.broadcasted_iota(jnp.int32, (SUB, SUB), 1)
        for i in range(BLKS):
            scores = nt(queries_ref[blk(i)], keys_ref[blk(i)])
            near[i] = jnp.where(source <= target, scores, 0.0)
        for i in range(BLKS // 2):
            off1[i] = nt(queries_ref[blk(2 * i + 1)], keys_ref[blk(2 * i)]).astype(BF16)
        off2[...] = nt(queries_ref[HALF:], keys_ref[:HALF]).astype(BF16)

    factors = fac_ref[...]
    x = x_ref[...]
    wide = x.astype(F32)
    middle = expand(factors, MIDDLE, step)
    quarter = expand(factors, QUARTER, step)
    cols = pltpu.roll(col_ref[...], lax.rem(128 - HPS * step, 128), 1)
    far = nn(off2[...], (wide[:HALF] * middle[:HALF]).astype(BF16)) * middle[HALF:]
    skip = skip_ref[...] * wide
    for i in range(BLKS):
        total = skip[blk(i)]
        if i % 2:
            before = (wide[blk(i - 1)] * quarter[blk(i - 1)]).astype(BF16)
            total += nn(off1[i // 2], before) * quarter[blk(i)]
        if i >= 2:
            total += far[blk(i - 2)]
        scores = near[i]
        for pair in range(WIDE // SLICE):
            lanes = slice(pair * SLICE, (pair + 1) * SLICE)
            both = []
            for j in (2 * pair, 2 * pair + 1):
                row = row_ref[0, HPS + j : HPS + j + 1, blk(i)]
                both.append(weights(cols[blk(i), j : j + 1], row, scores))
            within = nn(jnp.concatenate(both, 1), two_heads(x[blk(i), lanes]))
            out_ref[blk(i), lanes] = total[:, lanes] + within


def forward_scan_kernel(in_ref, out_ref):
    running = jnp.zeros((N, SLICE), F32)
    for k in range(SEGS):
        out_ref[k] = running.astype(BF16)
        decay = in_ref[k, N : N + TAIL][:1].astype(F32)
        running = running * decay + in_ref[k, :N].astype(F32)


def backward_scan_kernel(in_ref, decay_ref, out_ref):
    running = jnp.zeros((N, SLICE), F32)
    for k in reversed(range(SEGS)):
        out_ref[k] = running.astype(BF16)
        running = running * decay_ref[k][:1].astype(F32) + in_ref[k].astype(F32)


def state_of(ref):
    return jnp.concatenate([ref[part] for part in range(WIDE // SLICE)], 1)


def gate_kernel(local_ref, state_ref, queries_ref, fac_ref, gate_ref, gain_ref, grad_ref, mixed_ref, sums_ref, square, product):
    step = pl.program_id(0)

    @pl.when(step == 0)
    def _():
        square[...] = jnp.zeros_like(square)
        product[...] = jnp.zeros_like(product)

    carried = nn(queries_ref[...], state_of(state_ref)) * expand(fac_ref[...], START, step)
    mixed = local_ref[...] + carried
    mixed_ref[...] = mixed
    gate = gate_ref[...].astype(F32)
    gated = mixed * (gate * jax.nn.sigmoid(gate))
    squares = gated * gated
    products = gated * (gain_ref[...] * grad_ref[...].astype(F32))
    square[...] += squares[:, :128] + squares[:, 128:]
    product[...] += products[:, :128] + products[:, 128:]

    @pl.when(step == STEPS - 1)
    def _():
        both = jnp.concatenate(
            [jnp.sum(square[...].T, axis=0, keepdims=True), jnp.sum(product[...].T, axis=0, keepdims=True)], 0
        )
        for part in range(PARTS):
            sums_ref[part] = both


def norm_terms(sums_ref, inverse, slope):
    total = sums_ref[0]
    for part in range(1, PARTS):
        total += sums_ref[part]
    inv_rms = lax.rsqrt(total[:1] / (H * P_SIZE) + EPS)
    ratio = inv_rms * inv_rms * inv_rms * total[1:] / (H * P_SIZE)
    inverse[...] = jnp.broadcast_to(inv_rms, (128, TOK)).T
    slope[...] = jnp.broadcast_to(ratio, (128, TOK)).T


def wide_of(ref):
    return jnp.concatenate([ref[...]] * (WIDE // 128), 1)


def grad_kernel(mixed_ref, sums_ref, queries_ref, fac_ref, gate_ref, gain_ref, grad_ref, dy_ref, out_ref, inverse, slope, queries_t):
    step = pl.program_id(0)

    @pl.when(step == 0)
    def _():
        norm_terms(sums_ref, inverse, slope)
        queries_t[...] = transposed(queries_ref[...])

    gate = gate_ref[...].astype(F32)
    silu = gate * jax.nn.sigmoid(gate)
    gated = mixed_ref[...] * silu
    grad_gated = wide_of(inverse) * (gain_ref[...] * grad_ref[...].astype(F32)) - gated * wide_of(slope)
    dy = grad_gated * silu
    dy_ref[...] = dy.astype(BF16)
    weighted = (dy * expand(fac_ref[...], START, step)).astype(BF16)
    local = nn(queries_t[...], weighted).astype(BF16)
    for part in range(WIDE // SLICE):
        out_ref[part] = local[:, part * SLICE : (part + 1) * SLICE]


def norm_kernel(mixed_ref, sums_ref, gate_ref, gain_ref, grad_ref, normed_ref, out_ref, inverse, slope):
    step = pl.program_id(0)

    @pl.when(step == 0)
    def _():
        norm_terms(sums_ref, inverse, slope)

    gate = gate_ref[...].astype(F32)
    sig = jax.nn.sigmoid(gate)
    mixed = mixed_ref[...]
    gated = mixed * (gate * sig)
    gain = wide_of(inverse) * gain_ref[...]
    normed_ref[...] = (gated * gain).astype(BF16)
    grad_gated = gain * grad_ref[...].astype(F32) - gated * wide_of(slope)
    out_ref[...] = (grad_gated * mixed * (sig * (1.0 + gate * (1.0 - sig)))).astype(BF16)


def back_kernel(
    x_ref, dy_ref, state_ref, keys_ref, queries_ref, fac_ref, col_ref, row_ref, skip_ref,
    dx_ref, scaled_ref, dkeys_ref, dqueries_ref,
    near, off1, off2, dnear, doff1, doff2, dq,
):
    step = pl.program_id(0)

    @pl.when(step == 0)
    def _():
        source = lax.broadcasted_iota(jnp.int32, (SUB, SUB), 0)
        target = lax.broadcasted_iota(jnp.int32, (SUB, SUB), 1)
        for i in range(BLKS):
            scores = nt(keys_ref[blk(i)], queries_ref[blk(i)])
            near[i] = jnp.where(source <= target, scores, 0.0)
        for i in range(BLKS // 2):
            off1[i] = nt(keys_ref[blk(2 * i)], queries_ref[blk(2 * i + 1)]).astype(BF16)
        off2[...] = nt(keys_ref[:HALF], queries_ref[HALF:]).astype(BF16)
        dnear[...] = jnp.zeros_like(dnear)
        doff1[...] = jnp.zeros_like(doff1)
        doff2[...] = jnp.zeros_like(doff2)
        dq[...] = jnp.zeros_like(dq)

    factors = fac_ref[...]
    x = x_ref[...]
    wide = x.astype(F32)
    dy = dy_ref[...]
    dwide = dy.astype(F32)
    scaled_ref[...] = (wide * expand(factors, END, step)).astype(BF16)
    weighted = (dwide * expand(factors, START, step)).astype(BF16)
    dq[...] += nt(weighted, state_of(state_ref))
    middle = expand(factors, MIDDLE, step)
    quarter = expand(factors, QUARTER, step)
    cols = pltpu.roll(col_ref[...], lax.rem(128 - HPS * step, 128), 1)
    above = (wide[:HALF] * middle[:HALF]).astype(BF16)
    below = (dwide[HALF:] * middle[HALF:]).astype(BF16)
    far = nn(off2[...], below) * middle[:HALF]
    doff2[...] += nt(above, below)
    skip = skip_ref[...] * dwide
    for i in range(BLKS):
        total = skip[blk(i)]
        if i % 2 == 0:
            above = (wide[blk(i)] * quarter[blk(i)]).astype(BF16)
            below = (dwide[blk(i + 1)] * quarter[blk(i + 1)]).astype(BF16)
            total += nn(off1[i // 2], below) * quarter[blk(i)]
            doff1[i // 2] += nt(above, below)
        if i < 2:
            total += far[blk(i)]
        scores = near[i]
        dscores = dnear[i]
        for pair in range(WIDE // SLICE):
            lanes = slice(pair * SLICE, (pair + 1) * SLICE)
            dy_two = two_heads(dy[blk(i), lanes])
            dweights = nt(x[blk(i), lanes], dy_two)
            both = []
            for place, j in enumerate((2 * pair, 2 * pair + 1)):
                row = row_ref[0, j : j + 1, blk(i)]
                decay = jnp.exp2(jnp.minimum(row - cols[blk(i), HEADS + j : HEADS + j + 1], 0.0))
                both.append((decay * scores).astype(BF16))
                dscores += decay * dweights[:, place * SUB : (place + 1) * SUB]
            dx_ref[blk(i), lanes] = total[:, lanes] + nn(jnp.concatenate(both, 1), dy_two)
        dnear[i] = dscores

    @pl.when(step == STEPS - 1)
    def _():
        source = lax.broadcasted_iota(jnp.int32, (SUB, SUB), 0)
        target = lax.broadcasted_iota(jnp.int32, (SUB, SUB), 1)
        last = doff2[...]
        dkeys_ref[...] = jnp.zeros_like(dkeys_ref)
        dkeys_ref[:HALF] += nn(last.astype(BF16), queries_ref[HALF:])
        dq[HALF:] += nn(last.T.astype(BF16), keys_ref[:HALF])
        for i in range(BLKS // 2):
            part = doff1[i]
            dkeys_ref[blk(2 * i)] += nn(part.astype(BF16), queries_ref[blk(2 * i + 1)])
            dq[blk(2 * i + 1)] += nn(part.T.astype(BF16), keys_ref[blk(2 * i)])
        for i in range(BLKS):
            part = jnp.where(source <= target, dnear[i], 0.0)
            dkeys_ref[blk(i)] += nn(part.astype(BF16), queries_ref[blk(i)])
            dq[blk(i)] += nn(part.T.astype(BF16), keys_ref[blk(i)])
        dqueries_ref[...] = dq[...].astype(BF16)


def final_kernel(dx_ref, scaled_ref, grad_ref, keys_ref, fac_ref, dkeys_ref, out_ref, out_keys_ref, total):
    step = pl.program_id(0)

    @pl.when(step == 0)
    def _():
        total[...] = dkeys_ref[...]

    state_grad = state_of(grad_ref)
    from_end = nn(keys_ref[...], state_grad) * expand(fac_ref[...], END, step)
    out_ref[...] = (dx_ref[...] + from_end).astype(BF16)
    total[...] += nt(scaled_ref[...], state_grad)

    @pl.when(step == STEPS - 1)
    def _():
        out_keys_ref[...] = total[...].astype(BF16)


def whole(shape):
    return pl.BlockSpec(shape, lambda i: (0,) * len(shape))


TOKENS_BY_STEP = pl.BlockSpec((TOK, WIDE), lambda i: (0, i))
ROW_BY_STEP = pl.BlockSpec((1, WIDE), lambda i: (0, i))
MAP = whole((TOK, N))
FACTORS = whole((TOK, 2 * SLICE))
COLUMNS = whole((TOK, 128))
ROWS = whole((STEPS, 2 * HPS, TOK))
ROWS_BY_STEP = pl.BlockSpec((1, 2 * HPS, TOK), lambda i: (i, 0, 0))
SUMS = whole((PARTS, 2, TOK))


def state_by_step(rows):
    return pl.BlockSpec((WIDE // SLICE, rows, SLICE), lambda i: (i, 0, 0))


def shape(*dims, dtype=F32):
    return jax.ShapeDtypeStruct(dims, dtype)


def call(kernel, name, in_specs, out_specs, out_shape, scratch=(), gmacs=1.0, mib=8.0, limit=24):
    return pl.pallas_call(
        kernel,
        name=name,
        grid=(STEPS,),
        in_specs=in_specs,
        out_specs=out_specs,
        out_shape=out_shape,
        scratch_shapes=list(scratch),
        compiler_params=pltpu.CompilerParams(vmem_limit_bytes=limit << 20),
        cost_estimate=pl.CostEstimate(flops=int(2e9 * gmacs), bytes_accessed=int(mib * 2**20), transcendentals=0),
    )


def whole_call(kernel, name, in_specs, out_specs, out_shape):
    return pl.pallas_call(
        kernel,
        name=name,
        grid=(1,),
        in_specs=in_specs,
        out_specs=out_specs,
        out_shape=out_shape,
        compiler_params=pltpu.CompilerParams(vmem_limit_bytes=16 << 20),
        cost_estimate=pl.CostEstimate(flops=2**24, bytes_accessed=2**21, transcendentals=0),
    )


def exchange(a, axis):
    return lax.all_to_all(a, axis, 0, 0)


def body(inputs, gate_input, step_size, input_map, output_map, decay_rate, skip_weight, norm_gain, out_grad):
    rate = decay_rate.reshape(HEADS, 1)
    gain = norm_gain.reshape(1, COLS)
    skip = jnp.repeat(skip_weight, P_SIZE).reshape(1, COLS)
    tokens = shape(TOK, COLS)
    tokens_out = shape(TOK, COLS, dtype=BF16)
    score_scratch = [
        pltpu.VMEM((BLKS, SUB, SUB), F32),
        pltpu.VMEM((BLKS // 2, SUB, SUB), BF16),
        pltpu.VMEM((HALF, HALF), BF16),
    ]
    norm_scratch = [pltpu.VMEM((TOK, 128), F32)] * 2

    ends, factors, columns, rows = call(
        ends_kernel,
        "segment_ends",
        [whole((HEADS, TOK)), whole((HEADS, 1)), TOKENS_BY_STEP, MAP],
        [state_by_step(N + TAIL), FACTORS, COLUMNS, ROWS],
        [shape(SEGS, N + TAIL, SLICE, dtype=BF16), shape(TOK, 2 * SLICE, dtype=BF16), shape(TOK, 128), shape(STEPS, 2 * HPS, TOK)],
        [pltpu.VMEM((N, TOK), BF16)],
    )(step_size, rate, inputs, input_map)
    all_ends = exchange(ends, "ctx")

    mixed_local = call(
        local_kernel,
        "within_segment",
        [TOKENS_BY_STEP, MAP, MAP, FACTORS, COLUMNS, ROWS_BY_STEP, ROW_BY_STEP],
        TOKENS_BY_STEP,
        tokens,
        score_scratch,
        gmacs=4.0,
    )(inputs, input_map, output_map, factors, columns, rows, skip)

    starts = whole_call(
        forward_scan_kernel,
        "forward_scan",
        [whole((SEGS, N + TAIL, SLICE))],
        whole((SEGS, N, SLICE)),
        shape(SEGS, N, SLICE, dtype=BF16),
    )(all_ends)
    state_in = exchange(starts, "ctx")

    mixed, sums = call(
        gate_kernel,
        "carry_and_gate",
        [TOKENS_BY_STEP, state_by_step(N), MAP, FACTORS, TOKENS_BY_STEP, ROW_BY_STEP, TOKENS_BY_STEP],
        [TOKENS_BY_STEP, SUMS],
        [tokens, shape(PARTS, 2, TOK)],
        norm_scratch,
    )(mixed_local, state_in, output_map, factors, gate_input, gain, out_grad)
    sums = exchange(sums, "tp")

    dy, local_grads = call(
        grad_kernel,
        "local_grads",
        [TOKENS_BY_STEP, SUMS, MAP, FACTORS, TOKENS_BY_STEP, ROW_BY_STEP, TOKENS_BY_STEP],
        [TOKENS_BY_STEP, state_by_step(N)],
        [tokens_out, shape(SEGS, N, SLICE, dtype=BF16)],
        norm_scratch + [pltpu.VMEM((N, TOK), BF16)],
    )(mixed, sums, output_map, factors, gate_input, gain, out_grad)
    all_grads = exchange(local_grads, "ctx")

    normed, grad_gate = call(
        norm_kernel,
        "normed_and_gate",
        [TOKENS_BY_STEP, SUMS, TOKENS_BY_STEP, ROW_BY_STEP, TOKENS_BY_STEP],
        [TOKENS_BY_STEP, TOKENS_BY_STEP],
        [tokens_out, tokens_out],
        norm_scratch,
    )(mixed, sums, gate_input, gain, out_grad)

    dx, scaled, dkeys, dqueries = call(
        back_kernel,
        "within_segment_back",
        [TOKENS_BY_STEP, TOKENS_BY_STEP, state_by_step(N), MAP, MAP, FACTORS, COLUMNS, ROWS_BY_STEP, ROW_BY_STEP],
        [TOKENS_BY_STEP, TOKENS_BY_STEP, MAP, MAP],
        [tokens, tokens_out, shape(TOK, N), shape(TOK, N, dtype=BF16)],
        score_scratch
        + [
            pltpu.VMEM((BLKS, SUB, SUB), F32),
            pltpu.VMEM((BLKS // 2, SUB, SUB), F32),
            pltpu.VMEM((HALF, HALF), F32),
            pltpu.VMEM((TOK, N), F32),
        ],
        gmacs=6.0,
    )(inputs, dy, state_in, input_map, output_map, factors, columns, rows, skip)

    grad_starts = whole_call(
        backward_scan_kernel,
        "backward_scan",
        [whole((SEGS, N, SLICE)), pl.BlockSpec((SEGS, TAIL, SLICE), lambda i: (0, N // TAIL, 0))],
        whole((SEGS, N, SLICE)),
        shape(SEGS, N, SLICE, dtype=BF16),
    )(all_grads, all_ends)
    state_grad = exchange(grad_starts, "ctx")

    grad_inputs, grad_keys = call(
        final_kernel,
        "final_grads",
        [TOKENS_BY_STEP, TOKENS_BY_STEP, state_by_step(N), MAP, FACTORS, MAP],
        [TOKENS_BY_STEP, MAP],
        [tokens_out, shape(TOK, N, dtype=BF16)],
        [pltpu.VMEM((TOK, N), F32)],
    )(dx, scaled, state_grad, input_map, factors, dkeys)
    return normed, grad_inputs, grad_gate, grad_keys, dqueries


def solution(mesh):
    both = P("ctx", "tp")
    return jax.shard_map(
        body,
        mesh=mesh,
        in_specs=(both, both, P("tp", "ctx"), both, both, P("tp"), P("tp"), P("tp"), both),
        out_specs=(both,) * 5,
        check_vma=False,
    )
```

time: 413 us -> 148 us (0.36); the launches traced: 405 us -> 146 us
  other arithmetic: 101 us -> 0 us
  waiting for transfers between devices: 82.4 us -> 10.9 us
  matrix products: 66.2 us -> 0 us
  Pallas kernels: 0 us -> 50.1 us
  local copies, waits for them, and re-layouts: 81 us -> 36.3 us
  blocking collectives: 57.4 us -> 35.4 us
  between operations: 15.8 us -> 0.8 us
  starting transfers between devices: 0.08 us -> 12.6 us
    all_gather x2 -> x0, waiting for transfers between devices: 82.4 us -> none  [the longest x1 54.1 us: body(): all_grads = lax.all_gather(local_grad[None], 'ctx', axis=0, tiled=True)]
    select_n x32 -> x0, other arithmetic: 71.2 us -> none  [the longest x16 35.6 us: backward_turn(): return jnp.where(segment > position, updated, running)]
    dot_general x17 -> x0, matrix products: 66.2 us -> none  [the longest x3 21.7 us: segment_parts(): jnp.einsum('bghqs,bsghp->bqghp', weights, values, preferred_element_type=...]
    pallas_call x0 -> x9, Pallas kernels: none -> 50.1 us  [the longest x1 12.7 us: body(): call(back_kernel, 'within_segment_back', [TOKENS_BY_STEP, TOKENS_BY_STEP,...]
    unnamed x1 -> x0, blocking collectives: 42.7 us -> none
    all_to_all x0 -> x2, blocking collectives: none -> 35.4 us  [exchange(): return lax.all_to_all(a, axis, 0, 0)]
    convert_element_type x3 -> x0, local copies, waits for them, and re-layouts: 16.3 us -> none  [the longest x2 15.3 us: segment_parts(): mixed_out = within + carried + skip_heads * values.astype(jnp.float32)]
    psum x1 -> x0, blocking collectives: 14.7 us -> none  [body(): squares = lax.psum(jnp.sum(gated_out * gated_out, axis=1), 'tp')]
  transfers between devices with their start and end apart: 2 -> 3, of which waited for: 2 -> 2; matrix products, arithmetic and copies ran while one was open for 24% -> 0% of each run, Pallas kernels for 0% -> 17%
where the time goes in v1:
time: 148 us; the launch traced here: 146 us
  Pallas kernels  50.1 us (34%)
  local copies, waits for them, and re-layouts  36.3 us (25%)
  blocking collectives  35.4 us (24%)
  starting transfers between devices  12.6 us (9%)
  waiting for transfers between devices  10.9 us (7%)
    unnamed x68, local copies, waits for them, and re-layouts  35.4 us
    all_to_all x2, blocking collectives, exchange(): return lax.all_to_all(a, axis, 0, 0)  35.4 us
    pallas_call x1, Pallas kernels, body(): call(back_kernel, 'within_segment_back', [TOKENS_BY_STEP, TOKENS_BY_STEP,...  12.7 us
    all_to_all x3, starting transfers between devices, exchange(): return lax.all_to_all(a, axis, 0, 0)  12.6 us
    all_to_all x3, waiting for transfers between devices, exchange(): return lax.all_to_all(a, axis, 0, 0)  10.9 us
    pallas_call x1, Pallas kernels, body(): call(gate_kernel, 'carry_and_gate', [TOKENS_BY_STEP, state_by_step(N), MA...  6.37 us
    pallas_call x1, Pallas kernels, body(): call(local_kernel, 'within_segment', [TOKENS_BY_STEP, MAP, MAP, FACTORS,...  6.37 us
    pallas_call x1, Pallas kernels, body(): call(grad_kernel, 'local_grads', [TOKENS_BY_STEP, SUMS, MAP, FACTORS, TOK...  5.54 us
  transfers between devices with their start and end apart: 3, of which 2 were waited for; matrix products, arithmetic and copies ran while one was open for 0% of the time, Pallas kernels for 17%

profile of v1, /device:TPU:0, one launch (start us, length us, event | category | flops | bytes accessed | tf_op | source)
XLA Modules:
  0.0 146.1 jit_solution(10764035698750048662)
XLA Ops:
  0.6 0.7 copy.14.rate_ref
  1.4 0.9 copy-done.16
  2.3 1.6 %copy-done.21 = bf16[512,2048]{1,0:T(8,128)(2,1)S(1)} copy-done((bf16[512,2048]{1,0:T(8,128)(2,1)S(1)}, bf16[512,2048]{1,0:T(8,128)(2,1)}, u32[]{:S(2)}) %copy-start.21) | copy-done | bytes 2097176
  3.9 0.8 copy-done.26
  4.8 4.7 %segment_ends.1 = (bf16[16,272,128]{2,1,0:T(8,128)(2,1)S(1)}, bf16[512,256]{1,0:T(8,128)(2,1)S(1)}, f32[512,128]{1,0:T(8,128)S(1)}, f32[8,8,512]{2,1,0:T(8,128)S(1)}) custom-call(f32[32,512]{1,0:T(8,128)S(1)} %copy-done.26, f32[32,1]{1,0:T(8,128)S(1)} %copy.14.rate_ref, bf16[512,2048]{1,0:T(8,128)(2,1)S(1)} %copy-done.21, bf16[512,256]{1,0:T(8,128)(2,1)S(1)} %copy-done.16), custom_call_target="tpu_custom_call" | custom-call | flops 2000000000 | bytes 8388608 | tf_op jit(solution)/shard_map/segment_ends/pallas_call | solution.py:415
  9.5 0.0 copy-start.27
  9.5 0.0 copy-start.30
  9.5 25.7 %all_to_all.25.in_ref.decay_ref = bf16[16,272,128]{2,1,0:T(8,128)(2,1)S(1)} all-to-all(bf16[16,272,128]{2,1,0:T(8,128)(2,1)S(1)} %get-tuple-element.24), channel_id=1, replica_groups=mesh['ctx'=16,'tp'=8] {'ctx'}, dimensions={0} | all-to-all | bytes 2228224 | tf_op jit(solution)/shard_map/all_to_all | solution.py:399
  35.2 1.2 forward_scan.1
  36.4 4.3 %all-to-all-start.1 = ((bf16[16,256,128]{2,1,0:T(8,128)(2,1)}), bf16[16,256,128]{2,1,0:T(8,128)(2,1)}, u32[]{:S(2)}, u32[]{:S(2)}) async-start(bf16[16,256,128]{2,1,0:T(8,128)(2,1)} %forward_scan.1), calls=%async_computation.1 | async-start | bytes 2097152 | tf_op jit(solution)/shard_map/all_to_all | solution.py:399
  40.7 0.1 broadcast_in_dim.3
  40.8 0.1 reshape_reshape.3.skip_ref
  40.9 0.9 copy-done.10
  41.8 0.9 copy-done.17
  42.8 1.6 %copy-done.22 = bf16[512,2048]{1,0:T(8,128)(2,1)S(1)} copy-done((bf16[512,2048]{1,0:T(8,128)(2,1)S(1)}, bf16[512,2048]{1,0:T(8,128)(2,1)}, u32[]{:S(2)}) %copy-start.22) | copy-done | bytes 2097176
  44.4 0.9 copy-done.28
  45.3 0.9 copy-done.31
  46.2 6.4 %within_segment.1.local_ref = f32[512,2048]{1,0:T(8,128)S(1)} custom-call(bf16[512,2048]{1,0:T(8,128)(2,1)S(1)} %copy-done.22, bf16[512,256]{1,0:T(8,128)(2,1)S(1)} %copy-done.17, bf16[512,256]{1,0:T(8,128)(2,1)S(1)} %copy-done.10, bf16[512,256]{1,0:T(8,128)(2,1)S(1)} %get-tuple-element.21.fac_ref, f32[512,128]{1,0:T(8,128)S(1)} %copy-done.28, ...), custom_call_target="tpu_custom_call" | custom-call | flops 8000000000 | bytes 8388608 | tf_op jit(solution)/shard_map/within_segment/pallas_call | solution.py:425
  52.6 2.0 %copy-done.8 = f32[512,2048]{1,0:T(8,128)} copy-done((f32[512,2048]{1,0:T(8,128)}, f32[512,2048]{1,0:T(8,128)S(1)}, u32[]{:S(2)}) %copy-start.8) | copy-done | bytes 4194328
  54.6 2.6 %all-to-all-done.1.state_ref = bf16[16,256,128]{2,1,0:T(8,128)(2,1)} async-done(((bf16[16,256,128]{2,1,0:T(8,128)(2,1)}), bf16[16,256,128]{2,1,0:T(8,128)(2,1)}, u32[]{:S(2)}, u32[]{:S(2)}) %all-to-all-start.1) | async-done | bytes 1048608 | tf_op jit(solution)/shard_map/all_to_all | solution.py:399
  57.1 1.6 %copy-done.1 = bf16[512,2048]{1,0:T(8,128)(2,1)S(1)} copy-done((bf16[512,2048]{1,0:T(8,128)(2,1)S(1)}, bf16[512,2048]{1,0:T(8,128)(2,1)}, u32[]{:S(2)}) %copy-start.1) | copy-done | bytes 2097176
  58.7 2.2 %copy-done.9 = f32[512,2048]{1,0:T(8,128)S(1)} copy-done((f32[512,2048]{1,0:T(8,128)S(1)}, f32[512,2048]{1,0:T(8,128)}, u32[]{:S(2)}) %copy-start.9) | copy-done | bytes 4194328
  60.9 0.9 copy-done.11
  61.9 6.4 %carry_and_gate.1 = (f32[512,2048]{1,0:T(8,128)S(1)}, f32[8,2,512]{2,1,0:T(2,128)S(1)}) custom-call(f32[512,2048]{1,0:T(8,128)S(1)} %copy-done.9, bf16[16,256,128]{2,1,0:T(8,128)(2,1)} %all-to-all-done.1.state_ref, bf16[512,256]{1,0:T(8,128)(2,1)S(1)} %copy-done.11, bf16[512,256]{1,0:T(8,128)(2,1)S(1)} %get-tuple-element.21.fac_ref, ...), custom_call_target="tpu_custom_call" | custom-call | flops 2000000000 | bytes 8388608 | tf_op jit(solution)/shard_map/carry_and_gate/pallas_call | solution.py:444
  68.2 9.7 %all_to_all.26.sums_ref = f32[8,2,512]{2,1,0:T(2,128)S(1)} all-to-all(f32[8,2,512]{2,1,0:T(2,128)S(1)} %get-tuple-element.26), channel_id=1, replica_groups=mesh['ctx'=16,'tp'=8] {'tp'}, dimensions={0} | all-to-all | bytes 65536 | tf_op jit(solution)/shard_map/all_to_all | solution.py:399
  78.0 5.5 %local_grads.1 = (bf16[512,2048]{1,0:T(8,128)(2,1)S(1)}, bf16[16,256,128]{2,1,0:T(8,128)(2,1)S(1)}) custom-call(f32[512,2048]{1,0:T(8,128)S(1)} %get-tuple-element.25.mixed_ref, f32[8,2,512]{2,1,0:T(2,128)S(1)} %all_to_all.26.sums_ref, bf16[512,256]{1,0:T(8,128)(2,1)S(1)} %copy-done.11, bf16[512,256]{1,0:T(8,128)(2,1)S(1)} %get-tuple-element.21.fac_ref, ...), custom_call_target="tpu_custom_call" | custom-call | flops 2000000000 | bytes 8388608 | tf_op jit(solution)/shard_map/local_grads/pallas_call | solution.py:454
  83.5 1.0 copy-done.13
  84.5 1.3 copy-done.24
  85.8 4.6 %all-to-all-start.3 = ((bf16[16,256,128]{2,1,0:T(8,128)(2,1)}), bf16[16,256,128]{2,1,0:T(8,128)(2,1)}, u32[]{:S(2)}, u32[]{:S(2)}) async-start(bf16[16,256,128]{2,1,0:T(8,128)(2,1)} %copy-done.13), calls=%async_computation.3 | async-start | bytes 2097152 | tf_op jit(solution)/shard_map/all_to_all | solution.py:399
  90.4 1.6 %copy-done.3 = bf16[512,2048]{1,0:T(8,128)(2,1)S(1)} copy-done((bf16[512,2048]{1,0:T(8,128)(2,1)S(1)}, bf16[512,2048]{1,0:T(8,128)(2,1)}, u32[]{:S(2)}) %copy-start.3) | copy-done | bytes 2097176
  92.0 2.2 %copy-done.5 = f32[512,2048]{1,0:T(8,128)S(1)} copy-done((f32[512,2048]{1,0:T(8,128)S(1)}, f32[512,2048]{1,0:T(8,128)}, u32[]{:S(2)}) %copy-start.5) | copy-done | bytes 4194328
  94.2 5.5 %normed_and_gate.1 = (bf16[512,2048]{1,0:T(8,128)(2,1)}, bf16[512,2048]{1,0:T(8,128)(2,1)}) custom-call(f32[512,2048]{1,0:T(8,128)S(1)} %copy-done.5, f32[8,2,512]{2,1,0:T(2,128)S(1)} %all_to_all.26.sums_ref, bf16[512,2048]{1,0:T(8,128)(2,1)S(1)} %copy-done, f32[1,2048]{1,0:T(1,128)S(1)} %bitcast.4, bf16[512,2048]{1,0:T(8,128)(2,1)S(1)} %copy-done.3), custom_call_target="tpu_custom_call" | custom-call | flops 2000000000 | bytes 8388608 | tf_op jit(solution)/shard_map/normed_and_gate/pallas_call | solution.py:464
  99.7 8.4 %all-to-all-done.3.in_ref = bf16[16,256,128]{2,1,0:T(8,128)(2,1)} async-done(((bf16[16,256,128]{2,1,0:T(8,128)(2,1)}), bf16[16,256,128]{2,1,0:T(8,128)(2,1)}, u32[]{:S(2)}, u32[]{:S(2)}) %all-to-all-start.3) | async-done | bytes 1048608 | tf_op jit(solution)/shard_map/all_to_all | solution.py:399
  108.1 2.4 %backward_scan.1 = bf16[16,256,128]{2,1,0:T(8,128)(2,1)} custom-call(bf16[16,256,128]{2,1,0:T(8,128)(2,1)} %all-to-all-done.3.in_ref, bf16[16,272,128]{2,1,0:T(8,128)(2,1)S(1)} %all_to_all.25.in_ref.decay_ref), custom_call_target="tpu_custom_call" | custom-call | flops 16777216 | bytes 2097152 | tf_op jit(solution)/shard_map/backward_scan/pallas_call | solution.py:489
  110.5 3.7 %all-to-all-start.4 = ((bf16[16,256,128]{2,1,0:T(8,128)(2,1)}), bf16[16,256,128]{2,1,0:T(8,128)(2,1)S(1)}, u32[]{:S(2)}, u32[]{:S(2)}) async-start(bf16[16,256,128]{2,1,0:T(8,128)(2,1)} %backward_scan.1), calls=%async_computation.4 | async-start | bytes 2097152 | tf_op jit(solution)/shard_map/all_to_all | solution.py:399
  114.2 0.9 copy-done.12
  115.1 0.9 copy-done.18
  116.1 1.6 %copy-done.23 = bf16[512,2048]{1,0:T(8,128)(2,1)S(1)} copy-done((bf16[512,2048]{1,0:T(8,128)(2,1)S(1)}, bf16[512,2048]{1,0:T(8,128)(2,1)}, u32[]{:S(2)}) %copy-start.23) | copy-done | bytes 2097176
  117.6 1.6 %copy-done.25 = bf16[512,2048]{1,0:T(8,128)(2,1)S(1)} copy-done((bf16[512,2048]{1,0:T(8,128)(2,1)S(1)}, bf16[512,2048]{1,0:T(8,128)(2,1)}, u32[]{:S(2)}) %copy-start.25) | copy-done | bytes 2097176
  119.2 0.9 copy-done.29
  120.2 0.9 copy-done.32
  121.1 12.7 %within_segment_back.1 = (f32[512,2048]{1,0:T(8,128)S(1)}, bf16[512,2048]{1,0:T(8,128)(2,1)S(1)}, f32[512,256]{1,0:T(8,128)S(1)}, bf16[512,256]{1,0:T(8,128)(2,1)}) custom-call(bf16[512,2048]{1,0:T(8,128)(2,1)S(1)} %copy-done.23, bf16[512,2048]{1,0:T(8,128)(2,1)S(1)} %copy-done.25, bf16[16,256,128]{2,1,0:T(8,128)(2,1)} %all-to-all-done.1.state_ref, ...), custom_call_target="tpu_custom_call" | custom-call | flops 12000000000 | bytes 8388608 | tf_op jit(solution)/shard_map/within_segment_back/pallas_call | solution.py:473
  133.8 2.0 %copy-done.6 = f32[512,2048]{1,0:T(8,128)} copy-done((f32[512,2048]{1,0:T(8,128)}, f32[512,2048]{1,0:T(8,128)S(1)}, u32[]{:S(2)}) %copy-start.6) | copy-done | bytes 4194328
  135.8 0.8 copy-done.14
  136.6 2.2 %copy-done.7 = f32[512,2048]{1,0:T(8,128)S(1)} copy-done((f32[512,2048]{1,0:T(8,128)S(1)}, f32[512,2048]{1,0:T(8,128)}, u32[]{:S(2)}) %copy-start.7) | copy-done | bytes 4194328
  138.8 1.0 copy-done.15
  139.8 0.9 copy-done.19
  140.8 5.3 %final_grads.1 = (bf16[512,2048]{1,0:T(8,128)(2,1)}, bf16[512,256]{1,0:T(8,128)(2,1)}) custom-call(f32[512,2048]{1,0:T(8,128)S(1)} %copy-done.7, bf16[512,2048]{1,0:T(8,128)(2,1)S(1)} %get-tuple-element.30.scaled_ref, bf16[16,256,128]{2,1,0:T(8,128)(2,1)S(1)} %all-to-all-done.4.grad_ref, bf16[512,256]{1,0:T(8,128)(2,1)S(1)} %copy-done.19, ...), custom_call_target="tpu_custom_call" | custom-call | flops 2000000000 | bytes 8388608 | tf_op jit(solution)/shard_map/final_grads/pallas_call | solution.py:498
  (40 shorter events, 0.1 us)
Async XLA Ops:
  1.4 0.9 copy-start.16
  2.3 1.6 %copy-start.21 = (bf16[512,2048]{1,0:T(8,128)(2,1)S(1)}, bf16[512,2048]{1,0:T(8,128)(2,1)}, u32[]{:S(2)}) copy-start(bf16[512,2048]{1,0:T(8,128)(2,1)} %x_ref.5) | copy-start | bytes 6291460
  3.9 0.8 copy-start.26
  9.5 25.7 %copy-start.27 = (f32[512,128]{1,0:T(8,128)}, f32[512,128]{1,0:T(8,128)S(1)}, u32[]{:S(2)}) copy-start(f32[512,128]{1,0:T(8,128)S(1)} %get-tuple-element.22.col_ref) | copy-start | bytes 786436
  9.5 25.7 %copy-start.30 = (f32[8,8,512]{2,1,0:T(8,128)}, f32[8,8,512]{2,1,0:T(8,128)S(1)}, u32[]{:S(2)}) copy-start(f32[8,8,512]{2,1,0:T(8,128)S(1)} %get-tuple-element.23.row_ref) | copy-start | bytes 393220
  35.2 5.6 %copy-start.33 = (f32[32]{0:T(128)S(1)}, f32[32]{0:T(128)}, u32[]{:S(2)}) copy-start(f32[32]{0:T(128)} %param.15) | copy-start | bytes 388
  36.4 20.8 %all-to-all-start.1 = ((bf16[16,256,128]{2,1,0:T(8,128)(2,1)}), bf16[16,256,128]{2,1,0:T(8,128)(2,1)}, u32[]{:S(2)}, u32[]{:S(2)}) async-start(bf16[16,256,128]{2,1,0:T(8,128)(2,1)} %forward_scan.1), calls=%async_computation.1 | async-start | bytes 2097152 | tf_op jit(solution)/shard_map/all_to_all | solution.py:399
  40.9 1.0 copy-start.10
  41.8 0.9 copy-start.17
  42.8 1.6 %copy-start.22 = (bf16[512,2048]{1,0:T(8,128)(2,1)S(1)}, bf16[512,2048]{1,0:T(8,128)(2,1)}, u32[]{:S(2)}) copy-start(bf16[512,2048]{1,0:T(8,128)(2,1)} %x_ref.5) | copy-start | bytes 6291460
  44.4 0.9 copy-start.28
  45.3 0.9 copy-start.31
  46.2 10.9 %copy-start = (bf16[512,2048]{1,0:T(8,128)(2,1)S(1)}, bf16[512,2048]{1,0:T(8,128)(2,1)}, u32[]{:S(2)}) copy-start(bf16[512,2048]{1,0:T(8,128)(2,1)} %gate_ref.5) | copy-start | bytes 6291460
  46.2 10.9 %copy-start.20 = (f32[2048]{0:T(1024)S(1)}, f32[2048]{0:T(1024)}, u32[]{:S(2)}) copy-start(f32[2048]{0:T(1024)} %param.16) | copy-start | bytes 24580
  52.6 2.0 %copy-start.8 = (f32[512,2048]{1,0:T(8,128)}, f32[512,2048]{1,0:T(8,128)S(1)}, u32[]{:S(2)}) copy-start(f32[512,2048]{1,0:T(8,128)S(1)} %within_segment.1.local_ref) | copy-start | bytes 12582916
  57.1 1.6 %copy-start.1 = (bf16[512,2048]{1,0:T(8,128)(2,1)S(1)}, bf16[512,2048]{1,0:T(8,128)(2,1)}, u32[]{:S(2)}) copy-start(bf16[512,2048]{1,0:T(8,128)(2,1)} %grad_ref.5) | copy-start | bytes 6291460
  58.7 2.2 %copy-start.9 = (f32[512,2048]{1,0:T(8,128)S(1)}, f32[512,2048]{1,0:T(8,128)}, u32[]{:S(2)}) copy-start(f32[512,2048]{1,0:T(8,128)} %copy-done.8) | copy-start | bytes 12582916
  60.9 0.9 copy-start.11
  61.9 16.1 %copy-start.2 = (bf16[512,2048]{1,0:T(8,128)(2,1)S(1)}, bf16[512,2048]{1,0:T(8,128)(2,1)}, u32[]{:S(2)}) copy-start(bf16[512,2048]{1,0:T(8,128)(2,1)} %grad_ref.5) | copy-start | bytes 6291460
  68.2 15.3 %copy-start.4 = (f32[512,2048]{1,0:T(8,128)}, f32[512,2048]{1,0:T(8,128)S(1)}, u32[]{:S(2)}) copy-start(f32[512,2048]{1,0:T(8,128)S(1)} %get-tuple-element.25.mixed_ref) | copy-start | bytes 12582916
  83.5 1.0 copy-start.13
  84.5 1.3 copy-start.24
  85.8 22.2 %all-to-all-start.3 = ((bf16[16,256,128]{2,1,0:T(8,128)(2,1)}), bf16[16,256,128]{2,1,0:T(8,128)(2,1)}, u32[]{:S(2)}, u32[]{:S(2)}) async-start(bf16[16,256,128]{2,1,0:T(8,128)(2,1)} %copy-done.13), calls=%async_computation.3 | async-start | bytes 2097152 | tf_op jit(solution)/shard_map/all_to_all | solution.py:399
  90.4 1.6 %copy-start.3 = (bf16[512,2048]{1,0:T(8,128)(2,1)S(1)}, bf16[512,2048]{1,0:T(8,128)(2,1)}, u32[]{:S(2)}) copy-start(bf16[512,2048]{1,0:T(8,128)(2,1)} %grad_ref.5) | copy-start | bytes 6291460
  92.0 2.2 %copy-start.5 = (f32[512,2048]{1,0:T(8,128)S(1)}, f32[512,2048]{1,0:T(8,128)}, u32[]{:S(2)}) copy-start(f32[512,2048]{1,0:T(8,128)} %copy-done.4) | copy-start | bytes 12582916
  110.5 26.1 %all-to-all-start.4 = ((bf16[16,256,128]{2,1,0:T(8,128)(2,1)}), bf16[16,256,128]{2,1,0:T(8,128)(2,1)S(1)}, u32[]{:S(2)}, u32[]{:S(2)}) async-start(bf16[16,256,128]{2,1,0:T(8,128)(2,1)} %backward_scan.1), calls=%async_computation.4 | async-start | bytes 2097152 | tf_op jit(solution)/shard_map/all_to_all | solution.py:399
  114.2 1.0 copy-start.12
  115.1 0.9 copy-start.18
  116.1 1.6 %copy-start.23 = (bf16[512,2048]{1,0:T(8,128)(2,1)S(1)}, bf16[512,2048]{1,0:T(8,128)(2,1)}, u32[]{:S(2)}) copy-start(bf16[512,2048]{1,0:T(8,128)(2,1)} %x_ref.5) | copy-start | bytes 6291460
  117.6 1.6 %copy-start.25 = (bf16[512,2048]{1,0:T(8,128)(2,1)S(1)}, bf16[512,2048]{1,0:T(8,128)(2,1)}, u32[]{:S(2)}) copy-start(bf16[512,2048]{1,0:T(8,128)(2,1)} %copy-done.24) | copy-start | bytes 6291460
  119.2 0.9 copy-start.29
  120.2 0.9 copy-start.32
  133.8 2.0 %copy-start.6 = (f32[512,2048]{1,0:T(8,128)}, f32[512,2048]{1,0:T(8,128)S(1)}, u32[]{:S(2)}) copy-start(f32[512,2048]{1,0:T(8,128)S(1)} %get-tuple-element.29.dx_ref) | copy-start | bytes 12582916
  135.8 0.8 copy-start.14
  136.6 2.2 %copy-start.7 = (f32[512,2048]{1,0:T(8,128)S(1)}, f32[512,2048]{1,0:T(8,128)}, u32[]{:S(2)}) copy-start(f32[512,2048]{1,0:T(8,128)} %copy-done.6) | copy-start | bytes 12582916
  138.8 1.0 copy-start.15
  139.8 0.9 copy-start.19

commit v2 on v1

v2 whole, which is shorter than its diff:
```python
import jax
import jax.numpy as jnp
from jax import lax
from jax.experimental import pallas as pl
from jax.experimental.pallas import tpu as pltpu
from jax.sharding import PartitionSpec as P

H = 256
P_SIZE = 64
N = 256
EPS = 1e-05
LOG2E = 1.4426950408889634

SEGS = 16
PARTS = 8
TOK = 512
HEADS = 32
COLS = HEADS * P_SIZE
SLICE = 128
TAIL = 16
WIDE = 256
LONG = 1024
STEPS = COLS // WIDE
CHUNKS = COLS // LONG
HPS = WIDE // P_SIZE
VMEM_MIB = 36
SUB = 128
BLKS = TOK // SUB
HALF = TOK // 2

F32 = jnp.float32
BF16 = jnp.bfloat16
END, START, MIDDLE, QUARTER = range(4)


def nn(a, b):
    return jnp.dot(a, b, preferred_element_type=F32)


def nt(a, b):
    return lax.dot_general(a, b, (((1,), (1,)), ((), ())), preferred_element_type=F32)


def transposed(a):
    return a.astype(F32).T.astype(a.dtype)


def split(a):
    high = a.astype(BF16)
    return high, (a - high.astype(F32)).astype(BF16)


def expand(factors, which, step, width):
    row = lax.broadcasted_iota(jnp.int32, (2 * SLICE, width), 0)
    head = (lax.broadcasted_iota(jnp.int32, (2 * SLICE, width), 1) >> 6) + (width // P_SIZE) * step
    pick = jnp.where((row & 127) == head + HEADS * which, 1.0, 0.0).astype(BF16)
    return nn(factors, pick)


def two_heads(a):
    lane = lax.broadcasted_iota(jnp.int32, a.shape, 1)
    zero = jnp.zeros_like(a)
    return jnp.concatenate([jnp.where(lane < P_SIZE, a, zero), jnp.where(lane < P_SIZE, zero, a)], 0)


def blk(i):
    return slice(i * SUB, (i + 1) * SUB)


def columns_of(array, chunk):
    return array.at[:, pl.ds(pl.multiple_of(chunk * LONG, LONG), LONG)]


def slices_of(array, chunk):
    return array.at[pl.ds(chunk * (LONG // SLICE), LONG // SLICE)]


def ends_kernel(
    step_in, rate_in, x_in, keys_in, out, fac_out, col_out, row_out,
    step_ref, rate_ref, x_ref, keys_ref, ends_ref, fac_ref, col_ref, row_ref, keys_t, small, come, go,
):
    def fetch(chunk):
        return pltpu.make_async_copy(columns_of(x_in, chunk), x_ref.at[chunk], come.at[chunk])

    def send(chunk):
        return pltpu.make_async_copy(slices_of(ends_ref, chunk), slices_of(out, chunk), go.at[chunk])

    pairs = [(step_in, step_ref), (rate_in, rate_ref), (keys_in, keys_ref)]
    pairs += [(fac_ref, fac_out), (col_ref, col_out), (row_ref, row_out)]
    copies = [pltpu.make_async_copy(a, b, small.at[i]) for i, (a, b) in enumerate(pairs)]
    for copy in copies[:3]:
        copy.start()
    for chunk in range(CHUNKS):
        fetch(chunk).start()
    copies[0].wait()
    copies[1].wait()

    steps = step_ref[...]
    diagonal = lax.broadcasted_iota(jnp.int32, (HEADS, HEADS), 0) == lax.broadcasted_iota(jnp.int32, (HEADS, HEADS), 1)
    rate = jnp.sum(jnp.where(diagonal, rate_ref[...], 0.0), axis=1, keepdims=True)
    logs = steps * (rate * -LOG2E)
    high = logs.astype(BF16)
    rest = logs - high.astype(F32)
    mid, low = split(rest)
    source = lax.broadcasted_iota(jnp.int32, (TOK, TOK), 0)
    target = lax.broadcasted_iota(jnp.int32, (TOK, TOK), 1)
    upper = jnp.where(source <= target, 1.0, 0.0).astype(BF16)
    sums = nn(jnp.concatenate([high.astype(F32), mid.astype(F32), low.astype(F32)], 0).astype(BF16), upper)
    cum = sums[:HEADS] + sums[HEADS : 2 * HEADS] + sums[2 * HEADS :]
    shifted = cum - jnp.log(steps) * LOG2E
    token = lax.broadcasted_iota(jnp.int32, (HEADS, TOK), 1)
    one = jnp.ones_like(steps)
    end = jnp.exp2(cum[:, TOK - 1 :] - cum) * steps
    start = jnp.exp2(cum)
    middle = jnp.exp2(-jnp.abs(cum - cum[:, HALF - 1 : HALF])) * jnp.where(token < HALF, steps, one)
    near = jnp.where(token < HALF, cum[:, SUB - 1 : SUB], cum[:, 3 * SUB - 1 : 3 * SUB])
    quarter = jnp.exp2(-jnp.abs(cum - near)) * jnp.where((token & SUB) == 0, steps, one)
    high, low = split(jnp.concatenate([end, start, middle, quarter], 0).T)
    fac_ref[:, :128] = high
    fac_ref[:, 128:] = low
    copies[3].start()
    copies[2].wait()
    keys_t[...] = transposed(keys_ref[...])

    @pl.loop(0, CHUNKS)
    def _(chunk):
        fetch(chunk).wait()
        factors = fac_ref[...]
        scaled = (x_ref[chunk].astype(F32) * expand(factors, END, chunk, LONG)).astype(BF16)
        ends = nn(keys_t[...], scaled).astype(BF16)
        decay = expand(factors[TOK - 16 :], START, chunk, LONG)
        decay = jnp.broadcast_to(decay[15:16], (TAIL, LONG)).astype(BF16)
        for part in range(LONG // SLICE):
            lanes = slice(part * SLICE, (part + 1) * SLICE)
            ends_ref[chunk * (LONG // SLICE) + part, :N] = ends[:, lanes]
            ends_ref[chunk * (LONG // SLICE) + part, N:] = decay[:, lanes]
        send(chunk).start()

    col_ref[...] = jnp.concatenate([cum, shifted, cum, shifted], 0).T
    for part in range(STEPS):
        heads = slice(part * HPS, (part + 1) * HPS)
        row_ref[part] = jnp.concatenate([cum[heads], shifted[heads]], 0)
    copies[4].start()
    copies[5].start()
    for copy in copies[3:]:
        copy.wait()
    for chunk in range(CHUNKS):
        send(chunk).wait()


def weights(col, row, scores):
    return (jnp.exp2(jnp.minimum(col - row, 0.0)) * scores).astype(BF16)


def local_kernel(x_ref, gate_ref, keys_ref, queries_ref, fac_ref, col_ref, row_ref, skip_ref, out_ref, silu_ref, scaled_ref, near, off1, off2):
    step = pl.program_id(0)

    @pl.when(step == 0)
    def _():
        target = lax.broadcasted_iota(jnp.int32, (SUB, SUB), 0)
        source = lax.broadcasted_iota(jnp.int32, (SUB, SUB), 1)
        for i in range(BLKS):
            scores = nt(queries_ref[blk(i)], keys_ref[blk(i)])
            near[i] = jnp.where(source <= target, scores, 0.0)
        for i in range(BLKS // 2):
            off1[i] = nt(queries_ref[blk(2 * i + 1)], keys_ref[blk(2 * i)]).astype(BF16)
        off2[...] = nt(queries_ref[HALF:], keys_ref[:HALF]).astype(BF16)

    factors = fac_ref[...]
    x = x_ref[...]
    wide = x.astype(F32)
    middle = expand(factors, MIDDLE, step, WIDE)
    quarter = expand(factors, QUARTER, step, WIDE)
    cols = pltpu.roll(col_ref[...], lax.rem(128 - HPS * step, 128), 1)
    scaled_ref[...] = (wide * expand(factors, END, step, WIDE)).astype(BF16)
    gate = gate_ref[...].astype(F32)
    silu_ref[...] = (gate * jax.nn.sigmoid(gate)).astype(BF16)
    far = nn(off2[...], (wide[:HALF] * middle[:HALF]).astype(BF16)) * middle[HALF:]
    skip = skip_ref[...] * wide
    for i in range(BLKS):
        total = skip[blk(i)]
        if i % 2:
            before = (wide[blk(i - 1)] * quarter[blk(i - 1)]).astype(BF16)
            total += nn(off1[i // 2], before) * quarter[blk(i)]
        if i >= 2:
            total += far[blk(i - 2)]
        scores = near[i]
        for pair in range(WIDE // SLICE):
            lanes = slice(pair * SLICE, (pair + 1) * SLICE)
            both = []
            for j in (2 * pair, 2 * pair + 1):
                row = row_ref[0, HPS + j : HPS + j + 1, blk(i)]
                both.append(weights(cols[blk(i), j : j + 1], row, scores))
            within = nn(jnp.concatenate(both, 1), two_heads(x[blk(i), lanes]))
            out_ref[blk(i), lanes] = (total[:, lanes] + within).astype(BF16)


def forward_scan_kernel(in_ref, out_ref):
    running = jnp.zeros((N, SLICE), F32)
    for k in range(SEGS):
        out_ref[k] = running.astype(BF16)
        decay = in_ref[k, N : N + TAIL][:1].astype(F32)
        running = running * decay + in_ref[k, :N].astype(F32)


def backward_scan_kernel(in_ref, decay_ref, out_ref):
    running = jnp.zeros((N, SLICE), F32)
    for k in reversed(range(SEGS)):
        out_ref[k] = running.astype(BF16)
        running = running * decay_ref[k][:1].astype(F32) + in_ref[k].astype(F32)


def state_of(ref):
    return jnp.concatenate([ref[part] for part in range(ref.shape[0])], 1)


def fold(a):
    total = a[:, :128]
    for lane in range(128, a.shape[1], 128):
        total += a[:, lane : lane + 128]
    return total


def gate_kernel(local_ref, state_ref, queries_ref, fac_ref, silu_ref, gain_ref, grad_ref, mixed_ref, sums_ref, square, product):
    step = pl.program_id(0)

    @pl.when(step == 0)
    def _():
        square[...] = jnp.zeros_like(square)
        product[...] = jnp.zeros_like(product)

    carried = nn(queries_ref[...], state_of(state_ref)) * expand(fac_ref[...], START, step, LONG)
    mixed = local_ref[...].astype(F32) + carried
    mixed_ref[...] = mixed.astype(BF16)
    gated = mixed * silu_ref[...].astype(F32)
    squares = gated * gated
    products = gated * (gain_ref[...] * grad_ref[...].astype(F32))
    square[...] += fold(squares)
    product[...] += fold(products)

    @pl.when(step == COLS // LONG - 1)
    def _():
        both = jnp.concatenate(
            [jnp.sum(square[...].T, axis=0, keepdims=True), jnp.sum(product[...].T, axis=0, keepdims=True)], 0
        )
        for part in range(PARTS):
            sums_ref[part] = both


def norm_terms(sums_ref, inverse, slope):
    total = sums_ref[0]
    for part in range(1, PARTS):
        total += sums_ref[part]
    inv_rms = lax.rsqrt(total[:1] / (H * P_SIZE) + EPS)
    ratio = inv_rms * inv_rms * inv_rms * total[1:] / (H * P_SIZE)
    inverse[...] = jnp.broadcast_to(inv_rms, (128, TOK)).T
    slope[...] = jnp.broadcast_to(ratio, (128, TOK)).T


def wide_of(ref):
    return jnp.concatenate([ref[...]] * (LONG // 128), 1)


def grad_kernel(mixed_ref, sums_ref, queries_ref, fac_ref, silu_ref, gain_ref, grad_ref, dy_ref, out_ref, inverse, slope, queries_t):
    step = pl.program_id(0)

    @pl.when(step == 0)
    def _():
        norm_terms(sums_ref, inverse, slope)
        queries_t[...] = transposed(queries_ref[...])

    silu = silu_ref[...].astype(F32)
    gated = mixed_ref[...].astype(F32) * silu
    grad_gated = wide_of(inverse) * (gain_ref[...] * grad_ref[...].astype(F32)) - gated * wide_of(slope)
    dy = grad_gated * silu
    dy_ref[...] = dy.astype(BF16)
    weighted = (dy * expand(fac_ref[...], START, step, LONG)).astype(BF16)
    local = nn(queries_t[...], weighted).astype(BF16)
    for part in range(LONG // SLICE):
        out_ref[part] = local[:, part * SLICE : (part + 1) * SLICE]


def norm_kernel(mixed_ref, sums_ref, gate_ref, gain_ref, grad_ref, normed_ref, out_ref, inverse, slope):
    step = pl.program_id(0)

    @pl.when(step == 0)
    def _():
        norm_terms(sums_ref, inverse, slope)

    gate = gate_ref[...].astype(F32)
    sig = jax.nn.sigmoid(gate)
    mixed = mixed_ref[...].astype(F32)
    gated = mixed * (gate * sig)
    gain = wide_of(inverse) * gain_ref[...]
    normed_ref[...] = (gated * gain).astype(BF16)
    grad_gated = gain * grad_ref[...].astype(F32) - gated * wide_of(slope)
    out_ref[...] = (grad_gated * mixed * (sig * (1.0 + gate * (1.0 - sig)))).astype(BF16)


def back_kernel(
    x_ref, dy_ref, state_ref, keys_ref, queries_ref, fac_ref, col_ref, row_ref, skip_ref,
    dx_ref, dkeys_ref, dqueries_ref,
    near, off1, off2, dnear, doff1, doff2, dq,
):
    step = pl.program_id(0)

    @pl.when(step == 0)
    def _():
        source = lax.broadcasted_iota(jnp.int32, (SUB, SUB), 0)
        target = lax.broadcasted_iota(jnp.int32, (SUB, SUB), 1)
        for i in range(BLKS):
            scores = nt(keys_ref[blk(i)], queries_ref[blk(i)])
            near[i] = jnp.where(source <= target, scores, 0.0)
        for i in range(BLKS // 2):
            off1[i] = nt(keys_ref[blk(2 * i)], queries_ref[blk(2 * i + 1)]).astype(BF16)
        off2[...] = nt(keys_ref[:HALF], queries_ref[HALF:]).astype(BF16)
        dnear[...] = jnp.zeros_like(dnear)
        doff1[...] = jnp.zeros_like(doff1)
        doff2[...] = jnp.zeros_like(doff2)
        dq[...] = jnp.zeros_like(dq)

    factors = fac_ref[...]
    x = x_ref[...]
    wide = x.astype(F32)
    dy = dy_ref[...]
    dwide = dy.astype(F32)
    weighted = (dwide * expand(factors, START, step, WIDE)).astype(BF16)
    dq[...] += nt(weighted, state_of(state_ref))
    middle = expand(factors, MIDDLE, step, WIDE)
    quarter = expand(factors, QUARTER, step, WIDE)
    cols = pltpu.roll(col_ref[...], lax.rem(128 - HPS * step, 128), 1)
    above = (wide[:HALF] * middle[:HALF]).astype(BF16)
    below = (dwide[HALF:] * middle[HALF:]).astype(BF16)
    far = nn(off2[...], below) * middle[:HALF]
    doff2[...] += nt(above, below)
    skip = skip_ref[...] * dwide
    for i in range(BLKS):
        total = skip[blk(i)]
        if i % 2 == 0:
            above = (wide[blk(i)] * quarter[blk(i)]).astype(BF16)
            below = (dwide[blk(i + 1)] * quarter[blk(i + 1)]).astype(BF16)
            total += nn(off1[i // 2], below) * quarter[blk(i)]
            doff1[i // 2] += nt(above, below)
        if i < 2:
            total += far[blk(i)]
        scores = near[i]
        dscores = dnear[i]
        for pair in range(WIDE // SLICE):
            lanes = slice(pair * SLICE, (pair + 1) * SLICE)
            dy_two = two_heads(dy[blk(i), lanes])
            dweights = nt(x[blk(i), lanes], dy_two)
            both = []
            for place, j in enumerate((2 * pair, 2 * pair + 1)):
                row = row_ref[0, j : j + 1, blk(i)]
                decay = jnp.exp2(jnp.minimum(row - cols[blk(i), HEADS + j : HEADS + j + 1], 0.0))
                both.append((decay * scores).astype(BF16))
                dscores += decay * dweights[:, place * SUB : (place + 1) * SUB]
            dx_ref[blk(i), lanes] = (total[:, lanes] + nn(jnp.concatenate(both, 1), dy_two)).astype(BF16)
        dnear[i] = dscores

    @pl.when(step == STEPS - 1)
    def _():
        source = lax.broadcasted_iota(jnp.int32, (SUB, SUB), 0)
        target = lax.broadcasted_iota(jnp.int32, (SUB, SUB), 1)
        last = doff2[...]
        dkeys_ref[...] = jnp.zeros_like(dkeys_ref)
        dkeys_ref[:HALF] += nn(last.astype(BF16), queries_ref[HALF:])
        dq[HALF:] += nn(last.T.astype(BF16), keys_ref[:HALF])
        for i in range(BLKS // 2):
            part = doff1[i]
            dkeys_ref[blk(2 * i)] += nn(part.astype(BF16), queries_ref[blk(2 * i + 1)])
            dq[blk(2 * i + 1)] += nn(part.T.astype(BF16), keys_ref[blk(2 * i)])
        for i in range(BLKS):
            part = jnp.where(source <= target, dnear[i], 0.0)
            dkeys_ref[blk(i)] += nn(part.astype(BF16), queries_ref[blk(i)])
            dq[blk(i)] += nn(part.T.astype(BF16), keys_ref[blk(i)])
        dqueries_ref[...] = dq[...].astype(BF16)


def final_kernel(
    dx_in, scaled_in, grad_in, keys_in, fac_in, dkeys_in, out, out_keys,
    dx_ref, scaled_ref, grad_ref, keys_ref, fac_ref, dkeys_ref, out_ref, out_keys_ref, total, small, come, go,
):
    def fetch(chunk):
        return (
            pltpu.make_async_copy(slices_of(grad_in, chunk), slices_of(grad_ref, chunk), come.at[0, chunk]),
            pltpu.make_async_copy(columns_of(scaled_in, chunk), scaled_ref.at[chunk], come.at[1, chunk]),
            pltpu.make_async_copy(columns_of(dx_in, chunk), dx_ref.at[chunk], come.at[2, chunk]),
        )

    def send(chunk):
        return pltpu.make_async_copy(out_ref.at[chunk], columns_of(out, chunk), go.at[chunk])

    pairs = [(keys_in, keys_ref), (fac_in, fac_ref), (dkeys_in, dkeys_ref), (out_keys_ref, out_keys)]
    copies = [pltpu.make_async_copy(a, b, small.at[i]) for i, (a, b) in enumerate(pairs)]
    copies[0].start()
    copies[1].start()
    for chunk in range(CHUNKS):
        for copy in fetch(chunk):
            copy.start()
    copies[2].start()
    total[...] = jnp.zeros_like(total)
    copies[0].wait()
    copies[1].wait()

    @pl.loop(0, CHUNKS)
    def _(chunk):
        for copy in fetch(chunk):
            copy.wait()
        first = chunk * (LONG // SLICE)
        state_grad = jnp.concatenate([grad_ref[first + part] for part in range(LONG // SLICE)], 1)
        from_end = nn(keys_ref[...], state_grad) * expand(fac_ref[...], END, chunk, LONG)
        out_ref[chunk] = (dx_ref[chunk].astype(F32) + from_end).astype(BF16)
        send(chunk).start()
        total[...] += nt(scaled_ref[chunk], state_grad)

    copies[2].wait()
    out_keys_ref[...] = (total[...] + dkeys_ref[...]).astype(BF16)
    copies[3].start()
    copies[3].wait()
    for chunk in range(CHUNKS):
        send(chunk).wait()


def whole(shape):
    return pl.BlockSpec(shape, lambda i: (0,) * len(shape))


TOKENS_BY_STEP = pl.BlockSpec((TOK, WIDE), lambda i: (0, i))
ROW_BY_STEP = pl.BlockSpec((1, WIDE), lambda i: (0, i))
TOKENS_BY_LONG = pl.BlockSpec((TOK, LONG), lambda i: (0, i))
ROW_BY_LONG = pl.BlockSpec((1, LONG), lambda i: (0, i))
MAP = whole((TOK, N))
FACTORS = whole((TOK, 2 * SLICE))
COLUMNS = whole((TOK, 128))
ROWS = whole((STEPS, 2 * HPS, TOK))
ROWS_BY_STEP = pl.BlockSpec((1, 2 * HPS, TOK), lambda i: (i, 0, 0))
SUMS = whole((PARTS, 2, TOK))


def state_by(width, rows=N):
    return pl.BlockSpec((width // SLICE, rows, SLICE), lambda i: (i, 0, 0))


def shape(*dims, dtype=F32):
    return jax.ShapeDtypeStruct(dims, dtype)


def in_hbm(*dims, dtype=F32):
    return pltpu.HBM(dims, dtype)


def hbm(*arrays):
    return [pltpu.with_memory_space_constraint(a, pltpu.HBM) for a in arrays]


ANY = pl.BlockSpec(memory_space=pl.ANY)


def manual_call(kernel, name, operands, out_shape, scratch):
    return pl.pallas_call(
        kernel,
        name=name,
        in_specs=[ANY] * len(operands),
        out_specs=[ANY] * len(out_shape),
        out_shape=out_shape,
        scratch_shapes=scratch,
        compiler_params=pltpu.CompilerParams(vmem_limit_bytes=VMEM_MIB << 20),
        cost_estimate=pl.CostEstimate(flops=2**30, bytes_accessed=8 * 2**20, transcendentals=0),
    )(*operands)


def call(kernel, name, in_specs, out_specs, out_shape, scratch=(), gmacs=1.0, mib=8.0, steps=COLS // LONG):
    return pl.pallas_call(
        kernel,
        name=name,
        grid=(steps,),
        in_specs=in_specs,
        out_specs=out_specs,
        out_shape=out_shape,
        scratch_shapes=list(scratch),
        compiler_params=pltpu.CompilerParams(vmem_limit_bytes=VMEM_MIB << 20),
        cost_estimate=pl.CostEstimate(flops=int(2e9 * gmacs), bytes_accessed=int(mib * 2**20), transcendentals=0),
    )


def whole_call(kernel, name, in_specs, out_specs, out_shape):
    return pl.pallas_call(
        kernel,
        name=name,
        grid=(1,),
        in_specs=in_specs,
        out_specs=out_specs,
        out_shape=out_shape,
        compiler_params=pltpu.CompilerParams(vmem_limit_bytes=VMEM_MIB << 20),
        cost_estimate=pl.CostEstimate(flops=2**24, bytes_accessed=2**21, transcendentals=0),
    )


def exchange(a, axis):
    return lax.all_to_all(a, axis, 0, 0)


def body(inputs, gate_input, step_size, input_map, output_map, decay_rate, skip_weight, norm_gain, out_grad):
    rate = decay_rate.reshape(1, HEADS)
    gain = norm_gain.reshape(1, COLS)
    skip = jnp.repeat(skip_weight, P_SIZE).reshape(1, COLS)
    tokens = shape(TOK, COLS, dtype=BF16)
    score_scratch = [
        pltpu.VMEM((BLKS, SUB, SUB), F32),
        pltpu.VMEM((BLKS // 2, SUB, SUB), BF16),
        pltpu.VMEM((HALF, HALF), BF16),
    ]
    norm_scratch = [pltpu.VMEM((TOK, 128), F32)] * 2

    queries = output_map
    inputs, gate_input, step_size, input_map, output_map, rate, skip = hbm(
        inputs, gate_input, step_size, input_map, output_map, rate, skip
    )
    chunk_scratch = pltpu.VMEM((CHUNKS, TOK, LONG), BF16)
    dma = pltpu.SemaphoreType.DMA

    ends, factors, columns, rows = manual_call(
        ends_kernel,
        "segment_ends",
        (step_size, rate, inputs, input_map),
        [
            in_hbm(SEGS, N + TAIL, SLICE, dtype=BF16),
            in_hbm(TOK, 2 * SLICE, dtype=BF16),
            in_hbm(TOK, 128),
            in_hbm(STEPS, 2 * HPS, TOK),
        ],
        [
            pltpu.VMEM((HEADS, TOK), F32),
            pltpu.VMEM((1, HEADS), F32),
            chunk_scratch,
            pltpu.VMEM((TOK, N), BF16),
            pltpu.VMEM((SEGS, N + TAIL, SLICE), BF16),
            pltpu.VMEM((TOK, 2 * SLICE), BF16),
            pltpu.VMEM((TOK, 128), F32),
            pltpu.VMEM((STEPS, 2 * HPS, TOK), F32),
            pltpu.VMEM((N, TOK), BF16),
            dma((6,)),
            dma((CHUNKS,)),
            dma((CHUNKS,)),
        ],
    )
    all_ends = exchange(ends, "ctx")

    mixed_local, silu, scaled = call(
        local_kernel,
        "within_segment",
        [TOKENS_BY_STEP, TOKENS_BY_STEP, MAP, MAP, FACTORS, COLUMNS, ROWS_BY_STEP, ROW_BY_STEP],
        [TOKENS_BY_STEP] * 3,
        [in_hbm(TOK, COLS, dtype=BF16)] * 3,
        score_scratch,
        steps=STEPS,
        gmacs=4.0,
    )(inputs, gate_input, input_map, output_map, factors, columns, rows, skip)
    all_ends, mixed_local, silu, scaled = lax.optimization_barrier((all_ends, mixed_local, silu, scaled))

    starts = whole_call(
        forward_scan_kernel,
        "forward_scan",
        [whole((SEGS, N + TAIL, SLICE))],
        whole((SEGS, N, SLICE)),
        shape(SEGS, N, SLICE, dtype=BF16),
    )(all_ends)
    state_in = exchange(starts, "ctx")

    mixed, sums = call(
        gate_kernel,
        "carry_and_gate",
        [TOKENS_BY_LONG, state_by(LONG), MAP, FACTORS, TOKENS_BY_LONG, ROW_BY_LONG, TOKENS_BY_LONG],
        [TOKENS_BY_LONG, SUMS],
        [tokens, shape(PARTS, 2, TOK)],
        norm_scratch,
    )(mixed_local, state_in, queries, factors, silu, gain, *hbm(out_grad))
    sums = exchange(sums, "tp")

    dy, local_grads = call(
        grad_kernel,
        "local_grads",
        [TOKENS_BY_LONG, SUMS, MAP, FACTORS, TOKENS_BY_LONG, ROW_BY_LONG, TOKENS_BY_LONG],
        [TOKENS_BY_LONG, state_by(LONG)],
        [in_hbm(TOK, COLS, dtype=BF16), in_hbm(SEGS, N, SLICE, dtype=BF16)],
        norm_scratch + [pltpu.VMEM((N, TOK), BF16)],
    )(mixed, sums, queries, factors, silu, gain, out_grad)
    all_grads = exchange(local_grads, "ctx")

    normed, grad_gate = call(
        norm_kernel,
        "normed_and_gate",
        [TOKENS_BY_LONG, SUMS, TOKENS_BY_LONG, ROW_BY_LONG, TOKENS_BY_LONG],
        [TOKENS_BY_LONG, TOKENS_BY_LONG],
        [tokens, tokens],
        norm_scratch,
    )(*hbm(mixed, sums, gate_input, gain, out_grad))

    dx, dkeys, dqueries = call(
        back_kernel,
        "within_segment_back",
        [TOKENS_BY_STEP, TOKENS_BY_STEP, state_by(WIDE), MAP, MAP, FACTORS, COLUMNS, ROWS_BY_STEP, ROW_BY_STEP],
        [TOKENS_BY_STEP, MAP, MAP],
        [in_hbm(TOK, COLS, dtype=BF16), in_hbm(TOK, N), shape(TOK, N, dtype=BF16)],
        score_scratch
        + [
            pltpu.VMEM((BLKS, SUB, SUB), F32),
            pltpu.VMEM((BLKS // 2, SUB, SUB), F32),
            pltpu.VMEM((HALF, HALF), F32),
            pltpu.VMEM((TOK, N), F32),
        ],
        steps=STEPS,
        gmacs=6.0,
    )(inputs, dy, *hbm(state_in), input_map, output_map, factors, columns, rows, skip)

    grad_starts = whole_call(
        backward_scan_kernel,
        "backward_scan",
        [whole((SEGS, N, SLICE)), pl.BlockSpec((SEGS, TAIL, SLICE), lambda i: (0, N // TAIL, 0))],
        whole((SEGS, N, SLICE)),
        shape(SEGS, N, SLICE, dtype=BF16),
    )(all_grads, all_ends)
    state_grad = exchange(grad_starts, "ctx")

    grad_inputs, grad_keys = manual_call(
        final_kernel,
        "final_grads",
        (*hbm(dx, scaled), state_grad, *hbm(input_map, factors, dkeys)),
        [tokens, shape(TOK, N, dtype=BF16)],
        [
            chunk_scratch,
            chunk_scratch,
            pltpu.VMEM((SEGS, N, SLICE), BF16),
            pltpu.VMEM((TOK, N), BF16),
            pltpu.VMEM((TOK, 2 * SLICE), BF16),
            pltpu.VMEM((TOK, N), F32),
            chunk_scratch,
            pltpu.VMEM((TOK, N), BF16),
            pltpu.VMEM((TOK, N), F32),
            dma((4,)),
            dma((3, CHUNKS)),
            dma((CHUNKS,)),
        ],
    )
    return normed, grad_inputs, grad_gate, grad_keys, dqueries


def solution(mesh):
    both = P("ctx", "tp")
    return jax.shard_map(
        body,
        mesh=mesh,
        in_specs=(both, both, P("tp", "ctx"), both, both, P("tp"), P("tp"), P("tp"), both),
        out_specs=(both,) * 5,
        check_vma=False,
    )
```

time: 148 us -> 119 us (0.80); the launches traced: 146 us -> 119 us
  local copies, waits for them, and re-layouts: 36.3 us -> 2.39 us
  waiting for transfers between devices: 10.9 us -> 21.9 us
  blocking collectives: 35.4 us -> 30 us
  starting transfers between devices: 12.6 us -> 15.6 us
  Pallas kernels: 50.1 us -> 47.8 us
    unnamed x68 -> x26, local copies, waits for them, and re-layouts: 35.4 us -> 1.64 us
    all_to_all x3, waiting for transfers between devices: 10.9 us -> 21.9 us  [exchange(): return lax.all_to_all(a, axis, 0, 0)]
    all_to_all x2, blocking collectives: 35.4 us -> 30 us  [exchange(): return lax.all_to_all(a, axis, 0, 0)]
    all_to_all x3, starting transfers between devices: 12.6 us -> 15.6 us  [exchange(): return lax.all_to_all(a, axis, 0, 0)]
  transfers between devices with their start and end apart: 3 -> 3, of which waited for: 2 -> 3; matrix products, arithmetic and copies ran while one was open for 0% -> 1% of each run, Pallas kernels for 17% -> 24%
where the time goes in v2:
time: 119 us
  Pallas kernels  47.8 us (40%)
  blocking collectives  30 us (25%)
  waiting for transfers between devices  21.9 us (18%)
  starting transfers between devices  15.6 us (13%)
  local copies, waits for them, and re-layouts  2.39 us (2%)
    all_to_all x2, blocking collectives, exchange(): return lax.all_to_all(a, axis, 0, 0)  30 us
    all_to_all x3, waiting for transfers between devices, exchange(): return lax.all_to_all(a, axis, 0, 0)  21.9 us
    all_to_all x3, starting transfers between devices, exchange(): return lax.all_to_all(a, axis, 0, 0)  15.6 us
    pallas_call x1, Pallas kernels, body(): call(back_kernel, 'within_segment_back', [TOKENS_BY_STEP, TOKENS_BY_STEP,...  11.9 us
    pallas_call x1, Pallas kernels, body(): call(local_kernel, 'within_segment', [TOKENS_BY_STEP, TOKENS_BY_STEP, MAP...  10.5 us
    pallas_call x2, Pallas kernels, manual_call(): pl.pallas_call(kernel, name=name, in_specs=[ANY] * len(operands), out_spe...  8.88 us
    pallas_call x1, Pallas kernels, body(): call(norm_kernel, 'normed_and_gate', [TOKENS_BY_LONG, SUMS, TOKENS_BY_LON...  6.42 us
    pallas_call x1, Pallas kernels, body(): call(gate_kernel, 'carry_and_gate', [TOKENS_BY_LONG, state_by(LONG), MAP,...  4.73 us
  transfers between devices with their start and end apart: 3, of which 3 were waited for; matrix products, arithmetic and copies ran while one was open for 1% of the time, Pallas kernels for 24%

profile of v2, /device:TPU:0, one launch (start us, length us, event | category | flops | bytes accessed | tf_op | source)
XLA Modules:
  0.0 118.6 jit_solution(16788600336334596707)
XLA Ops:
  0.6 4.0 %segment_ends.1 = (bf16[16,272,128]{2,1,0:T(8,128)(2,1)}, bf16[512,256]{1,0:T(8,128)(2,1)}, f32[512,128]{1,0:T(8,128)}, f32[8,8,512]{2,1,0:T(8,128)}) custom-call(f32[32,512]{1,0:T(8,128)} %step_in.1, f32[1,32]{1,0:T(1,128)} %bitcast.5, bf16[512,2048]{1,0:T(8,128)(2,1)} %x_ref.3, bf16[512,256]{1,0:T(8,128)(2,1)} %keys_in.3), custom_call_target="tpu_custom_call" | custom-call | flops 1073741824 | bytes 8388608 | tf_op jit(solution)/shard_map/segment_ends/pallas_call | solution.py:461
  4.7 0.0 copy-start.12
  4.7 0.0 copy-start.4
  4.7 0.0 copy-start.10
  4.7 0.0 copy-start.11
  4.7 8.1 %all-to-all-start = ((bf16[16,272,128]{2,1,0:T(8,128)(2,1)}), bf16[16,272,128]{2,1,0:T(8,128)(2,1)S(1)}, u32[]{:S(2)}, u32[]{:S(2)}) async-start(bf16[16,272,128]{2,1,0:T(8,128)(2,1)} %get-tuple-element.27), calls=%async_computation | async-start | bytes 2228224 | tf_op jit(solution)/shard_map/all_to_all | solution.py:501
  12.8 0.0 copy-done.12
  12.8 0.1 broadcast_in_dim.3
  12.9 0.7 reshape_reshape.3.skip_ref
  13.6 0.0 copy-done.4
  13.6 0.0 copy-done.10
  13.6 0.0 copy-done.11
  13.6 0.0 copy-start.5
  13.6 10.5 %within_segment.1 = (bf16[512,2048]{1,0:T(8,128)(2,1)}, bf16[512,2048]{1,0:T(8,128)(2,1)}, bf16[512,2048]{1,0:T(8,128)(2,1)}) custom-call(bf16[512,2048]{1,0:T(8,128)(2,1)} %x_ref.3, bf16[512,2048]{1,0:T(8,128)(2,1)} %gate_ref.3, bf16[512,256]{1,0:T(8,128)(2,1)} %keys_in.3, bf16[512,256]{1,0:T(8,128)(2,1)} %queries_ref.7, bf16[512,256]{1,0:T(8,128)(2,1)S(1)} %copy-done.4, ...), custom_call_target="tpu_custom_call" | custom-call | flops 8000000000 | bytes 8388608 | tf_op jit(solution)/shard_map/within_segment/pallas_call | solution.py:550
  24.1 7.2 %all-to-all-done.in_ref.decay_ref = bf16[16,272,128]{2,1,0:T(8,128)(2,1)S(1)} async-done(((bf16[16,272,128]{2,1,0:T(8,128)(2,1)}), bf16[16,272,128]{2,1,0:T(8,128)(2,1)S(1)}, u32[]{:S(2)}, u32[]{:S(2)}) %all-to-all-start) | async-done | bytes 1114144 | tf_op jit(solution)/shard_map/all_to_all | solution.py:501
  31.2 0.0 copy-start.2
  31.2 0.0 copy-start.3
  31.2 0.0 copy-start.7
  31.2 0.2 forward_scan.1
  31.5 20.3 %all_to_all.25.state_ref = bf16[16,256,128]{2,1,0:T(8,128)(2,1)S(1)} all-to-all(bf16[16,256,128]{2,1,0:T(8,128)(2,1)S(1)} %forward_scan.1), channel_id=1, replica_groups=mesh['ctx'=16,'tp'=8] {'ctx'}, dimensions={0} | all-to-all | bytes 2097152 | tf_op jit(solution)/shard_map/all_to_all | solution.py:501
  51.7 0.0 copy-start
  51.7 0.0 copy-done.5
  51.8 0.0 copy-done.2
  51.8 0.0 copy-done.3
  51.8 0.0 copy-done.7
  51.8 0.0 copy-start.1
  51.8 4.7 %carry_and_gate.1 = (bf16[512,2048]{1,0:T(8,128)(2,1)S(1)}, f32[8,2,512]{2,1,0:T(2,128)S(1)}) custom-call(bf16[512,2048]{1,0:T(8,128)(2,1)S(1)} %copy-done.3, bf16[16,256,128]{2,1,0:T(8,128)(2,1)S(1)} %all_to_all.25.state_ref, bf16[512,256]{1,0:T(8,128)(2,1)S(1)} %copy-done.5, bf16[512,256]{1,0:T(8,128)(2,1)S(1)} %copy-done.4, ...), custom_call_target="tpu_custom_call" | custom-call | flops 2000000000 | bytes 8388608 | tf_op jit(solution)/shard_map/carry_and_gate/pallas_call | solution.py:571
  56.5 0.0 copy-done
  56.5 0.0 copy-start.8
  56.5 9.7 %all_to_all.26.sums_ref = f32[8,2,512]{2,1,0:T(2,128)S(1)} all-to-all(f32[8,2,512]{2,1,0:T(2,128)S(1)} %get-tuple-element.38), channel_id=1, replica_groups=mesh['ctx'=16,'tp'=8] {'tp'}, dimensions={0} | all-to-all | bytes 65536 | tf_op jit(solution)/shard_map/all_to_all | solution.py:501
  66.3 0.0 copy-start.6
  66.3 0.0 copy-done.1
  66.3 4.0 %local_grads.1 = (bf16[512,2048]{1,0:T(8,128)(2,1)}, bf16[16,256,128]{2,1,0:T(8,128)(2,1)}) custom-call(bf16[512,2048]{1,0:T(8,128)(2,1)S(1)} %get-tuple-element.37.mixed_ref, f32[8,2,512]{2,1,0:T(2,128)S(1)} %all_to_all.26.sums_ref, bf16[512,256]{1,0:T(8,128)(2,1)S(1)} %copy-done.5, bf16[512,256]{1,0:T(8,128)(2,1)S(1)} %copy-done.4, ...), custom_call_target="tpu_custom_call" | custom-call | flops 2000000000 | bytes 8388608 | tf_op jit(solution)/shard_map/local_grads/pallas_call | solution.py:581
  70.2 0.0 copy-done.8
  70.2 0.0 copy-done.6
  70.3 3.7 %all-to-all-start.3 = ((bf16[16,256,128]{2,1,0:T(8,128)(2,1)}), bf16[16,256,128]{2,1,0:T(8,128)(2,1)S(1)}, u32[]{:S(2)}, u32[]{:S(2)}) async-start(bf16[16,256,128]{2,1,0:T(8,128)(2,1)} %get-tuple-element.43), calls=%async_computation.3 | async-start | bytes 2097152 | tf_op jit(solution)/shard_map/all_to_all | solution.py:501
  73.9 6.4 %normed_and_gate.1 = (bf16[512,2048]{1,0:T(8,128)(2,1)}, bf16[512,2048]{1,0:T(8,128)(2,1)}) custom-call(bf16[512,2048]{1,0:T(8,128)(2,1)} %copy-done.8, f32[8,2,512]{2,1,0:T(2,128)} %copy-done.6, bf16[512,2048]{1,0:T(8,128)(2,1)} %gate_ref.3, f32[1,2048]{1,0:T(1,128)} %bitcast.2, bf16[512,2048]{1,0:T(8,128)(2,1)} %grad_ref.5), custom_call_target="tpu_custom_call" | custom-call | flops 2000000000 | bytes 8388608 | tf_op jit(solution)/shard_map/normed_and_gate/pallas_call | solution.py:591
  80.3 11.3 %all-to-all-done.3.in_ref = bf16[16,256,128]{2,1,0:T(8,128)(2,1)S(1)} async-done(((bf16[16,256,128]{2,1,0:T(8,128)(2,1)}), bf16[16,256,128]{2,1,0:T(8,128)(2,1)S(1)}, u32[]{:S(2)}, u32[]{:S(2)}) %all-to-all-start.3) | async-done | bytes 1048608 | tf_op jit(solution)/shard_map/all_to_all | solution.py:501
  91.7 1.2 %backward_scan.1 = bf16[16,256,128]{2,1,0:T(8,128)(2,1)} custom-call(bf16[16,256,128]{2,1,0:T(8,128)(2,1)S(1)} %all-to-all-done.3.in_ref, bf16[16,272,128]{2,1,0:T(8,128)(2,1)S(1)} %all-to-all-done.in_ref.decay_ref), custom_call_target="tpu_custom_call" | custom-call | flops 16777216 | bytes 2097152 | tf_op jit(solution)/shard_map/backward_scan/pallas_call | solution.py:617
  92.9 3.8 %all-to-all-start.4 = ((bf16[16,256,128]{2,1,0:T(8,128)(2,1)}), bf16[16,256,128]{2,1,0:T(8,128)(2,1)S(1)}, u32[]{:S(2)}, u32[]{:S(2)}) async-start(bf16[16,256,128]{2,1,0:T(8,128)(2,1)} %backward_scan.1), calls=%async_computation.4 | async-start | bytes 2097152 | tf_op jit(solution)/shard_map/all_to_all | solution.py:501
  96.8 0.0 copy-start.9
  96.8 1.6 %copy-done.9 = bf16[512,2048]{1,0:T(8,128)(2,1)S(1)} copy-done((bf16[512,2048]{1,0:T(8,128)(2,1)S(1)}, bf16[512,2048]{1,0:T(8,128)(2,1)}, u32[]{:S(2)}) %copy-start.9) | copy-done | bytes 2097176
  98.3 11.9 %within_segment_back.1 = (bf16[512,2048]{1,0:T(8,128)(2,1)}, f32[512,256]{1,0:T(8,128)}, bf16[512,256]{1,0:T(8,128)(2,1)}) custom-call(bf16[512,2048]{1,0:T(8,128)(2,1)} %x_ref.3, bf16[512,2048]{1,0:T(8,128)(2,1)S(1)} %copy-done.9, bf16[16,256,128]{2,1,0:T(8,128)(2,1)} %copy-done, bf16[512,256]{1,0:T(8,128)(2,1)} %keys_in.3, bf16[512,256]{1,0:T(8,128)(2,1)} %queries_ref.7, ...), custom_call_target="tpu_custom_call" | custom-call | flops 12000000000 | bytes 8388608 | tf_op jit(solution)/shard_map/within_segment_back/pallas_call | solution.py:600
  110.2 3.4 %all-to-all-done.4.grad_in = bf16[16,256,128]{2,1,0:T(8,128)(2,1)S(1)} async-done(((bf16[16,256,128]{2,1,0:T(8,128)(2,1)}), bf16[16,256,128]{2,1,0:T(8,128)(2,1)S(1)}, u32[]{:S(2)}, u32[]{:S(2)}) %all-to-all-start.4) | async-done | bytes 1048608 | tf_op jit(solution)/shard_map/all_to_all | solution.py:501
  113.6 4.9 %final_grads.1 = (bf16[512,2048]{1,0:T(8,128)(2,1)}, bf16[512,256]{1,0:T(8,128)(2,1)}) custom-call(bf16[512,2048]{1,0:T(8,128)(2,1)} %get-tuple-element.41.dx_in, bf16[512,2048]{1,0:T(8,128)(2,1)} %get-tuple-element.42.scaled_in, bf16[16,256,128]{2,1,0:T(8,128)(2,1)S(1)} %all-to-all-done.4.grad_in, bf16[512,256]{1,0:T(8,128)(2,1)} %keys_in.3, ...), custom_call_target="tpu_custom_call" | custom-call | flops 1073741824 | bytes 8388608 | tf_op jit(solution)/shard_map/final_grads/pallas_call | solution.py:461
Async XLA Ops:
  4.7 8.2 %copy-start.12 = (f32[32]{0:T(128)S(1)}, f32[32]{0:T(128)}, u32[]{:S(2)}) copy-start(f32[32]{0:T(128)} %param.15) | copy-start | bytes 388
  4.7 8.9 %copy-start.4 = (bf16[512,256]{1,0:T(8,128)(2,1)S(1)}, bf16[512,256]{1,0:T(8,128)(2,1)}, u32[]{:S(2)}) copy-start(bf16[512,256]{1,0:T(8,128)(2,1)} %get-tuple-element.28.fac_ref.fac_in) | copy-start | bytes 786436
  4.7 8.9 %copy-start.10 = (f32[512,128]{1,0:T(8,128)S(1)}, f32[512,128]{1,0:T(8,128)}, u32[]{:S(2)}) copy-start(f32[512,128]{1,0:T(8,128)} %get-tuple-element.29.col_ref) | copy-start | bytes 786436
  4.7 8.9 %copy-start.11 = (f32[8,8,512]{2,1,0:T(8,128)S(1)}, f32[8,8,512]{2,1,0:T(8,128)}, u32[]{:S(2)}) copy-start(f32[8,8,512]{2,1,0:T(8,128)} %get-tuple-element.30.row_ref) | copy-start | bytes 393220
  4.7 26.5 %all-to-all-start = ((bf16[16,272,128]{2,1,0:T(8,128)(2,1)}), bf16[16,272,128]{2,1,0:T(8,128)(2,1)S(1)}, u32[]{:S(2)}, u32[]{:S(2)}) async-start(bf16[16,272,128]{2,1,0:T(8,128)(2,1)} %get-tuple-element.27), calls=%async_computation | async-start | bytes 2228224 | tf_op jit(solution)/shard_map/all_to_all | solution.py:501
  13.6 38.2 %copy-start.5 = (bf16[512,256]{1,0:T(8,128)(2,1)S(1)}, bf16[512,256]{1,0:T(8,128)(2,1)}, u32[]{:S(2)}) copy-start(bf16[512,256]{1,0:T(8,128)(2,1)} %queries_ref.7) | copy-start | bytes 786436
  31.2 20.5 %copy-start.2 = (bf16[512,2048]{1,0:T(8,128)(2,1)S(1)}, bf16[512,2048]{1,0:T(8,128)(2,1)}, u32[]{:S(2)}) copy-start(bf16[512,2048]{1,0:T(8,128)(2,1)} %get-tuple-element.36.silu_ref) | copy-start | bytes 6291460
  31.2 20.5 %copy-start.3 = (bf16[512,2048]{1,0:T(8,128)(2,1)S(1)}, bf16[512,2048]{1,0:T(8,128)(2,1)}, u32[]{:S(2)}) copy-start(bf16[512,2048]{1,0:T(8,128)(2,1)} %get-tuple-element.34.local_ref) | copy-start | bytes 6291460
  31.2 20.5 %copy-start.7 = (f32[2048]{0:T(1024)S(1)}, f32[2048]{0:T(1024)}, u32[]{:S(2)}) copy-start(f32[2048]{0:T(1024)} %param.16) | copy-start | bytes 24580
  51.7 4.8 %copy-start = (bf16[16,256,128]{2,1,0:T(8,128)(2,1)}, bf16[16,256,128]{2,1,0:T(8,128)(2,1)S(1)}, u32[]{:S(2)}) copy-start(bf16[16,256,128]{2,1,0:T(8,128)(2,1)S(1)} %all_to_all.25.state_ref) | copy-start | bytes 3145732
  51.8 14.5 %copy-start.1 = (bf16[512,2048]{1,0:T(8,128)(2,1)S(1)}, bf16[512,2048]{1,0:T(8,128)(2,1)}, u32[]{:S(2)}) copy-start(bf16[512,2048]{1,0:T(8,128)(2,1)} %grad_ref.5) | copy-start | bytes 6291460
  56.5 13.7 %copy-start.8 = (bf16[512,2048]{1,0:T(8,128)(2,1)}, bf16[512,2048]{1,0:T(8,128)(2,1)S(1)}, u32[]{:S(2)}) copy-start(bf16[512,2048]{1,0:T(8,128)(2,1)S(1)} %get-tuple-element.37.mixed_ref) | copy-start | bytes 6291460
  66.3 4.0 %copy-start.6 = (f32[8,2,512]{2,1,0:T(2,128)}, f32[8,2,512]{2,1,0:T(2,128)S(1)}, u32[]{:S(2)}) copy-start(f32[8,2,512]{2,1,0:T(2,128)S(1)} %all_to_all.26.sums_ref) | copy-start | bytes 98308
  70.3 21.4 %all-to-all-start.3 = ((bf16[16,256,128]{2,1,0:T(8,128)(2,1)}), bf16[16,256,128]{2,1,0:T(8,128)(2,1)S(1)}, u32[]{:S(2)}, u32[]{:S(2)}) async-start(bf16[16,256,128]{2,1,0:T(8,128)(2,1)} %get-tuple-element.43), calls=%async_computation.3 | async-start | bytes 2097152 | tf_op jit(solution)/shard_map/all_to_all | solution.py:501
  92.9 20.7 %all-to-all-start.4 = ((bf16[16,256,128]{2,1,0:T(8,128)(2,1)}), bf16[16,256,128]{2,1,0:T(8,128)(2,1)S(1)}, u32[]{:S(2)}, u32[]{:S(2)}) async-start(bf16[16,256,128]{2,1,0:T(8,128)(2,1)} %backward_scan.1), calls=%async_computation.4 | async-start | bytes 2097152 | tf_op jit(solution)/shard_map/all_to_all | solution.py:501
  96.8 1.6 %copy-start.9 = (bf16[512,2048]{1,0:T(8,128)(2,1)S(1)}, bf16[512,2048]{1,0:T(8,128)(2,1)}, u32[]{:S(2)}) copy-start(bf16[512,2048]{1,0:T(8,128)(2,1)} %get-tuple-element.40.dy_ref) | copy-start | bytes 6291460

commit v3 on v2

--- a/solution.py
+++ b/solution.py
@@ -125,11 +125,12 @@
     @pl.loop(0, CHUNKS)
     def _(chunk):
         fetch(chunk).wait()
-        factors = fac_ref[...]
-        scaled = (x_ref[chunk].astype(F32) * expand(factors, END, chunk, LONG)).astype(BF16)
-        ends = nn(keys_t[...], scaled).astype(BF16)
-        decay = expand(factors[TOK - 16 :], START, chunk, LONG)
-        decay = jnp.broadcast_to(decay[15:16], (TAIL, LONG)).astype(BF16)
+        factor = expand(fac_ref[...], END, chunk, LONG)
+        ends = nn(keys_t[...], (x_ref[chunk].astype(F32) * factor).astype(BF16)).astype(BF16)
+        head = (lax.broadcasted_iota(jnp.int32, (HEADS, LONG), 1) >> 6) + LONG // P_SIZE * chunk
+        own = lax.broadcasted_iota(jnp.int32, (HEADS, LONG), 0) == head
+        decay = jnp.sum(jnp.where(own, start[:, TOK - 1 :], 0.0), axis=0, keepdims=True)
+        decay = jnp.broadcast_to(decay, (TAIL, LONG)).astype(BF16)
         for part in range(LONG // SLICE):
             lanes = slice(part * SLICE, (part + 1) * SLICE)
             ends_ref[chunk * (LONG // SLICE) + part, :N] = ends[:, lanes]
@@ -152,7 +153,10 @@
     return (jnp.exp2(jnp.minimum(col - row, 0.0)) * scores).astype(BF16)
 
 
-def local_kernel(x_ref, gate_ref, keys_ref, queries_ref, fac_ref, col_ref, row_ref, skip_ref, out_ref, silu_ref, scaled_ref, near, off1, off2):
+def local_kernel(
+    x_ref, gate_ref, keys_ref, queries_ref, fac_ref, col_ref, row_ref, skip_ref,
+    out_ref, gated_ref, ratio_ref, scaled_ref, near, off1, off2,
+):
     step = pl.program_id(0)
 
     @pl.when(step == 0)
@@ -174,7 +178,8 @@
     cols = pltpu.roll(col_ref[...], lax.rem(128 - HPS * step, 128), 1)
     scaled_ref[...] = (wide * expand(factors, END, step, WIDE)).astype(BF16)
     gate = gate_ref[...].astype(F32)
-    silu_ref[...] = (gate * jax.nn.sigmoid(gate)).astype(BF16)
+    silu = gate * jax.nn.sigmoid(gate)
+    ratio_ref[...] = (silu * expand(factors, START, step, WIDE)).astype(BF16)
     far = nn(off2[...], (wide[:HALF] * middle[:HALF]).astype(BF16)) * middle[HALF:]
     skip = skip_ref[...] * wide
     for i in range(BLKS):
@@ -192,7 +197,9 @@
                 row = row_ref[0, HPS + j : HPS + j + 1, blk(i)]
                 both.append(weights(cols[blk(i), j : j + 1], row, scores))
             within = nn(jnp.concatenate(both, 1), two_heads(x[blk(i), lanes]))
-            out_ref[blk(i), lanes] = (total[:, lanes] + within).astype(BF16)
+            mixed = total[:, lanes] + within
+            out_ref[blk(i), lanes] = mixed.astype(BF16)
+            gated_ref[blk(i), lanes] = (mixed * silu[blk(i), lanes]).astype(BF16)
 
 
 def forward_scan_kernel(in_ref, out_ref):
@@ -203,11 +210,18 @@
         running = running * decay + in_ref[k, :N].astype(F32)
 
 
-def backward_scan_kernel(in_ref, decay_ref, out_ref):
+def backward_scan_kernel(in_ref, ends_in, out, out_ref, decay_ref, sems):
+    decays = pltpu.make_async_copy(ends_in.at[:, pl.ds(N, TAIL)], decay_ref, sems.at[SEGS])
+    decays.start()
+    sends = [pltpu.make_async_copy(out_ref.at[k], out.at[k], sems.at[k]) for k in range(SEGS)]
     running = jnp.zeros((N, SLICE), F32)
+    decays.wait()
     for k in reversed(range(SEGS)):
         out_ref[k] = running.astype(BF16)
+        sends[k].start()
         running = running * decay_ref[k][:1].astype(F32) + in_ref[k].astype(F32)
+    for send in sends:
+        send.wait()
 
 
 def state_of(ref):
@@ -221,30 +235,42 @@
     return total
 
 
-def gate_kernel(local_ref, state_ref, queries_ref, fac_ref, silu_ref, gain_ref, grad_ref, mixed_ref, sums_ref, square, product):
-    step = pl.program_id(0)
-
-    @pl.when(step == 0)
-    def _():
-        square[...] = jnp.zeros_like(square)
-        product[...] = jnp.zeros_like(product)
-
-    carried = nn(queries_ref[...], state_of(state_ref)) * expand(fac_ref[...], START, step, LONG)
-    mixed = local_ref[...].astype(F32) + carried
-    mixed_ref[...] = mixed.astype(BF16)
-    gated = mixed * silu_ref[...].astype(F32)
-    squares = gated * gated
-    products = gated * (gain_ref[...] * grad_ref[...].astype(F32))
-    square[...] += fold(squares)
-    product[...] += fold(products)
-
-    @pl.when(step == COLS // LONG - 1)
-    def _():
-        both = jnp.concatenate(
-            [jnp.sum(square[...].T, axis=0, keepdims=True), jnp.sum(product[...].T, axis=0, keepdims=True)], 0
-        )
-        for part in range(PARTS):
-            sums_ref[part] = both
+def chunk_lanes(chunk):
+    return pl.ds(pl.multiple_of(chunk * LONG, LONG), LONG)
+
+
+def state_chunk(ref, chunk):
+    first = chunk * (LONG // SLICE)
+    return jnp.concatenate([ref[first + part] for part in range(LONG // SLICE)], 1)
+
+
+def gate_kernel(
+    local_ref, state_ref, queries_ref, ratio_ref, gain_ref, grad_in, gated_ref, sums_ref,
+    grad_ref, square, product, come,
+):
+    def fetch(chunk):
+        return pltpu.make_async_copy(columns_of(grad_in, chunk), grad_ref.at[chunk], come.at[chunk])
+
+    for chunk in range(CHUNKS):
+        fetch(chunk).start()
+    square[...] = jnp.zeros_like(square)
+    product[...] = jnp.zeros_like(product)
+
+    @pl.loop(0, CHUNKS)
+    def _(chunk):
+        lanes = chunk_lanes(chunk)
+        carried = nn(queries_ref[...], state_chunk(state_ref, chunk))
+        gated = local_ref[:, lanes].astype(F32) + ratio_ref[:, lanes].astype(F32) * carried
+        gated_ref[:, lanes] = gated.astype(BF16)
+        square[...] += fold(gated * gated)
+        fetch(chunk).wait()
+        product[...] += fold(gated * (gain_ref[:, lanes] * grad_ref[chunk].astype(F32)))
+
+    both = jnp.concatenate(
+        [jnp.sum(square[...].T, axis=0, keepdims=True), jnp.sum(product[...].T, axis=0, keepdims=True)], 0
+    )
+    for part in range(PARTS):
+        sums_ref[part] = both
 
 
 def norm_terms(sums_ref, inverse, slope):
@@ -261,44 +287,60 @@
     return jnp.concatenate([ref[...]] * (LONG // 128), 1)
 
 
-def grad_kernel(mixed_ref, sums_ref, queries_ref, fac_ref, silu_ref, gain_ref, grad_ref, dy_ref, out_ref, inverse, slope, queries_t):
+def grad_kernel(
+    gated_ref, sums_ref, queries_ref, ratio_ref, gain_ref, grad_ref, out,
+    local_ref, inverse, slope, go,
+):
+    def send(chunk):
+        return pltpu.make_async_copy(slices_of(local_ref, chunk), slices_of(out, chunk), go.at[chunk])
+
+    norm_terms(sums_ref, inverse, slope)
+    queries_t = transposed(queries_ref[...])
+
+    @pl.loop(0, CHUNKS, unroll=True)
+    def _(chunk):
+        lanes = chunk_lanes(chunk)
+        gated = gated_ref[:, lanes].astype(F32)
+        grad_gated = wide_of(inverse) * (gain_ref[:, lanes] * grad_ref[:, lanes].astype(F32)) - gated * wide_of(slope)
+        weighted = (grad_gated * ratio_ref[:, lanes].astype(F32)).astype(BF16)
+        local = nn(queries_t, weighted).astype(BF16)
+        for part in range(LONG // SLICE):
+            local_ref[chunk * (LONG // SLICE) + part] = local[:, part * SLICE : (part + 1) * SLICE]
+        send(chunk).start()
+
+    for chunk in range(CHUNKS):
+        send(chunk).wait()
+
+
+def norm_kernel(
+    local_ref, sums_ref, gate_ref, gain_ref, grad_ref, state_ref, queries_ref, fac_ref,
+    normed_ref, out_ref, dy_ref, dq_ref, inverse, slope,
+):
     step = pl.program_id(0)
 
     @pl.when(step == 0)
     def _():
         norm_terms(sums_ref, inverse, slope)
-        queries_t[...] = transposed(queries_ref[...])
-
-    silu = silu_ref[...].astype(F32)
-    gated = mixed_ref[...].astype(F32) * silu
-    grad_gated = wide_of(inverse) * (gain_ref[...] * grad_ref[...].astype(F32)) - gated * wide_of(slope)
-    dy = grad_gated * silu
-    dy_ref[...] = dy.astype(BF16)
-    weighted = (dy * expand(fac_ref[...], START, step, LONG)).astype(BF16)
-    local = nn(queries_t[...], weighted).astype(BF16)
-    for part in range(LONG // SLICE):
-        out_ref[part] = local[:, part * SLICE : (part + 1) * SLICE]
-
-
-def norm_kernel(mixed_ref, sums_ref, gate_ref, gain_ref, grad_ref, normed_ref, out_ref, inverse, slope):
-    step = pl.program_id(0)
-
-    @pl.when(step == 0)
-    def _():
-        norm_terms(sums_ref, inverse, slope)
+        dq_ref[...] = jnp.zeros_like(dq_ref)
 
     gate = gate_ref[...].astype(F32)
     sig = jax.nn.sigmoid(gate)
-    mixed = mixed_ref[...].astype(F32)
-    gated = mixed * (gate * sig)
+    state = state_of(state_ref)
+    start = expand(fac_ref[...], START, step, LONG)
+    mixed = local_ref[...].astype(F32) + nn(queries_ref[...], state) * start
+    silu = gate * sig
+    gated = mixed * silu
     gain = wide_of(inverse) * gain_ref[...]
     normed_ref[...] = (gated * gain).astype(BF16)
     grad_gated = gain * grad_ref[...].astype(F32) - gated * wide_of(slope)
     out_ref[...] = (grad_gated * mixed * (sig * (1.0 + gate * (1.0 - sig)))).astype(BF16)
+    dy = grad_gated * silu
+    dy_ref[...] = dy.astype(BF16)
+    dq_ref[...] += nt((dy * start).astype(BF16), state)
 
 
 def back_kernel(
-    x_ref, dy_ref, state_ref, keys_ref, queries_ref, fac_ref, col_ref, row_ref, skip_ref,
+    x_ref, dy_ref, dq_ref, keys_ref, queries_ref, fac_ref, col_ref, row_ref, skip_ref,
     dx_ref, dkeys_ref, dqueries_ref,
     near, off1, off2, dnear, doff1, doff2, dq,
 ):
@@ -317,15 +359,13 @@
         dnear[...] = jnp.zeros_like(dnear)
         doff1[...] = jnp.zeros_like(doff1)
         doff2[...] = jnp.zeros_like(doff2)
-        dq[...] = jnp.zeros_like(dq)
+        dq[...] = dq_ref[...]
 
     factors = fac_ref[...]
     x = x_ref[...]
     wide = x.astype(F32)
     dy = dy_ref[...]
     dwide = dy.astype(F32)
-    weighted = (dwide * expand(factors, START, step, WIDE)).astype(BF16)
-    dq[...] += nt(weighted, state_of(state_ref))
     middle = expand(factors, MIDDLE, step, WIDE)
     quarter = expand(factors, QUARTER, step, WIDE)
     cols = pltpu.roll(col_ref[...], lax.rem(128 - HPS * step, 128), 1)
@@ -378,14 +418,13 @@
 
 
 def final_kernel(
-    dx_in, scaled_in, grad_in, keys_in, fac_in, dkeys_in, out, out_keys,
-    dx_ref, scaled_ref, grad_ref, keys_ref, fac_ref, dkeys_ref, out_ref, out_keys_ref, total, small, come, go,
+    dx_in, scaled_in, grad_ref, keys_in, fac_in, dkeys_in, out, out_keys,
+    dx_ref, scaled_ref, keys_ref, fac_ref, dkeys_ref, out_ref, out_keys_ref, total, small, come, go,
 ):
     def fetch(chunk):
         return (
-            pltpu.make_async_copy(slices_of(grad_in, chunk), slices_of(grad_ref, chunk), come.at[0, chunk]),
-            pltpu.make_async_copy(columns_of(scaled_in, chunk), scaled_ref.at[chunk], come.at[1, chunk]),
-            pltpu.make_async_copy(columns_of(dx_in, chunk), dx_ref.at[chunk], come.at[2, chunk]),
+            pltpu.make_async_copy(columns_of(scaled_in, chunk), scaled_ref.at[chunk], come.at[0, chunk]),
+            pltpu.make_async_copy(columns_of(dx_in, chunk), dx_ref.at[chunk], come.at[1, chunk]),
         )
 
     def send(chunk):
@@ -407,8 +446,7 @@
     def _(chunk):
         for copy in fetch(chunk):
             copy.wait()
-        first = chunk * (LONG // SLICE)
-        state_grad = jnp.concatenate([grad_ref[first + part] for part in range(LONG // SLICE)], 1)
+        state_grad = state_chunk(grad_ref, chunk)
         from_end = nn(keys_ref[...], state_grad) * expand(fac_ref[...], END, chunk, LONG)
         out_ref[chunk] = (dx_ref[chunk].astype(F32) + from_end).astype(BF16)
         send(chunk).start()
@@ -457,12 +495,15 @@
 ANY = pl.BlockSpec(memory_space=pl.ANY)
 
 
-def manual_call(kernel, name, operands, out_shape, scratch):
+HERE = pl.BlockSpec(memory_space=pltpu.VMEM)
+
+
+def manual_call(kernel, name, operands, out_shape, scratch, here=(), out_here=()):
     return pl.pallas_call(
         kernel,
         name=name,
-        in_specs=[ANY] * len(operands),
-        out_specs=[ANY] * len(out_shape),
+        in_specs=[HERE if i in here else ANY for i in range(len(operands))],
+        out_specs=[HERE if i in out_here else ANY for i in range(len(out_shape))],
         out_shape=out_shape,
         scratch_shapes=scratch,
         compiler_params=pltpu.CompilerParams(vmem_limit_bytes=VMEM_MIB << 20),
@@ -481,19 +522,6 @@
         scratch_shapes=list(scratch),
         compiler_params=pltpu.CompilerParams(vmem_limit_bytes=VMEM_MIB << 20),
         cost_estimate=pl.CostEstimate(flops=int(2e9 * gmacs), bytes_accessed=int(mib * 2**20), transcendentals=0),
-    )
-
-
-def whole_call(kernel, name, in_specs, out_specs, out_shape):
-    return pl.pallas_call(
-        kernel,
-        name=name,
-        grid=(1,),
-        in_specs=in_specs,
-        out_specs=out_specs,
-        out_shape=out_shape,
-        compiler_params=pltpu.CompilerParams(vmem_limit_bytes=VMEM_MIB << 20),
-        cost_estimate=pl.CostEstimate(flops=2**24, bytes_accessed=2**21, transcendentals=0),
     )
 
 
@@ -547,60 +575,60 @@
     )
     all_ends = exchange(ends, "ctx")
 
-    mixed_local, silu, scaled = call(
+    mixed_local, gated_local, ratio, scaled = call(
         local_kernel,
         "within_segment",
         [TOKENS_BY_STEP, TOKENS_BY_STEP, MAP, MAP, FACTORS, COLUMNS, ROWS_BY_STEP, ROW_BY_STEP],
-        [TOKENS_BY_STEP] * 3,
-        [in_hbm(TOK, COLS, dtype=BF16)] * 3,
+        [TOKENS_BY_STEP] * 4,
+        [in_hbm(TOK, COLS, dtype=BF16)] * 4,
         score_scratch,
         steps=STEPS,
         gmacs=4.0,
     )(inputs, gate_input, input_map, output_map, factors, columns, rows, skip)
-    all_ends, mixed_local, silu, scaled = lax.optimization_barrier((all_ends, mixed_local, silu, scaled))
-
-    starts = whole_call(
-        forward_scan_kernel,
-        "forward_scan",
-        [whole((SEGS, N + TAIL, SLICE))],
-        whole((SEGS, N, SLICE)),
-        shape(SEGS, N, SLICE, dtype=BF16),
-    )(all_ends)
+    all_ends, mixed_local, gated_local, ratio, scaled = lax.optimization_barrier(
+        (all_ends, mixed_local, gated_local, ratio, scaled)
+    )
+
+    (starts,) = manual_call(
+        forward_scan_kernel, "forward_scan", (all_ends,), [shape(SEGS, N, SLICE, dtype=BF16)], [], (0,), (0,)
+    )
     state_in = exchange(starts, "ctx")
 
-    mixed, sums = call(
+    gated, sums = manual_call(
         gate_kernel,
         "carry_and_gate",
-        [TOKENS_BY_LONG, state_by(LONG), MAP, FACTORS, TOKENS_BY_LONG, ROW_BY_LONG, TOKENS_BY_LONG],
-        [TOKENS_BY_LONG, SUMS],
+        (gated_local, state_in, queries, ratio, gain, *hbm(out_grad)),
         [tokens, shape(PARTS, 2, TOK)],
-        norm_scratch,
-    )(mixed_local, state_in, queries, factors, silu, gain, *hbm(out_grad))
+        [chunk_scratch] + norm_scratch + [dma((CHUNKS,))],
+        here=range(5),
+        out_here=range(2),
+    )
     sums = exchange(sums, "tp")
 
-    dy, local_grads = call(
+    (local_grads,) = manual_call(
         grad_kernel,
         "local_grads",
-        [TOKENS_BY_LONG, SUMS, MAP, FACTORS, TOKENS_BY_LONG, ROW_BY_LONG, TOKENS_BY_LONG],
-        [TOKENS_BY_LONG, state_by(LONG)],
-        [in_hbm(TOK, COLS, dtype=BF16), in_hbm(SEGS, N, SLICE, dtype=BF16)],
-        norm_scratch + [pltpu.VMEM((N, TOK), BF16)],
-    )(mixed, sums, queries, factors, silu, gain, out_grad)
+        (gated, sums, queries, ratio, gain, out_grad),
+        [in_hbm(SEGS, N, SLICE, dtype=BF16)],
+        [pltpu.VMEM((SEGS, N, SLICE), BF16)] + norm_scratch + [dma((CHUNKS,))],
+        here=range(6),
+    )
     all_grads = exchange(local_grads, "ctx")
 
-    normed, grad_gate = call(
+    normed, grad_gate, dy, dq = call(
         norm_kernel,
         "normed_and_gate",
-        [TOKENS_BY_LONG, SUMS, TOKENS_BY_LONG, ROW_BY_LONG, TOKENS_BY_LONG],
-        [TOKENS_BY_LONG, TOKENS_BY_LONG],
-        [tokens, tokens],
+        [TOKENS_BY_LONG, SUMS, TOKENS_BY_LONG, ROW_BY_LONG, TOKENS_BY_LONG, state_by(LONG), MAP, FACTORS],
+        [TOKENS_BY_LONG, TOKENS_BY_LONG, TOKENS_BY_LONG, MAP],
+        [tokens, tokens, in_hbm(TOK, COLS, dtype=BF16), in_hbm(TOK, N)],
         norm_scratch,
-    )(*hbm(mixed, sums, gate_input, gain, out_grad))
+        gmacs=2.0,
+    )(*hbm(mixed_local, sums, gate_input, gain, out_grad, state_in, output_map, factors))
 
     dx, dkeys, dqueries = call(
         back_kernel,
         "within_segment_back",
-        [TOKENS_BY_STEP, TOKENS_BY_STEP, state_by(WIDE), MAP, MAP, FACTORS, COLUMNS, ROWS_BY_STEP, ROW_BY_STEP],
+        [TOKENS_BY_STEP, TOKENS_BY_STEP, MAP, MAP, MAP, FACTORS, COLUMNS, ROWS_BY_STEP, ROW_BY_STEP],
         [TOKENS_BY_STEP, MAP, MAP],
         [in_hbm(TOK, COLS, dtype=BF16), in_hbm(TOK, N), shape(TOK, N, dtype=BF16)],
         score_scratch
@@ -612,15 +640,16 @@
         ],
         steps=STEPS,
         gmacs=6.0,
-    )(inputs, dy, *hbm(state_in), input_map, output_map, factors, columns, rows, skip)
-
-    grad_starts = whole_call(
+    )(inputs, *hbm(dy, dq), input_map, output_map, factors, columns, rows, skip)
+
+    (grad_starts,) = manual_call(
         backward_scan_kernel,
         "backward_scan",
-        [whole((SEGS, N, SLICE)), pl.BlockSpec((SEGS, TAIL, SLICE), lambda i: (0, N // TAIL, 0))],
-        whole((SEGS, N, SLICE)),
-        shape(SEGS, N, SLICE, dtype=BF16),
-    )(all_grads, all_ends)
+        (all_grads, all_ends),
+        [in_hbm(SEGS, N, SLICE, dtype=BF16)],
+        [pltpu.VMEM((SEGS, N, SLICE), BF16), pltpu.VMEM((SEGS, TAIL, SLICE), BF16), dma((SEGS + 1,))],
+        here=(0,),
+    )
     state_grad = exchange(grad_starts, "ctx")
 
     grad_inputs, grad_keys = manual_call(
@@ -631,7 +660,6 @@
         [
             chunk_scratch,
             chunk_scratch,
-            pltpu.VMEM((SEGS, N, SLICE), BF16),
             pltpu.VMEM((TOK, N), BF16),
             pltpu.VMEM((TOK, 2 * SLICE), BF16),
             pltpu.VMEM((TOK, N), F32),
@@ -639,9 +667,10 @@
             pltpu.VMEM((TOK, N), BF16),
             pltpu.VMEM((TOK, N), F32),
             dma((4,)),
-            dma((3, CHUNKS)),
+            dma((2, CHUNKS)),
             dma((CHUNKS,)),
         ],
+        here=(2,),
     )
     return normed, grad_inputs, grad_gate, grad_keys, dqueries
 

time: 119 us -> 116 us (0.975)
  local copies, waits for them, and re-layouts: 2.39 us -> 0.83 us
    pallas_call x6, Pallas kernels: 19 us -> 15.8 us  [manual_call(): pl.pallas_call(kernel, name=name, in_specs=[HERE if i in here else ANY fo...]
    pallas_call x1, Pallas kernels: 6.42 us -> 8.97 us  [body(): call(norm_kernel, 'normed_and_gate', [TOKENS_BY_LONG, SUMS, TOKENS_BY_LON...]
    unnamed x26 -> x30, local copies, waits for them, and re-layouts: 1.64 us -> 0.07 us
  transfers between devices with their start and end apart: 3 -> 3, of which waited for: 3 -> 3; matrix products, arithmetic and copies ran while one was open for 1% -> 1% of each run, Pallas kernels for 24% -> 27%
where the time goes in v3:
time: 116 us; the launch traced here: 115 us
  Pallas kernels  46.8 us (40%)
  blocking collectives  30 us (26%)
  waiting for transfers between devices  21.4 us (18%)
  starting transfers between devices  15.4 us (13%)
    all_to_all x2, blocking collectives, exchange(): return lax.all_to_all(a, axis, 0, 0)  30 us
    all_to_all x3, waiting for transfers between devices, exchange(): return lax.all_to_all(a, axis, 0, 0)  21.4 us
    pallas_call x6, Pallas kernels, manual_call(): pl.pallas_call(kernel, name=name, in_specs=[HERE if i in here else ANY fo...  15.8 us
    all_to_all x3, starting transfers between devices, exchange(): return lax.all_to_all(a, axis, 0, 0)  15.4 us
    pallas_call x1, Pallas kernels, body(): call(back_kernel, 'within_segment_back', [TOKENS_BY_STEP, TOKENS_BY_STEP,...  11.3 us
    pallas_call x1, Pallas kernels, body(): call(local_kernel, 'within_segment', [TOKENS_BY_STEP, TOKENS_BY_STEP, MAP...  10.7 us
    pallas_call x1, Pallas kernels, body(): call(norm_kernel, 'normed_and_gate', [TOKENS_BY_LONG, SUMS, TOKENS_BY_LON...  8.97 us
  transfers between devices with their start and end apart: 3, of which 3 were waited for; matrix products, arithmetic and copies ran while one was open for 1% of the time, Pallas kernels for 27%

profile of v3, /device:TPU:0, one launch (start us, length us, event | category | flops | bytes accessed | tf_op | source)
XLA Modules:
  0.0 115.3 jit_solution(8135855662738599697)
XLA Ops:
  0.6 3.9 %segment_ends.1 = (bf16[16,272,128]{2,1,0:T(8,128)(2,1)}, bf16[512,256]{1,0:T(8,128)(2,1)}, f32[512,128]{1,0:T(8,128)}, f32[8,8,512]{2,1,0:T(8,128)}) custom-call(f32[32,512]{1,0:T(8,128)} %step_in.1, f32[1,32]{1,0:T(1,128)} %bitcast.5, bf16[512,2048]{1,0:T(8,128)(2,1)} %x_ref.3, bf16[512,256]{1,0:T(8,128)(2,1)} %keys_in.3), custom_call_target="tpu_custom_call" | custom-call | flops 1073741824 | bytes 8388608 | tf_op jit(solution)/shard_map/segment_ends/pallas_call | solution.py:502
  4.6 0.0 copy-start.14
  4.6 0.0 copy-start.7
  4.6 0.0 copy-start.11
  4.6 0.0 copy-start.13
  4.6 8.1 %all-to-all-start = ((bf16[16,272,128]{2,1,0:T(8,128)(2,1)}), bf16[16,272,128]{2,1,0:T(8,128)(2,1)S(1)}, u32[]{:S(2)}, u32[]{:S(2)}) async-start(bf16[16,272,128]{2,1,0:T(8,128)(2,1)} %get-tuple-element.29), calls=%async_computation | async-start | bytes 2228224 | tf_op jit(solution)/shard_map/all_to_all | solution.py:529
  12.7 0.0 copy-done.14
  12.7 0.1 broadcast_in_dim.3
  12.8 0.7 reshape_reshape.3.skip_ref
  13.5 0.0 copy-done.7
  13.5 0.0 copy-done.11
  13.5 0.0 copy-done.13
  13.5 10.7 %within_segment.1 = (bf16[512,2048]{1,0:T(8,128)(2,1)}, bf16[512,2048]{1,0:T(8,128)(2,1)}, bf16[512,2048]{1,0:T(8,128)(2,1)}, bf16[512,2048]{1,0:T(8,128)(2,1)}) custom-call(bf16[512,2048]{1,0:T(8,128)(2,1)} %x_ref.3, bf16[512,2048]{1,0:T(8,128)(2,1)} %gate_ref.3, bf16[512,256]{1,0:T(8,128)(2,1)} %keys_in.3, bf16[512,256]{1,0:T(8,128)(2,1)} %queries_ref.9, ...), custom_call_target="tpu_custom_call" | custom-call | flops 8000000000 | bytes 8388608 | tf_op jit(solution)/shard_map/within_segment/pallas_call | solution.py:578
  24.2 6.9 %all-to-all-done.in_ref.ends_in = bf16[16,272,128]{2,1,0:T(8,128)(2,1)S(1)} async-done(((bf16[16,272,128]{2,1,0:T(8,128)(2,1)}), bf16[16,272,128]{2,1,0:T(8,128)(2,1)S(1)}, u32[]{:S(2)}, u32[]{:S(2)}) %all-to-all-start) | async-done | bytes 1114144 | tf_op jit(solution)/shard_map/all_to_all | solution.py:529
  31.2 0.0 copy-start.4
  31.2 0.0 copy-start.1
  31.2 0.0 copy-start.3
  31.2 0.0 copy-start.6
  31.2 0.0 copy-start.10
  31.2 0.2 forward_scan.1
  31.4 20.3 %all_to_all.25.state_ref = bf16[16,256,128]{2,1,0:T(8,128)(2,1)S(1)} all-to-all(bf16[16,256,128]{2,1,0:T(8,128)(2,1)S(1)} %forward_scan.1), channel_id=1, replica_groups=mesh['ctx'=16,'tp'=8] {'ctx'}, dimensions={0} | all-to-all | bytes 2097152 | tf_op jit(solution)/shard_map/all_to_all | solution.py:529
  51.7 0.0 copy-done.4
  51.7 0.0 copy-done.1
  51.7 0.0 copy-done.3
  51.7 0.0 copy-done.6
  51.7 0.0 copy-done.10
  51.7 0.0 copy-start
  51.7 3.1 %carry_and_gate.1 = (bf16[512,2048]{1,0:T(8,128)(2,1)S(1)}, f32[8,2,512]{2,1,0:T(2,128)S(1)}) custom-call(bf16[512,2048]{1,0:T(8,128)(2,1)S(1)} %copy-done.3, bf16[16,256,128]{2,1,0:T(8,128)(2,1)S(1)} %all_to_all.25.state_ref, bf16[512,256]{1,0:T(8,128)(2,1)S(1)} %copy-done.6, bf16[512,2048]{1,0:T(8,128)(2,1)S(1)} %copy-done.1, f32[1,2048]{1,0:T(1,128)S(1)} %bitcast.3, ...), custom_call_target="tpu_custom_call" | custom-call | flops 1073741824 | bytes 8388608 | tf_op jit(solution)/shard_map/carry_and_gate/pallas_call | solution.py:502
  54.8 0.0 copy-done.2
  54.8 9.7 %all_to_all.26.sums_ref = f32[8,2,512]{2,1,0:T(2,128)S(1)} all-to-all(f32[8,2,512]{2,1,0:T(2,128)S(1)} %get-tuple-element.41), channel_id=1, replica_groups=mesh['ctx'=16,'tp'=8] {'tp'}, dimensions={0} | all-to-all | bytes 65536 | tf_op jit(solution)/shard_map/all_to_all | solution.py:529
  64.5 0.0 copy-start.9
  64.5 0.0 copy-done
  64.5 2.5 %local_grads.1 = bf16[16,256,128]{2,1,0:T(8,128)(2,1)} custom-call(bf16[512,2048]{1,0:T(8,128)(2,1)S(1)} %get-tuple-element.47.gated_ref, f32[8,2,512]{2,1,0:T(2,128)S(1)} %all_to_all.26.sums_ref, bf16[512,256]{1,0:T(8,128)(2,1)S(1)} %copy-done.6, bf16[512,2048]{1,0:T(8,128)(2,1)S(1)} %copy-done.1, f32[1,2048]{1,0:T(1,128)S(1)} %bitcast.4, ...), custom_call_target="tpu_custom_call" | custom-call | flops 1073741824 | bytes 8388608 | tf_op jit(solution)/shard_map/local_grads/pallas_call | solution.py:502
  67.0 0.0 copy-done.9
  67.0 3.7 %all-to-all-start.3 = ((bf16[16,256,128]{2,1,0:T(8,128)(2,1)}), bf16[16,256,128]{2,1,0:T(8,128)(2,1)S(1)}, u32[]{:S(2)}, u32[]{:S(2)}) async-start(bf16[16,256,128]{2,1,0:T(8,128)(2,1)} %local_grads.1), calls=%async_computation.3 | async-start | bytes 2097152 | tf_op jit(solution)/shard_map/all_to_all | solution.py:529
  70.7 0.0 copy-start.5
  70.7 9.0 %normed_and_gate.1 = (bf16[512,2048]{1,0:T(8,128)(2,1)}, bf16[512,2048]{1,0:T(8,128)(2,1)}, bf16[512,2048]{1,0:T(8,128)(2,1)}, f32[512,256]{1,0:T(8,128)}) custom-call(bf16[512,2048]{1,0:T(8,128)(2,1)} %get-tuple-element.37.local_ref, f32[8,2,512]{2,1,0:T(2,128)} %copy-done.9, bf16[512,2048]{1,0:T(8,128)(2,1)} %gate_ref.3, f32[1,2048]{1,0:T(1,128)} %bitcast.2, ...), custom_call_target="tpu_custom_call" | custom-call | flops 4000000000 | bytes 8388608 | tf_op jit(solution)/shard_map/normed_and_gate/pallas_call | solution.py:618
  79.7 0.0 copy-start.8
  79.7 0.0 copy-start.12
  79.7 8.8 %all-to-all-done.3.in_ref = bf16[16,256,128]{2,1,0:T(8,128)(2,1)S(1)} async-done(((bf16[16,256,128]{2,1,0:T(8,128)(2,1)}), bf16[16,256,128]{2,1,0:T(8,128)(2,1)S(1)}, u32[]{:S(2)}, u32[]{:S(2)}) %all-to-all-start.3) | async-done | bytes 1048608 | tf_op jit(solution)/shard_map/all_to_all | solution.py:529
  88.5 0.0 copy-done.5
  88.5 1.3 %backward_scan.1 = bf16[16,256,128]{2,1,0:T(8,128)(2,1)} custom-call(bf16[16,256,128]{2,1,0:T(8,128)(2,1)S(1)} %all-to-all-done.3.in_ref, bf16[16,272,128]{2,1,0:T(8,128)(2,1)S(1)} %copy-done.5), custom_call_target="tpu_custom_call" | custom-call | flops 1073741824 | bytes 8388608 | tf_op jit(solution)/shard_map/backward_scan/pallas_call | solution.py:502
  89.8 3.7 %all-to-all-start.4 = ((bf16[16,256,128]{2,1,0:T(8,128)(2,1)}), bf16[16,256,128]{2,1,0:T(8,128)(2,1)S(1)}, u32[]{:S(2)}, u32[]{:S(2)}) async-start(bf16[16,256,128]{2,1,0:T(8,128)(2,1)} %backward_scan.1), calls=%async_computation.4 | async-start | bytes 2097152 | tf_op jit(solution)/shard_map/all_to_all | solution.py:529
  93.4 0.0 copy-done.8
  93.4 0.0 copy-done.12
  93.5 11.3 %within_segment_back.1 = (bf16[512,2048]{1,0:T(8,128)(2,1)}, f32[512,256]{1,0:T(8,128)}, bf16[512,256]{1,0:T(8,128)(2,1)}) custom-call(bf16[512,2048]{1,0:T(8,128)(2,1)} %x_ref.3, bf16[512,2048]{1,0:T(8,128)(2,1)} %get-tuple-element.43.dy_ref, f32[512,256]{1,0:T(8,128)} %get-tuple-element.44.dq_ref, bf16[512,256]{1,0:T(8,128)(2,1)} %keys_in.3, ...), custom_call_target="tpu_custom_call" | custom-call | flops 12000000000 | bytes 8388608 | tf_op jit(solution)/shard_map/within_segment_back/pallas_call | solution.py:628
  104.8 5.7 %all-to-all-done.4.grad_ref = bf16[16,256,128]{2,1,0:T(8,128)(2,1)S(1)} async-done(((bf16[16,256,128]{2,1,0:T(8,128)(2,1)}), bf16[16,256,128]{2,1,0:T(8,128)(2,1)S(1)}, u32[]{:S(2)}, u32[]{:S(2)}) %all-to-all-start.4) | async-done | bytes 1048608 | tf_op jit(solution)/shard_map/all_to_all | solution.py:529
  110.5 4.8 %final_grads.1 = (bf16[512,2048]{1,0:T(8,128)(2,1)}, bf16[512,256]{1,0:T(8,128)(2,1)}) custom-call(bf16[512,2048]{1,0:T(8,128)(2,1)} %get-tuple-element.45.dx_in, bf16[512,2048]{1,0:T(8,128)(2,1)} %get-tuple-element.46.scaled_in, bf16[16,256,128]{2,1,0:T(8,128)(2,1)S(1)} %all-to-all-done.4.grad_ref, bf16[512,256]{1,0:T(8,128)(2,1)} %keys_in.3, ...), custom_call_target="tpu_custom_call" | custom-call | flops 1073741824 | bytes 8388608 | tf_op jit(solution)/shard_map/final_grads/pallas_call | solution.py:502
  (1 shorter events, 0.0 us)
Async XLA Ops:
  4.6 8.2 %copy-start.14 = (f32[32]{0:T(128)S(1)}, f32[32]{0:T(128)}, u32[]{:S(2)}) copy-start(f32[32]{0:T(128)} %param.15) | copy-start | bytes 388
  4.6 8.9 %copy-start.7 = (bf16[512,256]{1,0:T(8,128)(2,1)S(1)}, bf16[512,256]{1,0:T(8,128)(2,1)}, u32[]{:S(2)}) copy-start(bf16[512,256]{1,0:T(8,128)(2,1)} %get-tuple-element.30.fac_ref.fac_in) | copy-start | bytes 786436
  4.6 8.9 %copy-start.11 = (f32[512,128]{1,0:T(8,128)S(1)}, f32[512,128]{1,0:T(8,128)}, u32[]{:S(2)}) copy-start(f32[512,128]{1,0:T(8,128)} %get-tuple-element.31.col_ref) | copy-start | bytes 786436
  4.6 8.9 %copy-start.13 = (f32[8,8,512]{2,1,0:T(8,128)S(1)}, f32[8,8,512]{2,1,0:T(8,128)}, u32[]{:S(2)}) copy-start(f32[8,8,512]{2,1,0:T(8,128)} %get-tuple-element.32.row_ref) | copy-start | bytes 393220
  4.6 26.6 %all-to-all-start = ((bf16[16,272,128]{2,1,0:T(8,128)(2,1)}), bf16[16,272,128]{2,1,0:T(8,128)(2,1)S(1)}, u32[]{:S(2)}, u32[]{:S(2)}) async-start(bf16[16,272,128]{2,1,0:T(8,128)(2,1)} %get-tuple-element.29), calls=%async_computation | async-start | bytes 2228224 | tf_op jit(solution)/shard_map/all_to_all | solution.py:529
  31.2 20.5 %copy-start.4 = (bf16[16,272,128]{2,1,0:T(8,128)(2,1)}, bf16[16,272,128]{2,1,0:T(8,128)(2,1)S(1)}, u32[]{:S(2)}) copy-start(bf16[16,272,128]{2,1,0:T(8,128)(2,1)S(1)} %all-to-all-done.in_ref.ends_in) | copy-start | bytes 3342340
  31.2 20.5 %copy-start.1 = (bf16[512,2048]{1,0:T(8,128)(2,1)S(1)}, bf16[512,2048]{1,0:T(8,128)(2,1)}, u32[]{:S(2)}) copy-start(bf16[512,2048]{1,0:T(8,128)(2,1)} %get-tuple-element.40.ratio_ref) | copy-start | bytes 6291460
  31.2 20.5 %copy-start.3 = (bf16[512,2048]{1,0:T(8,128)(2,1)S(1)}, bf16[512,2048]{1,0:T(8,128)(2,1)}, u32[]{:S(2)}) copy-start(bf16[512,2048]{1,0:T(8,128)(2,1)} %get-tuple-element.38.local_ref) | copy-start | bytes 6291460
  31.2 20.5 %copy-start.6 = (bf16[512,256]{1,0:T(8,128)(2,1)S(1)}, bf16[512,256]{1,0:T(8,128)(2,1)}, u32[]{:S(2)}) copy-start(bf16[512,256]{1,0:T(8,128)(2,1)} %queries_ref.9) | copy-start | bytes 786436
  31.2 20.5 %copy-start.10 = (f32[2048]{0:T(1024)S(1)}, f32[2048]{0:T(1024)}, u32[]{:S(2)}) copy-start(f32[2048]{0:T(1024)} %param.16) | copy-start | bytes 24580
  51.7 3.1 %copy-start.2 = (bf16[16,256,128]{2,1,0:T(8,128)(2,1)}, bf16[16,256,128]{2,1,0:T(8,128)(2,1)S(1)}, u32[]{:S(2)}) copy-start(bf16[16,256,128]{2,1,0:T(8,128)(2,1)S(1)} %all_to_all.25.state_ref) | copy-start | bytes 3145732
  51.7 12.8 %copy-start = (bf16[512,2048]{1,0:T(8,128)(2,1)S(1)}, bf16[512,2048]{1,0:T(8,128)(2,1)}, u32[]{:S(2)}) copy-start(bf16[512,2048]{1,0:T(8,128)(2,1)} %grad_ref.3) | copy-start | bytes 6291460
  64.5 2.5 %copy-start.9 = (f32[8,2,512]{2,1,0:T(2,128)}, f32[8,2,512]{2,1,0:T(2,128)S(1)}, u32[]{:S(2)}) copy-start(f32[8,2,512]{2,1,0:T(2,128)S(1)} %all_to_all.26.sums_ref) | copy-start | bytes 98308
  67.0 21.4 %all-to-all-start.3 = ((bf16[16,256,128]{2,1,0:T(8,128)(2,1)}), bf16[16,256,128]{2,1,0:T(8,128)(2,1)S(1)}, u32[]{:S(2)}, u32[]{:S(2)}) async-start(bf16[16,256,128]{2,1,0:T(8,128)(2,1)} %local_grads.1), calls=%async_computation.3 | async-start | bytes 2097152 | tf_op jit(solution)/shard_map/all_to_all | solution.py:529
  70.7 17.8 %copy-start.5 = (bf16[16,272,128]{2,1,0:T(8,128)(2,1)S(1)}, bf16[16,272,128]{2,1,0:T(8,128)(2,1)}, u32[]{:S(2)}) copy-start(bf16[16,272,128]{2,1,0:T(8,128)(2,1)} %copy-done.4) | copy-start | bytes 3342340
  79.7 13.8 %copy-start.8 = (bf16[512,256]{1,0:T(8,128)(2,1)S(1)}, bf16[512,256]{1,0:T(8,128)(2,1)}, u32[]{:S(2)}) copy-start(bf16[512,256]{1,0:T(8,128)(2,1)} %get-tuple-element.30.fac_ref.fac_in) | copy-start | bytes 786436
  79.7 13.8 %copy-start.12 = (f32[512,128]{1,0:T(8,128)S(1)}, f32[512,128]{1,0:T(8,128)}, u32[]{:S(2)}) copy-start(f32[512,128]{1,0:T(8,128)} %get-tuple-element.31.col_ref) | copy-start | bytes 786436
  89.8 20.7 %all-to-all-start.4 = ((bf16[16,256,128]{2,1,0:T(8,128)(2,1)}), bf16[16,256,128]{2,1,0:T(8,128)(2,1)S(1)}, u32[]{:S(2)}, u32[]{:S(2)}) async-start(bf16[16,256,128]{2,1,0:T(8,128)(2,1)} %backward_scan.1), calls=%async_computation.4 | async-start | bytes 2097152 | tf_op jit(solution)/shard_map/all_to_all | solution.py:529

commit v4 on v3

--- a/solution.py
+++ b/solution.py
@@ -1,3 +1,5 @@
+import functools
+
 import jax
 import jax.numpy as jnp
 from jax import lax
@@ -24,6 +26,10 @@
 CHUNKS = COLS // LONG
 HPS = WIDE // P_SIZE
 VMEM_MIB = 36
+NORM = 512
+NORM_CHUNKS = COLS // NORM
+EARLY_STEPS = 2
+EARLY_CHUNKS = 1
 SUB = 128
 BLKS = TOK // SUB
 HALF = TOK // 2
@@ -61,6 +67,18 @@
     lane = lax.broadcasted_iota(jnp.int32, a.shape, 1)
     zero = jnp.zeros_like(a)
     return jnp.concatenate([jnp.where(lane < P_SIZE, a, zero), jnp.where(lane < P_SIZE, zero, a)], 0)
+
+
+def column_of(row_ref):
+    place = lax.broadcasted_iota(jnp.int32, (HEADS, HEADS), 0)
+    diagonal = place == lax.broadcasted_iota(jnp.int32, (HEADS, HEADS), 1)
+    return jnp.sum(jnp.where(diagonal, row_ref[...], 0.0), axis=1, keepdims=True)
+
+
+def channel_row(column, step):
+    head = (lax.broadcasted_iota(jnp.int32, (HEADS, WIDE), 1) >> 6) + HPS * step
+    own = lax.broadcasted_iota(jnp.int32, (HEADS, WIDE), 0) == head
+    return jnp.sum(jnp.where(own, column, 0.0), axis=0, keepdims=True)
 
 
 def blk(i):
@@ -96,9 +114,7 @@
     copies[1].wait()
 
     steps = step_ref[...]
-    diagonal = lax.broadcasted_iota(jnp.int32, (HEADS, HEADS), 0) == lax.broadcasted_iota(jnp.int32, (HEADS, HEADS), 1)
-    rate = jnp.sum(jnp.where(diagonal, rate_ref[...], 0.0), axis=1, keepdims=True)
-    logs = steps * (rate * -LOG2E)
+    logs = steps * (column_of(rate_ref) * -LOG2E)
     high = logs.astype(BF16)
     rest = logs - high.astype(F32)
     mid, low = split(rest)
@@ -153,14 +169,45 @@
     return (jnp.exp2(jnp.minimum(col - row, 0.0)) * scores).astype(BF16)
 
 
-def local_kernel(
-    x_ref, gate_ref, keys_ref, queries_ref, fac_ref, col_ref, row_ref, skip_ref,
-    out_ref, gated_ref, ratio_ref, scaled_ref, near, off1, off2,
-):
-    step = pl.program_id(0)
-
-    @pl.when(step == 0)
+def steps_of(array, step):
+    return array.at[:, pl.ds(pl.multiple_of(step * WIDE, WIDE), WIDE)]
+
+
+def bounds(part, early, total):
+    count = early * (1 - lax.axis_index("tp") % 2)
+    return (0, count) if part == 0 else (count, total)
+
+
+def local_kernel(part, x_in, gate_in, *refs):
+    small_in, refs = refs[:6], refs[6:]
+    outs, refs = refs[-19:-15], refs[-15:]
+    x_buf, gate_buf, small_refs, results = refs[0], refs[1], refs[2:8], refs[8]
+    near, off1, off2, small, come, go = refs[9:]
+    keys_ref, queries_ref, fac_ref, col_ref, row_ref, skip_ref = small_refs
+    first, last = bounds(part, EARLY_STEPS, STEPS)
+
+    def fetch(step):
+        return (
+            pltpu.make_async_copy(steps_of(x_in, step), x_buf.at[step], come.at[0, step]),
+            pltpu.make_async_copy(steps_of(gate_in, step), gate_buf.at[step], come.at[1, step]),
+        )
+
+    def send(step):
+        return [pltpu.make_async_copy(results.at[i, step], steps_of(out, step), go.at[i, step]) for i, out in enumerate(outs)]
+
+    @pl.when(first < last)
     def _():
+        copies = [pltpu.make_async_copy(a, b, small.at[i]) for i, (a, b) in enumerate(zip(small_in, small_refs))]
+        for copy in copies:
+            copy.start()
+
+        @pl.loop(first, last)
+        def _(step):
+            for copy in fetch(step):
+                copy.start()
+
+        for copy in copies:
+            copy.wait()
         target = lax.broadcasted_iota(jnp.int32, (SUB, SUB), 0)
         source = lax.broadcasted_iota(jnp.int32, (SUB, SUB), 1)
         for i in range(BLKS):
@@ -170,36 +217,47 @@
             off1[i] = nt(queries_ref[blk(2 * i + 1)], keys_ref[blk(2 * i)]).astype(BF16)
         off2[...] = nt(queries_ref[HALF:], keys_ref[:HALF]).astype(BF16)
 
-    factors = fac_ref[...]
-    x = x_ref[...]
-    wide = x.astype(F32)
-    middle = expand(factors, MIDDLE, step, WIDE)
-    quarter = expand(factors, QUARTER, step, WIDE)
-    cols = pltpu.roll(col_ref[...], lax.rem(128 - HPS * step, 128), 1)
-    scaled_ref[...] = (wide * expand(factors, END, step, WIDE)).astype(BF16)
-    gate = gate_ref[...].astype(F32)
-    silu = gate * jax.nn.sigmoid(gate)
-    ratio_ref[...] = (silu * expand(factors, START, step, WIDE)).astype(BF16)
-    far = nn(off2[...], (wide[:HALF] * middle[:HALF]).astype(BF16)) * middle[HALF:]
-    skip = skip_ref[...] * wide
-    for i in range(BLKS):
-        total = skip[blk(i)]
-        if i % 2:
-            before = (wide[blk(i - 1)] * quarter[blk(i - 1)]).astype(BF16)
-            total += nn(off1[i // 2], before) * quarter[blk(i)]
-        if i >= 2:
-            total += far[blk(i - 2)]
-        scores = near[i]
-        for pair in range(WIDE // SLICE):
-            lanes = slice(pair * SLICE, (pair + 1) * SLICE)
-            both = []
-            for j in (2 * pair, 2 * pair + 1):
-                row = row_ref[0, HPS + j : HPS + j + 1, blk(i)]
-                both.append(weights(cols[blk(i), j : j + 1], row, scores))
-            within = nn(jnp.concatenate(both, 1), two_heads(x[blk(i), lanes]))
-            mixed = total[:, lanes] + within
-            out_ref[blk(i), lanes] = mixed.astype(BF16)
-            gated_ref[blk(i), lanes] = (mixed * silu[blk(i), lanes]).astype(BF16)
+        @pl.loop(first, last)
+        def _(step):
+            for copy in fetch(step):
+                copy.wait()
+            factors = fac_ref[...]
+            x = x_buf[step]
+            wide = x.astype(F32)
+            middle = expand(factors, MIDDLE, step, WIDE)
+            quarter = expand(factors, QUARTER, step, WIDE)
+            cols = pltpu.roll(col_ref[...], lax.rem(128 - HPS * step, 128), 1)
+            results[3, step] = (wide * expand(factors, END, step, WIDE)).astype(BF16)
+            gate = gate_buf[step].astype(F32)
+            silu = gate * jax.nn.sigmoid(gate)
+            results[2, step] = (silu * expand(factors, START, step, WIDE)).astype(BF16)
+            far = nn(off2[...], (wide[:HALF] * middle[:HALF]).astype(BF16)) * middle[HALF:]
+            skip = channel_row(column_of(skip_ref), step) * wide
+            for i in range(BLKS):
+                total = skip[blk(i)]
+                if i % 2:
+                    before = (wide[blk(i - 1)] * quarter[blk(i - 1)]).astype(BF16)
+                    total += nn(off1[i // 2], before) * quarter[blk(i)]
+                if i >= 2:
+                    total += far[blk(i - 2)]
+                scores = near[i]
+                for pair in range(WIDE // SLICE):
+                    lanes = slice(pair * SLICE, (pair + 1) * SLICE)
+                    both = []
+                    for j in (2 * pair, 2 * pair + 1):
+                        row = row_ref[step, HPS + j : HPS + j + 1, blk(i)]
+                        both.append(weights(cols[blk(i), j : j + 1], row, scores))
+                    within = nn(jnp.concatenate(both, 1), two_heads(x[blk(i), lanes]))
+                    mixed = total[:, lanes] + within
+                    results[0, step, blk(i), lanes] = mixed.astype(BF16)
+                    results[1, step, blk(i), lanes] = (mixed * silu[blk(i), lanes]).astype(BF16)
+            for copy in send(step):
+                copy.start()
+
+        @pl.loop(first, last)
+        def _(step):
+            for copy in send(step):
+                copy.wait()
 
 
 def forward_scan_kernel(in_ref, out_ref):
@@ -263,8 +321,12 @@
         gated = local_ref[:, lanes].astype(F32) + ratio_ref[:, lanes].astype(F32) * carried
         gated_ref[:, lanes] = gated.astype(BF16)
         square[...] += fold(gated * gated)
+
+    @pl.loop(0, CHUNKS)
+    def _(chunk):
+        lanes = chunk_lanes(chunk)
         fetch(chunk).wait()
-        product[...] += fold(gated * (gain_ref[:, lanes] * grad_ref[chunk].astype(F32)))
+        product[...] += fold(gated_ref[:, lanes].astype(F32) * (gain_ref[:, lanes] * grad_ref[chunk].astype(F32)))
 
     both = jnp.concatenate(
         [jnp.sum(square[...].T, axis=0, keepdims=True), jnp.sum(product[...].T, axis=0, keepdims=True)], 0
@@ -283,8 +345,8 @@
     slope[...] = jnp.broadcast_to(ratio, (128, TOK)).T
 
 
-def wide_of(ref):
-    return jnp.concatenate([ref[...]] * (LONG // 128), 1)
+def wide_of(ref, width=LONG):
+    return jnp.concatenate([ref[...]] * (width // 128), 1)
 
 
 def grad_kernel(
@@ -312,31 +374,86 @@
         send(chunk).wait()
 
 
-def norm_kernel(
-    local_ref, sums_ref, gate_ref, gain_ref, grad_ref, state_ref, queries_ref, fac_ref,
-    normed_ref, out_ref, dy_ref, dq_ref, inverse, slope,
-):
-    step = pl.program_id(0)
-
-    @pl.when(step == 0)
+def norm_columns(array, chunk):
+    return array.at[:, pl.ds(pl.multiple_of(chunk * NORM, NORM), NORM)]
+
+
+def norm_kernel(part, local_in, gate_in, grad_in, *refs):
+    small_in, refs = refs[:5], refs[5:]
+    dq_in = refs[3]
+    outs, dq_out, refs = refs[-16:-13], refs[-13], refs[-12:]
+    bufs, small_refs, dq_ref, results = refs[0], refs[1:6], refs[6], refs[7]
+    inverse, slope, small, come = refs[8:]
+    sums_ref, gain_ref, state_ref, queries_ref, fac_ref = small_refs
+    first, last = bounds(part, EARLY_CHUNKS, NORM_CHUNKS)
+
+    def fetch(chunk):
+        return [
+            pltpu.make_async_copy(norm_columns(a, chunk), bufs.at[i, chunk], come.at[i, chunk])
+            for i, a in enumerate((local_in, gate_in, grad_in))
+        ]
+
+    def send(chunk):
+        return [
+            pltpu.make_async_copy(results.at[i, chunk], norm_columns(out, chunk), come.at[3 + i, chunk])
+            for i, out in enumerate(outs)
+        ]
+
+    @pl.when(first < last)
     def _():
+        copies = [pltpu.make_async_copy(a, b, small.at[i]) for i, (a, b) in enumerate(zip(small_in, small_refs))]
+        for copy in copies:
+            copy.start()
+
+        @pl.loop(first, last)
+        def _(chunk):
+            for copy in fetch(chunk):
+                copy.start()
+
+        for copy in copies:
+            copy.wait()
+
+        dq_ref[...] = jnp.zeros_like(dq_ref)
+
+        @pl.when(first > 0)
+        def _():
+            earlier = pltpu.make_async_copy(dq_in, dq_ref, small.at[5])
+            earlier.start()
+            earlier.wait()
+
         norm_terms(sums_ref, inverse, slope)
-        dq_ref[...] = jnp.zeros_like(dq_ref)
-
-    gate = gate_ref[...].astype(F32)
-    sig = jax.nn.sigmoid(gate)
-    state = state_of(state_ref)
-    start = expand(fac_ref[...], START, step, LONG)
-    mixed = local_ref[...].astype(F32) + nn(queries_ref[...], state) * start
-    silu = gate * sig
-    gated = mixed * silu
-    gain = wide_of(inverse) * gain_ref[...]
-    normed_ref[...] = (gated * gain).astype(BF16)
-    grad_gated = gain * grad_ref[...].astype(F32) - gated * wide_of(slope)
-    out_ref[...] = (grad_gated * mixed * (sig * (1.0 + gate * (1.0 - sig)))).astype(BF16)
-    dy = grad_gated * silu
-    dy_ref[...] = dy.astype(BF16)
-    dq_ref[...] += nt((dy * start).astype(BF16), state)
+
+        @pl.loop(first, last)
+        def _(chunk):
+            for copy in fetch(chunk):
+                copy.wait()
+            gate = bufs[1, chunk].astype(F32)
+            sig = jax.nn.sigmoid(gate)
+            parts = NORM // SLICE
+            state = jnp.concatenate([state_ref[chunk * parts + i] for i in range(parts)], 1)
+            start = expand(fac_ref[...], START, chunk, NORM)
+            mixed = bufs[0, chunk].astype(F32) + nn(queries_ref[...], state) * start
+            silu = gate * sig
+            gated = mixed * silu
+            gain = wide_of(inverse, NORM) * gain_ref[:, pl.ds(pl.multiple_of(chunk * NORM, NORM), NORM)]
+            results[0, chunk] = (gated * gain).astype(BF16)
+            grad_gated = gain * bufs[2, chunk].astype(F32) - gated * wide_of(slope, NORM)
+            results[1, chunk] = (grad_gated * mixed * (sig * (1.0 + gate * (1.0 - sig)))).astype(BF16)
+            dy = grad_gated * silu
+            results[2, chunk] = dy.astype(BF16)
+            dq_ref[...] += nt((dy * start).astype(BF16), state)
+            for copy in send(chunk):
+                copy.start()
+
+        final = pltpu.make_async_copy(dq_ref, dq_out, small.at[6])
+        final.start()
+
+        @pl.loop(first, last)
+        def _(chunk):
+            for copy in send(chunk):
+                copy.wait()
+
+        final.wait()
 
 
 def back_kernel(
@@ -373,7 +490,7 @@
     below = (dwide[HALF:] * middle[HALF:]).astype(BF16)
     far = nn(off2[...], below) * middle[:HALF]
     doff2[...] += nt(above, below)
-    skip = skip_ref[...] * dwide
+    skip = channel_row(column_of(skip_ref), step) * dwide
     for i in range(BLKS):
         total = skip[blk(i)]
         if i % 2 == 0:
@@ -525,6 +642,25 @@
     )
 
 
+def split_call(kernel, name, here_first, operands, out_shape, scratch, limit, gmacs):
+    def call_part(part, given):
+        return pl.pallas_call(
+            functools.partial(kernel, part),
+            name=name,
+            in_specs=[ANY] * (len(operands) + len(given)),
+            out_specs=[ANY] * len(out_shape),
+            out_shape=out_shape,
+            input_output_aliases={len(operands) + i: i for i in range(len(given))},
+            scratch_shapes=scratch,
+            compiler_params=pltpu.CompilerParams(vmem_limit_bytes=limit << 20),
+            cost_estimate=pl.CostEstimate(flops=int(2e9 * gmacs), bytes_accessed=12 * 2**20, transcendentals=0),
+        )(*operands, *given)
+
+    before = call_part(0, [])
+    here, *before = lax.optimization_barrier((here_first, *before))
+    return here, lambda: call_part(1, before)
+
+
 def exchange(a, axis):
     return lax.all_to_all(a, axis, 0, 0)
 
@@ -532,7 +668,7 @@
 def body(inputs, gate_input, step_size, input_map, output_map, decay_rate, skip_weight, norm_gain, out_grad):
     rate = decay_rate.reshape(1, HEADS)
     gain = norm_gain.reshape(1, COLS)
-    skip = jnp.repeat(skip_weight, P_SIZE).reshape(1, COLS)
+    skip = skip_weight.reshape(1, HEADS)
     tokens = shape(TOK, COLS, dtype=BF16)
     score_scratch = [
         pltpu.VMEM((BLKS, SUB, SUB), F32),
@@ -573,18 +709,33 @@
             dma((CHUNKS,)),
         ],
     )
-    all_ends = exchange(ends, "ctx")
-
-    mixed_local, gated_local, ratio, scaled = call(
+    score_steps = pltpu.VMEM((STEPS, TOK, WIDE), BF16)
+    ends, rest = split_call(
         local_kernel,
         "within_segment",
-        [TOKENS_BY_STEP, TOKENS_BY_STEP, MAP, MAP, FACTORS, COLUMNS, ROWS_BY_STEP, ROW_BY_STEP],
-        [TOKENS_BY_STEP] * 4,
+        ends,
+        hbm(inputs, gate_input, input_map, output_map, factors, columns, rows, skip),
         [in_hbm(TOK, COLS, dtype=BF16)] * 4,
-        score_scratch,
-        steps=STEPS,
-        gmacs=4.0,
-    )(inputs, gate_input, input_map, output_map, factors, columns, rows, skip)
+        [
+            score_steps,
+            score_steps,
+            pltpu.VMEM((TOK, N), BF16),
+            pltpu.VMEM((TOK, N), BF16),
+            pltpu.VMEM((TOK, 2 * SLICE), BF16),
+            pltpu.VMEM((TOK, 128), F32),
+            pltpu.VMEM((STEPS, 2 * HPS, TOK), F32),
+            pltpu.VMEM((1, HEADS), F32),
+            pltpu.VMEM((4, STEPS, TOK, WIDE), BF16),
+            *score_scratch,
+            dma((6,)),
+            dma((2, STEPS)),
+            dma((4, STEPS)),
+        ],
+        40,
+        4.0,
+    )
+    all_ends = exchange(ends, "ctx")
+    mixed_local, gated_local, ratio, scaled = rest()
     all_ends, mixed_local, gated_local, ratio, scaled = lax.optimization_barrier(
         (all_ends, mixed_local, gated_local, ratio, scaled)
     )
@@ -613,22 +764,35 @@
         [pltpu.VMEM((SEGS, N, SLICE), BF16)] + norm_scratch + [dma((CHUNKS,))],
         here=range(6),
     )
-    all_grads = exchange(local_grads, "ctx")
-
-    normed, grad_gate, dy, dq = call(
+    local_grads, rest = split_call(
         norm_kernel,
         "normed_and_gate",
-        [TOKENS_BY_LONG, SUMS, TOKENS_BY_LONG, ROW_BY_LONG, TOKENS_BY_LONG, state_by(LONG), MAP, FACTORS],
-        [TOKENS_BY_LONG, TOKENS_BY_LONG, TOKENS_BY_LONG, MAP],
-        [tokens, tokens, in_hbm(TOK, COLS, dtype=BF16), in_hbm(TOK, N)],
-        norm_scratch,
-        gmacs=2.0,
-    )(*hbm(mixed_local, sums, gate_input, gain, out_grad, state_in, output_map, factors))
+        local_grads,
+        hbm(mixed_local, gate_input, out_grad, sums, gain, state_in, output_map, factors),
+        [in_hbm(TOK, COLS, dtype=BF16)] * 3 + [in_hbm(TOK, N)],
+        [
+            pltpu.VMEM((3, NORM_CHUNKS, TOK, NORM), BF16),
+            pltpu.VMEM((PARTS, 2, TOK), F32),
+            pltpu.VMEM((1, COLS), F32),
+            pltpu.VMEM((SEGS, N, SLICE), BF16),
+            pltpu.VMEM((TOK, N), BF16),
+            pltpu.VMEM((TOK, 2 * SLICE), BF16),
+            pltpu.VMEM((TOK, N), F32),
+            pltpu.VMEM((3, NORM_CHUNKS, TOK, NORM), BF16),
+            *norm_scratch,
+            dma((7,)),
+            dma((6, NORM_CHUNKS)),
+        ],
+        48,
+        2.0,
+    )
+    all_grads = exchange(local_grads, "ctx")
+    normed, grad_gate, dy, dq = rest()
 
     dx, dkeys, dqueries = call(
         back_kernel,
         "within_segment_back",
-        [TOKENS_BY_STEP, TOKENS_BY_STEP, MAP, MAP, MAP, FACTORS, COLUMNS, ROWS_BY_STEP, ROW_BY_STEP],
+        [TOKENS_BY_STEP, TOKENS_BY_STEP, MAP, MAP, MAP, FACTORS, COLUMNS, ROWS_BY_STEP, whole((1, HEADS))],
         [TOKENS_BY_STEP, MAP, MAP],
         [in_hbm(TOK, COLS, dtype=BF16), in_hbm(TOK, N), shape(TOK, N, dtype=BF16)],
         score_scratch

time: 116 us -> 111 us (0.957)
  waiting for transfers between devices: 21.4 us -> 15.6 us
  Pallas kernels: 46.8 us -> 52 us
  blocking collectives: 30 us -> 25.7 us
    all_to_all x3, waiting for transfers between devices: 21.4 us -> 15.6 us  [exchange(): return lax.all_to_all(a, axis, 0, 0)]
    pallas_call x2 -> x4, Pallas kernels: 19.7 us -> 25.4 us  [call_part(): pl.pallas_call(functools.partial(kernel, part), name=name, in_specs=[ANY]...]
    all_to_all x2, blocking collectives: 30 us -> 25.7 us  [exchange(): return lax.all_to_all(a, axis, 0, 0)]
  transfers between devices with their start and end apart: 3 -> 3, of which waited for: 3 -> 3; matrix products, arithmetic and copies ran while one was open for 1% -> 0% of each run, Pallas kernels for 27% -> 25%
where the time goes in v4:
time: 111 us; the launch traced here: 110 us
  Pallas kernels  52 us (47%)
  blocking collectives  25.7 us (23%)
  waiting for transfers between devices  15.6 us (14%)
  starting transfers between devices  15.5 us (14%)
    all_to_all x2, blocking collectives, exchange(): return lax.all_to_all(a, axis, 0, 0)  25.7 us
    pallas_call x4, Pallas kernels, call_part(): pl.pallas_call(functools.partial(kernel, part), name=name, in_specs=[ANY]...  25.4 us
    all_to_all x3, waiting for transfers between devices, exchange(): return lax.all_to_all(a, axis, 0, 0)  15.6 us
    all_to_all x3, starting transfers between devices, exchange(): return lax.all_to_all(a, axis, 0, 0)  15.5 us
    pallas_call x6, Pallas kernels, manual_call(): pl.pallas_call(kernel, name=name, in_specs=[HERE if i in here else ANY fo...  15.2 us
    pallas_call x1, Pallas kernels, body(): call(back_kernel, 'within_segment_back', [TOKENS_BY_STEP, TOKENS_BY_STEP,...  11.3 us
  transfers between devices with their start and end apart: 3, of which 3 were waited for; matrix products, arithmetic and copies ran while one was open for 0% of the time, Pallas kernels for 25%

profile of v4, /device:TPU:0, one launch (start us, length us, event | category | flops | bytes accessed | tf_op | source)
XLA Modules:
  0.0 109.9 jit_solution(2140256691274236923)
XLA Ops:
  0.6 3.9 %segment_ends.1 = (bf16[16,272,128]{2,1,0:T(8,128)(2,1)}, bf16[512,256]{1,0:T(8,128)(2,1)}, f32[512,128]{1,0:T(8,128)}, f32[8,8,512]{2,1,0:T(8,128)}) custom-call(f32[32,512]{1,0:T(8,128)} %step_in.1, f32[1,32]{1,0:T(1,128)} %bitcast.7, bf16[512,2048]{1,0:T(8,128)(2,1)} %x_ref.1, bf16[512,256]{1,0:T(8,128)(2,1)} %keys_in.3), custom_call_target="tpu_custom_call" | custom-call | flops 1073741824 | bytes 8388608 | tf_op jit(solution)/shard_map/segment_ends/pallas_call | solution.py:619
  4.6 4.7 %within_segment.2 = (bf16[512,2048]{1,0:T(8,128)(2,1)}, bf16[512,2048]{1,0:T(8,128)(2,1)}, bf16[512,2048]{1,0:T(8,128)(2,1)}, bf16[512,2048]{1,0:T(8,128)(2,1)}) custom-call(bf16[512,2048]{1,0:T(8,128)(2,1)} %x_ref.1, bf16[512,2048]{1,0:T(8,128)(2,1)} %gate_in.7, bf16[512,256]{1,0:T(8,128)(2,1)} %keys_in.3, bf16[512,256]{1,0:T(8,128)(2,1)} %queries_ref.5, ...), custom_call_target="tpu_custom_call" | custom-call | flops 8000000000 | bytes 12582912 | tf_op jit(solution)/shard_map/within_segment/pallas_call | solution.py:647
  9.3 8.0 %all-to-all-start = ((bf16[16,272,128]{2,1,0:T(8,128)(2,1)}), bf16[16,272,128]{2,1,0:T(8,128)(2,1)S(1)}, u32[]{:S(2)}, u32[]{:S(2)}) async-start(bf16[16,272,128]{2,1,0:T(8,128)(2,1)} %get-tuple-element.55), calls=%async_computation | async-start | bytes 2228224 | tf_op jit(solution)/shard_map/all_to_all | solution.py:665
  17.2 7.9 %within_segment.3 = (bf16[512,2048]{1,0:T(8,128)(2,1)}, bf16[512,2048]{1,0:T(8,128)(2,1)}, bf16[512,2048]{1,0:T(8,128)(2,1)}, bf16[512,2048]{1,0:T(8,128)(2,1)}) custom-call(bf16[512,2048]{1,0:T(8,128)(2,1)} %x_ref.1, bf16[512,2048]{1,0:T(8,128)(2,1)} %gate_in.7, ...), custom_call_target="tpu_custom_call", output_to_operand_aliasing={{0}: (8, {}), {1}: (9, {}), {2}: (10, {}), {3}: (11, {})} | custom-call | flops 8000000000 | bytes 12582912 | tf_op jit(solution)/shard_map/within_segment/pallas_call | solution.py:647
  25.1 6.8 %all-to-all-done.in_ref.ends_in = bf16[16,272,128]{2,1,0:T(8,128)(2,1)S(1)} async-done(((bf16[16,272,128]{2,1,0:T(8,128)(2,1)}), bf16[16,272,128]{2,1,0:T(8,128)(2,1)S(1)}, u32[]{:S(2)}, u32[]{:S(2)}) %all-to-all-start) | async-done | bytes 1114144 | tf_op jit(solution)/shard_map/all_to_all | solution.py:665
  31.9 0.0 copy-start.4
  31.9 0.0 copy-start.1
  31.9 0.0 copy-start.3
  31.9 0.0 copy-start.6
  31.9 0.0 copy-start.10
  31.9 0.2 forward_scan.1
  32.2 15.9 %all_to_all.25.state_ref.refs_2_ = bf16[16,256,128]{2,1,0:T(8,128)(2,1)S(1)} all-to-all(bf16[16,256,128]{2,1,0:T(8,128)(2,1)S(1)} %forward_scan.1), channel_id=1, replica_groups=mesh['ctx'=16,'tp'=8] {'ctx'}, dimensions={0} | all-to-all | bytes 2097152 | tf_op jit(solution)/shard_map/all_to_all | solution.py:665
  48.1 0.0 copy-done.4
  48.1 0.0 copy-start.2
  48.1 0.0 copy-done.1
  48.1 0.0 copy-done.3
  48.1 0.0 copy-done.6
  48.1 0.0 copy-done.10
  48.1 2.5 %carry_and_gate.1 = (bf16[512,2048]{1,0:T(8,128)(2,1)S(1)}, f32[8,2,512]{2,1,0:T(2,128)S(1)}) custom-call(bf16[512,2048]{1,0:T(8,128)(2,1)S(1)} %copy-done.3, bf16[16,256,128]{2,1,0:T(8,128)(2,1)S(1)} %all_to_all.25.state_ref.refs_2_, bf16[512,256]{1,0:T(8,128)(2,1)S(1)} %copy-done.6, bf16[512,2048]{1,0:T(8,128)(2,1)S(1)} %copy-done.1, ...), custom_call_target="tpu_custom_call" | custom-call | flops 1073741824 | bytes 8388608 | tf_op jit(solution)/shard_map/carry_and_gate/pallas_call | solution.py:619
  50.6 0.0 copy-done.2
  50.6 9.8 %all_to_all.26.sums_ref.refs_0_ = f32[8,2,512]{2,1,0:T(2,128)} all-to-all(f32[8,2,512]{2,1,0:T(2,128)S(1)} %get-tuple-element.68), channel_id=1, replica_groups=mesh['ctx'=16,'tp'=8] {'tp'}, dimensions={0} | all-to-all | bytes 65536 | tf_op jit(solution)/shard_map/all_to_all | solution.py:665
  60.4 0.0 copy-start
  60.4 0.0 copy-start.7
  60.4 0.0 copy-start.9
  60.4 0.0 copy-start.11
  60.5 4.6 %normed_and_gate.2 = (bf16[512,2048]{1,0:T(8,128)(2,1)}, bf16[512,2048]{1,0:T(8,128)(2,1)}, bf16[512,2048]{1,0:T(8,128)(2,1)}, f32[512,256]{1,0:T(8,128)}) custom-call(bf16[512,2048]{1,0:T(8,128)(2,1)} %get-tuple-element.64.local_in, bf16[512,2048]{1,0:T(8,128)(2,1)} %gate_in.7, bf16[512,2048]{1,0:T(8,128)(2,1)} %grad_in.5, ...), custom_call_target="tpu_custom_call" | custom-call | flops 4000000000 | bytes 12582912 | tf_op jit(solution)/shard_map/normed_and_gate/pallas_call | solution.py:647
  65.1 0.0 copy-done
  65.1 0.0 copy-done.7
  65.1 0.0 copy-done.9
  65.1 0.0 copy-done.11
  65.1 2.5 %local_grads.1 = bf16[16,256,128]{2,1,0:T(8,128)(2,1)} custom-call(bf16[512,2048]{1,0:T(8,128)(2,1)S(1)} %get-tuple-element.69.gated_ref, f32[8,2,512]{2,1,0:T(2,128)S(1)} %copy-done.9, bf16[512,256]{1,0:T(8,128)(2,1)S(1)} %copy-done.7, bf16[512,2048]{1,0:T(8,128)(2,1)S(1)} %copy-done.1, f32[1,2048]{1,0:T(1,128)S(1)} %bitcast.6, bf16[512,2048]{1,0:T(8,128)(2,1)S(1)} %copy-done), custom_call_target="tpu_custom_call" | custom-call | flops 1073741824 | bytes 8388608 | tf_op jit(solution)/shard_map/local_grads/pallas_call | solution.py:619
  67.6 3.7 %all-to-all-start.3 = ((bf16[16,256,128]{2,1,0:T(8,128)(2,1)}), bf16[16,256,128]{2,1,0:T(8,128)(2,1)S(1)}, u32[]{:S(2)}, u32[]{:S(2)}) async-start(bf16[16,256,128]{2,1,0:T(8,128)(2,1)} %local_grads.1), calls=%async_computation.3 | async-start | bytes 2097152 | tf_op jit(solution)/shard_map/all_to_all | solution.py:665
  71.3 0.0 copy-start.5
  71.3 8.3 %normed_and_gate.3 = (bf16[512,2048]{1,0:T(8,128)(2,1)}, bf16[512,2048]{1,0:T(8,128)(2,1)}, bf16[512,2048]{1,0:T(8,128)(2,1)}, f32[512,256]{1,0:T(8,128)}) custom-call(bf16[512,2048]{1,0:T(8,128)(2,1)} %get-tuple-element.64.local_in, bf16[512,2048]{1,0:T(8,128)(2,1)} %gate_in.7, ...), custom_call_target="tpu_custom_call", output_to_operand_aliasing={{0}: (8, {}), {1}: (9, {}), {2}: (10, {}), {3}: (11, {})} | custom-call | flops 4000000000 | bytes 12582912 | tf_op jit(solution)/shard_map/normed_and_gate/pallas_call | solution.py:647
  79.6 0.0 copy-start.8
  79.6 0.0 copy-start.12
  79.6 0.0 copy-start.13
  79.6 6.4 %all-to-all-done.3.in_ref = bf16[16,256,128]{2,1,0:T(8,128)(2,1)S(1)} async-done(((bf16[16,256,128]{2,1,0:T(8,128)(2,1)}), bf16[16,256,128]{2,1,0:T(8,128)(2,1)S(1)}, u32[]{:S(2)}, u32[]{:S(2)}) %all-to-all-start.3) | async-done | bytes 1048608 | tf_op jit(solution)/shard_map/all_to_all | solution.py:665
  86.0 0.0 copy-done.5
  86.0 1.3 %backward_scan.1 = bf16[16,256,128]{2,1,0:T(8,128)(2,1)} custom-call(bf16[16,256,128]{2,1,0:T(8,128)(2,1)S(1)} %all-to-all-done.3.in_ref, bf16[16,272,128]{2,1,0:T(8,128)(2,1)S(1)} %copy-done.5), custom_call_target="tpu_custom_call" | custom-call | flops 1073741824 | bytes 8388608 | tf_op jit(solution)/shard_map/backward_scan/pallas_call | solution.py:619
  87.3 3.8 %all-to-all-start.4 = ((bf16[16,256,128]{2,1,0:T(8,128)(2,1)}), bf16[16,256,128]{2,1,0:T(8,128)(2,1)S(1)}, u32[]{:S(2)}, u32[]{:S(2)}) async-start(bf16[16,256,128]{2,1,0:T(8,128)(2,1)} %backward_scan.1), calls=%async_computation.4 | async-start | bytes 2097152 | tf_op jit(solution)/shard_map/all_to_all | solution.py:665
  91.1 0.0 copy-done.8
  91.2 0.0 copy-done.12
  91.2 0.0 copy-done.13
  91.2 11.3 %within_segment_back.1 = (bf16[512,2048]{1,0:T(8,128)(2,1)}, f32[512,256]{1,0:T(8,128)}, bf16[512,256]{1,0:T(8,128)(2,1)}) custom-call(bf16[512,2048]{1,0:T(8,128)(2,1)} %x_ref.1, bf16[512,2048]{1,0:T(8,128)(2,1)} %get-tuple-element.79.dy_ref, f32[512,256]{1,0:T(8,128)} %get-tuple-element.80.dq_ref, bf16[512,256]{1,0:T(8,128)(2,1)} %keys_in.3, ...), custom_call_target="tpu_custom_call" | custom-call | flops 12000000000 | bytes 8388608 | tf_op jit(solution)/shard_map/within_segment_back/pallas_call | solution.py:792
  102.5 2.5 %all-to-all-done.4.grad_ref = bf16[16,256,128]{2,1,0:T(8,128)(2,1)S(1)} async-done(((bf16[16,256,128]{2,1,0:T(8,128)(2,1)}), bf16[16,256,128]{2,1,0:T(8,128)(2,1)S(1)}, u32[]{:S(2)}, u32[]{:S(2)}) %all-to-all-start.4) | async-done | bytes 1048608 | tf_op jit(solution)/shard_map/all_to_all | solution.py:665
  105.0 4.8 %final_grads.1 = (bf16[512,2048]{1,0:T(8,128)(2,1)}, bf16[512,256]{1,0:T(8,128)(2,1)}) custom-call(bf16[512,2048]{1,0:T(8,128)(2,1)} %get-tuple-element.81.dx_in, bf16[512,2048]{1,0:T(8,128)(2,1)} %get-tuple-element.82.scaled_in, bf16[16,256,128]{2,1,0:T(8,128)(2,1)S(1)} %all-to-all-done.4.grad_ref, bf16[512,256]{1,0:T(8,128)(2,1)} %keys_in.3, ...), custom_call_target="tpu_custom_call" | custom-call | flops 1073741824 | bytes 8388608 | tf_op jit(solution)/shard_map/final_grads/pallas_call | solution.py:619
Async XLA Ops:
  9.3 22.7 %all-to-all-start = ((bf16[16,272,128]{2,1,0:T(8,128)(2,1)}), bf16[16,272,128]{2,1,0:T(8,128)(2,1)S(1)}, u32[]{:S(2)}, u32[]{:S(2)}) async-start(bf16[16,272,128]{2,1,0:T(8,128)(2,1)} %get-tuple-element.55), calls=%async_computation | async-start | bytes 2228224 | tf_op jit(solution)/shard_map/all_to_all | solution.py:665
  31.9 16.2 %copy-start.4 = (bf16[16,272,128]{2,1,0:T(8,128)(2,1)}, bf16[16,272,128]{2,1,0:T(8,128)(2,1)S(1)}, u32[]{:S(2)}) copy-start(bf16[16,272,128]{2,1,0:T(8,128)(2,1)S(1)} %all-to-all-done.in_ref.ends_in) | copy-start | bytes 3342340
  31.9 16.2 %copy-start.1 = (bf16[512,2048]{1,0:T(8,128)(2,1)S(1)}, bf16[512,2048]{1,0:T(8,128)(2,1)}, u32[]{:S(2)}) copy-start(bf16[512,2048]{1,0:T(8,128)(2,1)} %get-tuple-element.67.ratio_ref) | copy-start | bytes 6291460
  31.9 16.2 %copy-start.3 = (bf16[512,2048]{1,0:T(8,128)(2,1)S(1)}, bf16[512,2048]{1,0:T(8,128)(2,1)}, u32[]{:S(2)}) copy-start(bf16[512,2048]{1,0:T(8,128)(2,1)} %get-tuple-element.65.local_ref) | copy-start | bytes 6291460
  31.9 16.2 %copy-start.6 = (bf16[512,256]{1,0:T(8,128)(2,1)S(1)}, bf16[512,256]{1,0:T(8,128)(2,1)}, u32[]{:S(2)}) copy-start(bf16[512,256]{1,0:T(8,128)(2,1)} %queries_ref.5) | copy-start | bytes 786436
  31.9 16.2 %copy-start.10 = (f32[2048]{0:T(1024)S(1)}, f32[2048]{0:T(1024)}, u32[]{:S(2)}) copy-start(f32[2048]{0:T(1024)} %param.16) | copy-start | bytes 24580
  48.1 2.5 %copy-start.2 = (bf16[16,256,128]{2,1,0:T(8,128)(2,1)}, bf16[16,256,128]{2,1,0:T(8,128)(2,1)S(1)}, u32[]{:S(2)}) copy-start(bf16[16,256,128]{2,1,0:T(8,128)(2,1)S(1)} %all_to_all.25.state_ref.refs_2_) | copy-start | bytes 3145732
  60.4 4.6 %copy-start = (bf16[512,2048]{1,0:T(8,128)(2,1)S(1)}, bf16[512,2048]{1,0:T(8,128)(2,1)}, u32[]{:S(2)}) copy-start(bf16[512,2048]{1,0:T(8,128)(2,1)} %grad_in.5) | copy-start | bytes 6291460
  60.4 4.6 %copy-start.7 = (bf16[512,256]{1,0:T(8,128)(2,1)S(1)}, bf16[512,256]{1,0:T(8,128)(2,1)}, u32[]{:S(2)}) copy-start(bf16[512,256]{1,0:T(8,128)(2,1)} %queries_ref.5) | copy-start | bytes 786436
  60.4 4.6 %copy-start.9 = (f32[8,2,512]{2,1,0:T(2,128)S(1)}, f32[8,2,512]{2,1,0:T(2,128)}, u32[]{:S(2)}) copy-start(f32[8,2,512]{2,1,0:T(2,128)} %all_to_all.26.sums_ref.refs_0_) | copy-start | bytes 98308
  60.4 4.6 %copy-start.11 = (f32[2048]{0:T(1024)S(1)}, f32[2048]{0:T(1024)}, u32[]{:S(2)}) copy-start(f32[2048]{0:T(1024)} %param.16) | copy-start | bytes 24580
  67.6 18.4 %all-to-all-start.3 = ((bf16[16,256,128]{2,1,0:T(8,128)(2,1)}), bf16[16,256,128]{2,1,0:T(8,128)(2,1)S(1)}, u32[]{:S(2)}, u32[]{:S(2)}) async-start(bf16[16,256,128]{2,1,0:T(8,128)(2,1)} %local_grads.1), calls=%async_computation.3 | async-start | bytes 2097152 | tf_op jit(solution)/shard_map/all_to_all | solution.py:665
  71.3 14.7 %copy-start.5 = (bf16[16,272,128]{2,1,0:T(8,128)(2,1)S(1)}, bf16[16,272,128]{2,1,0:T(8,128)(2,1)}, u32[]{:S(2)}) copy-start(bf16[16,272,128]{2,1,0:T(8,128)(2,1)} %copy-done.4) | copy-start | bytes 3342340
  79.6 11.6 %copy-start.8 = (bf16[512,256]{1,0:T(8,128)(2,1)S(1)}, bf16[512,256]{1,0:T(8,128)(2,1)}, u32[]{:S(2)}) copy-start(bf16[512,256]{1,0:T(8,128)(2,1)} %get-tuple-element.48.refs_2_.refs_4_.fac_ref.fac_in) | copy-start | bytes 786436
  79.6 11.6 %copy-start.12 = (f32[512,128]{1,0:T(8,128)S(1)}, f32[512,128]{1,0:T(8,128)}, u32[]{:S(2)}) copy-start(f32[512,128]{1,0:T(8,128)} %get-tuple-element.49.refs_3_.col_ref) | copy-start | bytes 786436
  79.6 11.6 %copy-start.13 = (f32[8,8,512]{2,1,0:T(8,128)S(1)}, f32[8,8,512]{2,1,0:T(8,128)}, u32[]{:S(2)}) copy-start(f32[8,8,512]{2,1,0:T(8,128)} %get-tuple-element.50.refs_4_.row_ref) | copy-start | bytes 393220
  87.3 17.7 %all-to-all-start.4 = ((bf16[16,256,128]{2,1,0:T(8,128)(2,1)}), bf16[16,256,128]{2,1,0:T(8,128)(2,1)S(1)}, u32[]{:S(2)}, u32[]{:S(2)}) async-start(bf16[16,256,128]{2,1,0:T(8,128)(2,1)} %backward_scan.1), calls=%async_computation.4 | async-start | bytes 2097152 | tf_op jit(solution)/shard_map/all_to_all | solution.py:665

commit v5 on v4

--- a/solution.py
+++ b/solution.py
@@ -20,7 +20,7 @@
 COLS = HEADS * P_SIZE
 SLICE = 128
 TAIL = 16
-WIDE = 256
+WIDE = 512
 LONG = 1024
 STEPS = COLS // WIDE
 CHUNKS = COLS // LONG
@@ -28,7 +28,7 @@
 VMEM_MIB = 36
 NORM = 512
 NORM_CHUNKS = COLS // NORM
-EARLY_STEPS = 2
+EARLY_STEPS = 1
 EARLY_CHUNKS = 1
 SUB = 128
 BLKS = TOK // SUB

time: 111 us -> 111 us (level)
  waiting for transfers between devices: 15.6 us -> 17 us
  Pallas kernels: 52 us -> 50.7 us
    pallas_call x1, Pallas kernels: 11.3 us -> 9.6 us  [body(): call(back_kernel, 'within_segment_back', [TOKENS_BY_STEP, TOKENS_BY_STEP,...]
    all_to_all x3, waiting for transfers between devices: 15.6 us -> 17 us  [exchange(): return lax.all_to_all(a, axis, 0, 0)]
  transfers between devices with their start and end apart: 3 -> 3, of which waited for: 3 -> 3; matrix products, arithmetic and copies ran while one was open for 0% -> 0% of each run, Pallas kernels for 25% -> 24%
where the time goes in v5:
time: 111 us; the launch traced here: 110 us
  Pallas kernels  50.7 us (46%)
  blocking collectives  26 us (23%)
  waiting for transfers between devices  17 us (15%)
  starting transfers between devices  15.5 us (14%)
    all_to_all x2, blocking collectives, exchange(): return lax.all_to_all(a, axis, 0, 0)  26 us
    pallas_call x4, Pallas kernels, call_part(): pl.pallas_call(functools.partial(kernel, part), name=name, in_specs=[ANY]...  25.8 us
    all_to_all x3, waiting for transfers between devices, exchange(): return lax.all_to_all(a, axis, 0, 0)  17 us
    all_to_all x3, starting transfers between devices, exchange(): return lax.all_to_all(a, axis, 0, 0)  15.5 us
    pallas_call x6, Pallas kernels, manual_call(): pl.pallas_call(kernel, name=name, in_specs=[HERE if i in here else ANY fo...  15.2 us
    pallas_call x1, Pallas kernels, body(): call(back_kernel, 'within_segment_back', [TOKENS_BY_STEP, TOKENS_BY_STEP,...  9.6 us
  transfers between devices with their start and end apart: 3, of which 3 were waited for; matrix products, arithmetic and copies ran while one was open for 0% of the time, Pallas kernels for 24%

profile of v5, /device:TPU:0, one launch (start us, length us, event | category | flops | bytes accessed | tf_op | source)
XLA Modules:
  0.0 110.2 jit_solution(17095827572491573714)
XLA Ops:
  0.6 3.9 %segment_ends.1 = (bf16[16,272,128]{2,1,0:T(8,128)(2,1)}, bf16[512,256]{1,0:T(8,128)(2,1)}, f32[512,128]{1,0:T(8,128)}, f32[4,16,512]{2,1,0:T(8,128)}) custom-call(f32[32,512]{1,0:T(8,128)} %step_in.1, f32[1,32]{1,0:T(1,128)} %bitcast.7, bf16[512,2048]{1,0:T(8,128)(2,1)} %x_ref.1, bf16[512,256]{1,0:T(8,128)(2,1)} %keys_in.3), custom_call_target="tpu_custom_call" | custom-call | flops 1073741824 | bytes 8388608 | tf_op jit(solution)/shard_map/segment_ends/pallas_call | solution.py:619
  4.6 4.9 %within_segment.2 = (bf16[512,2048]{1,0:T(8,128)(2,1)}, bf16[512,2048]{1,0:T(8,128)(2,1)}, bf16[512,2048]{1,0:T(8,128)(2,1)}, bf16[512,2048]{1,0:T(8,128)(2,1)}) custom-call(bf16[512,2048]{1,0:T(8,128)(2,1)} %x_ref.1, bf16[512,2048]{1,0:T(8,128)(2,1)} %gate_in.7, bf16[512,256]{1,0:T(8,128)(2,1)} %keys_in.3, bf16[512,256]{1,0:T(8,128)(2,1)} %queries_ref.5, ...), custom_call_target="tpu_custom_call" | custom-call | flops 8000000000 | bytes 12582912 | tf_op jit(solution)/shard_map/within_segment/pallas_call | solution.py:647
  9.4 8.0 %all-to-all-start = ((bf16[16,272,128]{2,1,0:T(8,128)(2,1)}), bf16[16,272,128]{2,1,0:T(8,128)(2,1)S(1)}, u32[]{:S(2)}, u32[]{:S(2)}) async-start(bf16[16,272,128]{2,1,0:T(8,128)(2,1)} %get-tuple-element.55), calls=%async_computation | async-start | bytes 2228224 | tf_op jit(solution)/shard_map/all_to_all | solution.py:665
  17.4 8.1 %within_segment.3 = (bf16[512,2048]{1,0:T(8,128)(2,1)}, bf16[512,2048]{1,0:T(8,128)(2,1)}, bf16[512,2048]{1,0:T(8,128)(2,1)}, bf16[512,2048]{1,0:T(8,128)(2,1)}) custom-call(bf16[512,2048]{1,0:T(8,128)(2,1)} %x_ref.1, bf16[512,2048]{1,0:T(8,128)(2,1)} %gate_in.7, ...), custom_call_target="tpu_custom_call", output_to_operand_aliasing={{0}: (8, {}), {1}: (9, {}), {2}: (10, {}), {3}: (11, {})} | custom-call | flops 8000000000 | bytes 12582912 | tf_op jit(solution)/shard_map/within_segment/pallas_call | solution.py:647
  25.5 6.2 %all-to-all-done.in_ref.ends_in = bf16[16,272,128]{2,1,0:T(8,128)(2,1)S(1)} async-done(((bf16[16,272,128]{2,1,0:T(8,128)(2,1)}), bf16[16,272,128]{2,1,0:T(8,128)(2,1)S(1)}, u32[]{:S(2)}, u32[]{:S(2)}) %all-to-all-start) | async-done | bytes 1114144 | tf_op jit(solution)/shard_map/all_to_all | solution.py:665
  31.7 0.0 copy-start.4
  31.7 0.0 copy-start.1
  31.7 0.0 copy-start.3
  31.7 0.0 copy-start.6
  31.7 0.0 copy-start.10
  31.7 0.2 forward_scan.1
  32.0 16.2 %all_to_all.25.state_ref.refs_2_ = bf16[16,256,128]{2,1,0:T(8,128)(2,1)S(1)} all-to-all(bf16[16,256,128]{2,1,0:T(8,128)(2,1)S(1)} %forward_scan.1), channel_id=1, replica_groups=mesh['ctx'=16,'tp'=8] {'ctx'}, dimensions={0} | all-to-all | bytes 2097152 | tf_op jit(solution)/shard_map/all_to_all | solution.py:665
  48.2 0.0 copy-done.4
  48.2 0.0 copy-start.2
  48.2 0.0 copy-done.1
  48.2 0.0 copy-done.3
  48.2 0.0 copy-done.6
  48.2 0.0 copy-done.10
  48.2 2.5 %carry_and_gate.1 = (bf16[512,2048]{1,0:T(8,128)(2,1)S(1)}, f32[8,2,512]{2,1,0:T(2,128)S(1)}) custom-call(bf16[512,2048]{1,0:T(8,128)(2,1)S(1)} %copy-done.3, bf16[16,256,128]{2,1,0:T(8,128)(2,1)S(1)} %all_to_all.25.state_ref.refs_2_, bf16[512,256]{1,0:T(8,128)(2,1)S(1)} %copy-done.6, bf16[512,2048]{1,0:T(8,128)(2,1)S(1)} %copy-done.1, ...), custom_call_target="tpu_custom_call" | custom-call | flops 1073741824 | bytes 8388608 | tf_op jit(solution)/shard_map/carry_and_gate/pallas_call | solution.py:619
  50.7 0.0 copy-done.2
  50.7 9.8 %all_to_all.26.sums_ref.refs_0_ = f32[8,2,512]{2,1,0:T(2,128)} all-to-all(f32[8,2,512]{2,1,0:T(2,128)S(1)} %get-tuple-element.68), channel_id=1, replica_groups=mesh['ctx'=16,'tp'=8] {'tp'}, dimensions={0} | all-to-all | bytes 65536 | tf_op jit(solution)/shard_map/all_to_all | solution.py:665
  60.6 0.0 copy-start
  60.6 0.0 copy-start.7
  60.6 0.0 copy-start.9
  60.6 0.0 copy-start.11
  60.6 4.6 %normed_and_gate.2 = (bf16[512,2048]{1,0:T(8,128)(2,1)}, bf16[512,2048]{1,0:T(8,128)(2,1)}, bf16[512,2048]{1,0:T(8,128)(2,1)}, f32[512,256]{1,0:T(8,128)}) custom-call(bf16[512,2048]{1,0:T(8,128)(2,1)} %get-tuple-element.64.local_in, bf16[512,2048]{1,0:T(8,128)(2,1)} %gate_in.7, bf16[512,2048]{1,0:T(8,128)(2,1)} %grad_in.5, ...), custom_call_target="tpu_custom_call" | custom-call | flops 4000000000 | bytes 12582912 | tf_op jit(solution)/shard_map/normed_and_gate/pallas_call | solution.py:647
  65.2 0.0 copy-done
  65.2 0.0 copy-done.7
  65.2 0.0 copy-done.9
  65.2 0.0 copy-done.11
  65.2 2.5 %local_grads.1 = bf16[16,256,128]{2,1,0:T(8,128)(2,1)} custom-call(bf16[512,2048]{1,0:T(8,128)(2,1)S(1)} %get-tuple-element.69.gated_ref, f32[8,2,512]{2,1,0:T(2,128)S(1)} %copy-done.9, bf16[512,256]{1,0:T(8,128)(2,1)S(1)} %copy-done.7, bf16[512,2048]{1,0:T(8,128)(2,1)S(1)} %copy-done.1, f32[1,2048]{1,0:T(1,128)S(1)} %bitcast.6, bf16[512,2048]{1,0:T(8,128)(2,1)S(1)} %copy-done), custom_call_target="tpu_custom_call" | custom-call | flops 1073741824 | bytes 8388608 | tf_op jit(solution)/shard_map/local_grads/pallas_call | solution.py:619
  67.7 3.7 %all-to-all-start.3 = ((bf16[16,256,128]{2,1,0:T(8,128)(2,1)}), bf16[16,256,128]{2,1,0:T(8,128)(2,1)S(1)}, u32[]{:S(2)}, u32[]{:S(2)}) async-start(bf16[16,256,128]{2,1,0:T(8,128)(2,1)} %local_grads.1), calls=%async_computation.3 | async-start | bytes 2097152 | tf_op jit(solution)/shard_map/all_to_all | solution.py:665
  71.4 0.0 copy-start.5
  71.4 8.3 %normed_and_gate.3 = (bf16[512,2048]{1,0:T(8,128)(2,1)}, bf16[512,2048]{1,0:T(8,128)(2,1)}, bf16[512,2048]{1,0:T(8,128)(2,1)}, f32[512,256]{1,0:T(8,128)}) custom-call(bf16[512,2048]{1,0:T(8,128)(2,1)} %get-tuple-element.64.local_in, bf16[512,2048]{1,0:T(8,128)(2,1)} %gate_in.7, ...), custom_call_target="tpu_custom_call", output_to_operand_aliasing={{0}: (8, {}), {1}: (9, {}), {2}: (10, {}), {3}: (11, {})} | custom-call | flops 4000000000 | bytes 12582912 | tf_op jit(solution)/shard_map/normed_and_gate/pallas_call | solution.py:647
  79.7 0.0 copy-start.8
  79.7 0.0 copy-start.12
  79.7 0.0 copy-start.13
  79.7 6.4 %all-to-all-done.3.in_ref = bf16[16,256,128]{2,1,0:T(8,128)(2,1)S(1)} async-done(((bf16[16,256,128]{2,1,0:T(8,128)(2,1)}), bf16[16,256,128]{2,1,0:T(8,128)(2,1)S(1)}, u32[]{:S(2)}, u32[]{:S(2)}) %all-to-all-start.3) | async-done | bytes 1048608 | tf_op jit(solution)/shard_map/all_to_all | solution.py:665
  86.1 0.0 copy-done.5
  86.1 1.3 %backward_scan.1 = bf16[16,256,128]{2,1,0:T(8,128)(2,1)} custom-call(bf16[16,256,128]{2,1,0:T(8,128)(2,1)S(1)} %all-to-all-done.3.in_ref, bf16[16,272,128]{2,1,0:T(8,128)(2,1)S(1)} %copy-done.5), custom_call_target="tpu_custom_call" | custom-call | flops 1073741824 | bytes 8388608 | tf_op jit(solution)/shard_map/backward_scan/pallas_call | solution.py:619
  87.4 3.8 %all-to-all-start.4 = ((bf16[16,256,128]{2,1,0:T(8,128)(2,1)}), bf16[16,256,128]{2,1,0:T(8,128)(2,1)S(1)}, u32[]{:S(2)}, u32[]{:S(2)}) async-start(bf16[16,256,128]{2,1,0:T(8,128)(2,1)} %backward_scan.1), calls=%async_computation.4 | async-start | bytes 2097152 | tf_op jit(solution)/shard_map/all_to_all | solution.py:665
  91.3 0.0 copy-done.8
  91.3 0.0 copy-done.12
  91.3 0.0 copy-done.13
  91.3 9.6 %within_segment_back.1 = (bf16[512,2048]{1,0:T(8,128)(2,1)}, f32[512,256]{1,0:T(8,128)}, bf16[512,256]{1,0:T(8,128)(2,1)}) custom-call(bf16[512,2048]{1,0:T(8,128)(2,1)} %x_ref.1, bf16[512,2048]{1,0:T(8,128)(2,1)} %get-tuple-element.79.dy_ref, f32[512,256]{1,0:T(8,128)} %get-tuple-element.80.dq_ref, bf16[512,256]{1,0:T(8,128)(2,1)} %keys_in.3, ...), custom_call_target="tpu_custom_call" | custom-call | flops 12000000000 | bytes 8388608 | tf_op jit(solution)/shard_map/within_segment_back/pallas_call | solution.py:792
  100.9 4.4 %all-to-all-done.4.grad_ref = bf16[16,256,128]{2,1,0:T(8,128)(2,1)S(1)} async-done(((bf16[16,256,128]{2,1,0:T(8,128)(2,1)}), bf16[16,256,128]{2,1,0:T(8,128)(2,1)S(1)}, u32[]{:S(2)}, u32[]{:S(2)}) %all-to-all-start.4) | async-done | bytes 1048608 | tf_op jit(solution)/shard_map/all_to_all | solution.py:665
  105.3 4.8 %final_grads.1 = (bf16[512,2048]{1,0:T(8,128)(2,1)}, bf16[512,256]{1,0:T(8,128)(2,1)}) custom-call(bf16[512,2048]{1,0:T(8,128)(2,1)} %get-tuple-element.81.dx_in, bf16[512,2048]{1,0:T(8,128)(2,1)} %get-tuple-element.82.scaled_in, bf16[16,256,128]{2,1,0:T(8,128)(2,1)S(1)} %all-to-all-done.4.grad_ref, bf16[512,256]{1,0:T(8,128)(2,1)} %keys_in.3, ...), custom_call_target="tpu_custom_call" | custom-call | flops 1073741824 | bytes 8388608 | tf_op jit(solution)/shard_map/final_grads/pallas_call | solution.py:619
Async XLA Ops:
  9.4 22.3 %all-to-all-start = ((bf16[16,272,128]{2,1,0:T(8,128)(2,1)}), bf16[16,272,128]{2,1,0:T(8,128)(2,1)S(1)}, u32[]{:S(2)}, u32[]{:S(2)}) async-start(bf16[16,272,128]{2,1,0:T(8,128)(2,1)} %get-tuple-element.55), calls=%async_computation | async-start | bytes 2228224 | tf_op jit(solution)/shard_map/all_to_all | solution.py:665
  31.7 16.5 %copy-start.4 = (bf16[16,272,128]{2,1,0:T(8,128)(2,1)}, bf16[16,272,128]{2,1,0:T(8,128)(2,1)S(1)}, u32[]{:S(2)}) copy-start(bf16[16,272,128]{2,1,0:T(8,128)(2,1)S(1)} %all-to-all-done.in_ref.ends_in) | copy-start | bytes 3342340
  31.7 16.5 %copy-start.1 = (bf16[512,2048]{1,0:T(8,128)(2,1)S(1)}, bf16[512,2048]{1,0:T(8,128)(2,1)}, u32[]{:S(2)}) copy-start(bf16[512,2048]{1,0:T(8,128)(2,1)} %get-tuple-element.67.ratio_ref) | copy-start | bytes 6291460
  31.7 16.5 %copy-start.3 = (bf16[512,2048]{1,0:T(8,128)(2,1)S(1)}, bf16[512,2048]{1,0:T(8,128)(2,1)}, u32[]{:S(2)}) copy-start(bf16[512,2048]{1,0:T(8,128)(2,1)} %get-tuple-element.65.local_ref) | copy-start | bytes 6291460
  31.7 16.5 %copy-start.6 = (bf16[512,256]{1,0:T(8,128)(2,1)S(1)}, bf16[512,256]{1,0:T(8,128)(2,1)}, u32[]{:S(2)}) copy-start(bf16[512,256]{1,0:T(8,128)(2,1)} %queries_ref.5) | copy-start | bytes 786436
  31.7 16.5 %copy-start.10 = (f32[2048]{0:T(1024)S(1)}, f32[2048]{0:T(1024)}, u32[]{:S(2)}) copy-start(f32[2048]{0:T(1024)} %param.16) | copy-start | bytes 24580
  48.2 2.5 %copy-start.2 = (bf16[16,256,128]{2,1,0:T(8,128)(2,1)}, bf16[16,256,128]{2,1,0:T(8,128)(2,1)S(1)}, u32[]{:S(2)}) copy-start(bf16[16,256,128]{2,1,0:T(8,128)(2,1)S(1)} %all_to_all.25.state_ref.refs_2_) | copy-start | bytes 3145732
  60.6 4.6 %copy-start = (bf16[512,2048]{1,0:T(8,128)(2,1)S(1)}, bf16[512,2048]{1,0:T(8,128)(2,1)}, u32[]{:S(2)}) copy-start(bf16[512,2048]{1,0:T(8,128)(2,1)} %grad_in.5) | copy-start | bytes 6291460
  60.6 4.6 %copy-start.7 = (bf16[512,256]{1,0:T(8,128)(2,1)S(1)}, bf16[512,256]{1,0:T(8,128)(2,1)}, u32[]{:S(2)}) copy-start(bf16[512,256]{1,0:T(8,128)(2,1)} %queries_ref.5) | copy-start | bytes 786436
  60.6 4.6 %copy-start.9 = (f32[8,2,512]{2,1,0:T(2,128)S(1)}, f32[8,2,512]{2,1,0:T(2,128)}, u32[]{:S(2)}) copy-start(f32[8,2,512]{2,1,0:T(2,128)} %all_to_all.26.sums_ref.refs_0_) | copy-start | bytes 98308
  60.6 4.7 %copy-start.11 = (f32[2048]{0:T(1024)S(1)}, f32[2048]{0:T(1024)}, u32[]{:S(2)}) copy-start(f32[2048]{0:T(1024)} %param.16) | copy-start | bytes 24580
  67.7 18.4 %all-to-all-start.3 = ((bf16[16,256,128]{2,1,0:T(8,128)(2,1)}), bf16[16,256,128]{2,1,0:T(8,128)(2,1)S(1)}, u32[]{:S(2)}, u32[]{:S(2)}) async-start(bf16[16,256,128]{2,1,0:T(8,128)(2,1)} %local_grads.1), calls=%async_computation.3 | async-start | bytes 2097152 | tf_op jit(solution)/shard_map/all_to_all | solution.py:665
  71.4 14.7 %copy-start.5 = (bf16[16,272,128]{2,1,0:T(8,128)(2,1)S(1)}, bf16[16,272,128]{2,1,0:T(8,128)(2,1)}, u32[]{:S(2)}) copy-start(bf16[16,272,128]{2,1,0:T(8,128)(2,1)} %copy-done.4) | copy-start | bytes 3342340
  79.7 11.6 %copy-start.8 = (bf16[512,256]{1,0:T(8,128)(2,1)S(1)}, bf16[512,256]{1,0:T(8,128)(2,1)}, u32[]{:S(2)}) copy-start(bf16[512,256]{1,0:T(8,128)(2,1)} %get-tuple-element.48.refs_2_.refs_4_.fac_ref.fac_in) | copy-start | bytes 786436
  79.7 11.6 %copy-start.12 = (f32[512,128]{1,0:T(8,128)S(1)}, f32[512,128]{1,0:T(8,128)}, u32[]{:S(2)}) copy-start(f32[512,128]{1,0:T(8,128)} %get-tuple-element.49.refs_3_.col_ref) | copy-start | bytes 786436
  79.7 11.6 %copy-start.13 = (f32[4,16,512]{2,1,0:T(8,128)S(1)}, f32[4,16,512]{2,1,0:T(8,128)}, u32[]{:S(2)}) copy-start(f32[4,16,512]{2,1,0:T(8,128)} %get-tuple-element.50.refs_4_.row_ref) | copy-start | bytes 393220
  87.4 17.9 %all-to-all-start.4 = ((bf16[16,256,128]{2,1,0:T(8,128)(2,1)}), bf16[16,256,128]{2,1,0:T(8,128)(2,1)S(1)}, u32[]{:S(2)}, u32[]{:S(2)}) async-start(bf16[16,256,128]{2,1,0:T(8,128)(2,1)} %backward_scan.1), calls=%async_computation.4 | async-start | bytes 2097152 | tf_op jit(solution)/shard_map/all_to_all | solution.py:665
